TPU v7x, 256 devices: a whole 4x4x8 slice. The times are simulated.
256 devices in a mesh: gx: 16 (over z, core), gy: 16 (over x, y).
Axes of the slice: x: 4, y: 4, z: 8, core: 2. Of those that a mesh axis runs over, the one named last changes fastest.
Arguments:
- velocity: float32 [3, 8192, 8192], P(None, 'gx', 'gy'), may hold values from -6 to 6
- metric_first: float32 [8192], P('gy'), may hold values from 0.5 to 2
- metric_second: float32 [8192], P('gy'), may hold values from -4 to 4
Outputs:
- increment: float32 [3, 8192, 8192], P(None, 'gx', 'gy')
All inputs are finite; a program needn't handle non-finite values.
Results may differ from a plain program's by a relative error of at most 0.0003.
Values sent between devices are 32-bit elements; how exact they have to be, the bound alone decides.
No kernel may reach another device: no remote copies, remote signals or barrier semaphores. Data moves between devices by JAX's collectives and lax.ppermute only.
A program may use at most 128 MiB of HBM per device.

v0:
```python
import math

import jax
import jax.numpy as jnp
import numpy as np
from jax import lax
from jax.sharding import PartitionSpec as P

VISCOSITY = 0.2
DIFFUSION = 1.0
HIGHEST = lax.Precision.HIGHEST


def extended(cells, sides, width, closed):
    for axis, dim in sides:
        count = lax.axis_size(axis)
        ends = count if closed else count - 1
        head = lax.slice_in_dim(cells, 0, width, axis=dim)
        tail = lax.slice_in_dim(cells, cells.shape[dim] - width, cells.shape[dim], axis=dim)
        cells = jnp.concatenate(
            [
                lax.ppermute(tail, axis, [(i, (i + 1) % count) for i in range(ends)]),
                cells,
                lax.ppermute(head, axis, [((i + 1) % count, i) for i in range(ends)]),
            ],
            axis=dim,
        )
    return cells


def stencils(field, ahead):
    first_rhs = (
        45.0 * (ahead(1) - ahead(-1)) - 9.0 * (ahead(2) - ahead(-2)) + (ahead(3) - ahead(-3))
    ) / 60.0
    second_rhs = (
        270.0 * (ahead(1) + ahead(-1))
        - 27.0 * (ahead(2) + ahead(-2))
        + 2.0 * (ahead(3) + ahead(-3))
        - 490.0 * field
    ) / 180.0
    return (first_rhs, second_rhs)


def coefficients(cells):
    sigma = cells / 4.0
    diag = 1.0 + 2.0 * DIFFUSION + sigma
    return (-(DIFFUSION + sigma) / diag, -DIFFUSION / diag, diag, sigma)


def invert(matrix):
    order = matrix.shape[0]
    augmented = np.concatenate([matrix, np.eye(order)], axis=1)
    for pivot in range(order):
        augmented[pivot] = augmented[pivot] / augmented[pivot, pivot]
        column_k = augmented[:, pivot].copy()
        column_k[pivot] = 0.0
        augmented = augmented - np.outer(column_k, augmented[pivot])
    return augmented[:, order:]


def band_matrix(below, main, above, periodic):
    order = main.shape[0]
    matrix = np.eye(order) * main
    for row_at in range(1, order):
        matrix[row_at, row_at - 1] = below[row_at]
    for row_at in range(order - 1):
        matrix[row_at, row_at + 1] = above[row_at]
    if periodic:
        matrix[0, order - 1] = matrix[0, order - 1] + below[0]
        matrix[order - 1, 0] = matrix[order - 1, 0] + above[order - 1]
    return matrix


def block_parts(length, lower, upper):
    inner_len = length - 2
    ones = np.ones((inner_len,))
    inverse = invert(band_matrix(lower * ones, ones, upper * ones, False))
    head_col = -lower * inverse[:, 0]
    tail_col = -upper * inverse[:, -1]
    return (inverse, head_col, tail_col)


def reduced_inverse(blocks, lower, upper, head_col, tail_col, periodic):
    order_two = 2 * blocks
    is_even = np.arange(order_two) % 2 == 0
    below = np.where(is_even, lower, lower * head_col[-1])
    main = np.where(is_even, 1.0 + upper * head_col[0], 1.0 + lower * tail_col[-1])
    above = np.where(is_even, upper * tail_col[0], upper)
    return invert(band_matrix(below, main, above, periodic))


def constants(length, lower, upper, blocks, own_block, periodic):
    inverse, head_col, tail_col = block_parts(length, lower, upper)
    reduced = reduced_inverse(blocks, lower, upper, head_col, tail_col, periodic)
    own_rows = lax.dynamic_slice_in_dim(jnp.asarray(reduced, jnp.float32), 2 * own_block, 2, 0)
    return (
        jnp.asarray(inverse, jnp.float32),
        jnp.asarray(head_col, jnp.float32),
        jnp.asarray(tail_col, jnp.float32),
        own_rows,
    )


def make_fold(own_rows, total, piece):
    span_len = piece.shape[1]
    rows_used = lax.slice_in_dim(own_rows, 0, span_len, axis=1)
    return total + jnp.einsum("ij,cjl->cil", rows_used, piece, precision=HIGHEST)


def partitioned_x(right_side, lower, upper):
    inverse, head_col, tail_col, own_rows = constants(
        right_side.shape[1], lower, upper, lax.axis_size("gx"), lax.axis_index("gx"), True
    )
    interior = jnp.einsum("cjy,ij->ciy", right_side[:, 1:-1, :], inverse, precision=HIGHEST)
    head_val = right_side[:, 0, :] - upper * interior[:, 0, :]
    tail_val = right_side[:, -1, :] - lower * interior[:, -1, :]
    ends = jnp.stack([head_val, tail_val], axis=1)
    solved = make_fold(
        own_rows, jnp.zeros(ends.shape, jnp.float32), lax.all_gather(ends, "gx", axis=1, tiled=True)
    )
    head_x = solved[:, 0:1, :]
    tail_x = solved[:, 1:2, :]
    middle = interior + head_col[None, :, None] * head_x + tail_col[None, :, None] * tail_x
    return jnp.concatenate([head_x, middle, tail_x], axis=1)


def local(velocity, metric_first, metric_second):
    cells_x = velocity.shape[1]
    cells_y = velocity.shape[2]
    low_x, up_x, diag_x, sig_x = coefficients(lax.axis_size("gx") * cells_x)
    low_y, up_y, diag_y, sig_y = coefficients(lax.axis_size("gy") * cells_y)
    x_padded = extended(velocity, (("gx", 1),), 3, True)
    y_padded = extended(velocity, (("gy", 2),), 3, False)
    first_x, second_x = stencils(
        velocity, lambda steps: x_padded[:, 3 + steps : 3 + steps + cells_x, :]
    )
    first_eta, second_eta = stencils(
        velocity, lambda steps: y_padded[:, :, 3 + steps : 3 + steps + cells_y]
    )
    slope_y = metric_first * first_eta
    curve_y = metric_first * metric_first * second_eta + metric_second * first_eta
    tendency = -(velocity[0:1] * first_x + velocity[1:2] * slope_y) + VISCOSITY * (
        second_x + curve_y
    )
    right_side = tendency * (math.sqrt(sig_x * sig_y) / diag_x)
    half = partitioned_x(right_side, low_x, up_x)
    y_lines = half / diag_y
    inverse, head_col, tail_col, own_rows = constants(
        cells_y, low_y, up_y, lax.axis_size("gy"), lax.axis_index("gy"), False
    )
    interior = jnp.einsum("cxj,ij->cxi", y_lines[..., 1:-1], inverse, precision=HIGHEST)
    head_val = y_lines[..., 0] - up_y * interior[..., 0]
    tail_val = y_lines[..., -1] - low_y * interior[..., -1]
    ends = jnp.stack([head_val, tail_val], axis=1)
    solved = make_fold(
        own_rows, jnp.zeros(ends.shape, jnp.float32), lax.all_gather(ends, "gy", axis=1, tiled=True)
    )
    head_y = solved[:, 0][..., None]
    tail_y = solved[:, 1][..., None]
    middle = interior + head_col * head_y + tail_col * tail_y
    return jnp.concatenate([head_y, middle, tail_y], axis=-1)


def solution(mesh):
    in_specs = (P(None, "gx", "gy"), P("gy"), P("gy"))
    out_specs = P(None, "gx", "gy")
    return jax.shard_map(local, mesh=mesh, in_specs=in_specs, out_specs=out_specs, check_vma=False)
```

profile of v0, /device:TPU:32, one launch (start us, length us, event | category | flops | bytes accessed | tf_op | source)
XLA Modules:
  0.0 107.2 jit_solution(8872015902211756143)
XLA Ops:
  0.0 0.0 copy-start
  0.0 1.0 fusion.26
  1.0 0.0 collective-permute-start
  1.0 2.8 %fusion.27 = (f32[3,512,3]{2,1,0:T(8,128)}, f32[3,512,3]{2,1,0:T(8,128)}) fusion(f32[3,512,512]{2,1,0:T(8,128)} %param.11), kind=kLoop, calls=%fused_computation.64 | loop fusion | bytes 73728 | tf_op jit(solution)/shard_map/slice | solution.py:19
  3.8 0.0 copy-start.7
  3.8 0.0 copy-start.8
  3.8 1.4 %copy.40 = f32[3,512,3]{1,2,0:T(4,128)S(1)} copy(f32[3,512,3]{2,1,0:T(8,128)} %get-tuple-element.16) | data formatting | bytes 36864
  5.2 1.3 %collective-permute-start.2 = (f32[3,512,3]{1,2,0:T(4,128)S(1)}, f32[3,512,3]{1,2,0:T(4,128)S(1)}, u32[]{:S(2)}, u32[]{:S(2)}) collective-permute-start(f32[3,512,3]{1,2,0:T(4,128)S(1)} %copy.40), channel_id=1, source_target_pairs={{1,0},{2,1},{3,2},{4,3},{5,4},{6,5},{7,6},{8,7},{9,8},{10,9},{11,1... | collective-permute-start | bytes 55304 | tf_op jit(solution)/shard_map/ppermute | solution.py:24
  6.5 1.4 %copy.41 = f32[3,512,3]{1,2,0:T(4,128)S(1)} copy(f32[3,512,3]{2,1,0:T(8,128)} %get-tuple-element.15) | data formatting | bytes 36864
  7.9 4.8 %collective-permute-start.3 = (f32[3,512,3]{1,2,0:T(4,128)S(1)}, f32[3,512,3]{1,2,0:T(4,128)S(1)}, u32[]{:S(2)}, u32[]{:S(2)}) collective-permute-start(f32[3,512,3]{1,2,0:T(4,128)S(1)} %copy.41), channel_id=1, source_target_pairs={{0,1},{1,2},{2,3},{3,4},{4,5},{5,6},{6,7},{7,8},{8,9},{9,10},{10,1... | collective-permute-start | bytes 55304 | tf_op jit(solution)/shard_map/ppermute | solution.py:22
  12.7 0.0 collective-permute-start.1
  12.7 0.0 copy-done
  12.8 1.5 %multiply_bitcast_fusion = (f32[512,512]{1,0:T(8,128)}, f32[512,512]{1,0:T(8,128)}) fusion(f32[3,512,512]{2,1,0:T(8,128)S(1)} %copy-done), kind=kLoop, calls=%fused_computation.32 | loop fusion | flops 262144 | bytes 4194304 | tf_op jit(solution)/shard_map/mul | solution.py:142
  14.3 0.0 copy-done.7
  14.3 0.0 copy-done.8
  14.3 0.0 copy-done.1
  14.3 0.3 constant_dynamic-update-slice_fusion.1
  14.6 0.0 collective-permute-done
  14.7 0.0 collective-permute-done.2
  14.7 1.2 %copy.26 = f32[3,512,3]{2,1,0:T(8,128)} copy(f32[3,512,3]{1,2,0:T(4,128)S(1)} %collective-permute-done.2) | data formatting | bytes 36864 | tf_op jit(solution)/shard_map/ppermute | solution.py:24
  15.9 0.0 collective-permute-done.3
  15.9 1.2 %copy.28 = f32[3,512,3]{2,1,0:T(8,128)} copy(f32[3,512,3]{1,2,0:T(4,128)S(1)} %collective-permute-done.3) | data formatting | bytes 36864 | tf_op jit(solution)/shard_map/ppermute | solution.py:22
  17.2 0.0 collective-permute-done.1
  17.2 0.0 copy-start.4
  17.2 18.3 %add_multiply_fusion = f32[3,512,512]{2,1,0:T(8,128)S(1)} fusion(f32[3,512,512]{2,1,0:T(8,128)} %param.11, f32[3,512,3]{2,1,0:T(8,128)} %copy.26, f32[3,512,3]{2,1,0:T(8,128)} %copy.28, f32[3,3,512]{2,1,0:T(4,128)S(1)} %collective-permute-done.1, f32[3,515,512]{2,1,0:T(8,128)S(1)} %constant_dynamic-update-slice_fusion, f32[512]{0:T(512)S(1)} %get-tuple-element.25, ...), kind=kLoop, calls=%fused_computation.27 | loop fusion | flops 43253760 | bytes 17887232 | tf_op jit(solution)/shard_map/mul | solution.py:145
  35.4 0.0 copy-done.4
  35.5 0.0 copy-start.5
  35.5 0.0 copy-start.6
  35.5 5.6 %fusion.10 = f32[3,510,512]{2,1,0:T(8,128)S(1)} fusion(f32[510,510,1]{1,0,2:T(8,128)S(1)} %copy-done.4, f32[3,512,512]{2,1,0:T(8,128)S(1)} %add_multiply_fusion), kind=kOutput, calls=%fused_computation.28 | convolution fusion | flops 4794163200 | bytes 7319568 | tf_op jit(solution)/shard_map/cjy,ij->ciy/dot_general | solution.py:114
  41.2 20.5 %all_gather.6 = f32[3,32,512]{2,0,1:T(4,128)S(1)} all-gather(f32[3,2,512]{2,0,1:T(4,128)S(1)} %copy.29), channel_id=1, replica_groups=mesh['gx'=16,'gy'=16] {'gx'}, dimensions={1}, use_global_device_ids=true | all-gather | bytes 208896 | tf_op jit(solution)/shard_map/all_gather | solution.py:119
  61.7 1.0 convolution_bitcast_fusion.1
  62.7 0.0 copy-done.5
  62.7 0.0 copy-done.6
  62.7 0.5 multiply_add_fusion.1
  63.2 0.4 maximum_multiply_fusion
  63.7 5.5 %fusion.6 = f32[3,512,510]{1,2,0:T(8,128)S(1)} fusion(f32[510,510,1]{1,0,2:T(8,128)S(1)} %copy-done.4, f32[3,512,512]{2,1,0:T(8,128)S(1)} %maximum_multiply_fusion), kind=kOutput, calls=%fused_computation.16 | convolution fusion | flops 4794163200 | bytes 7319568 | tf_op jit(solution)/shard_map/cxj,ij->cxi/dot_general | solution.py:151
  69.1 0.0 copy-start.2
  69.1 1.7 %copy-done.2 = f32[3,512,510]{1,2,0:T(8,128)} copy-done((f32[3,512,510]{1,2,0:T(8,128)}, f32[3,512,510]{1,2,0:T(8,128)S(1)}, u32[]{:S(2)}) %copy-start.2) | copy-done | bytes 3133464
  70.8 1.2 %copy.42 = f32[3,512,1]{2,1,0:T(8,128)} copy(f32[3,512,1]{1,2,0:T(1,128)S(1)} %get-tuple-element.10) | data formatting | bytes 12288
  72.0 1.2 %copy.43 = f32[3,512,1]{2,1,0:T(8,128)} copy(f32[3,512,1]{1,2,0:T(1,128)S(1)} %get-tuple-element.9) | data formatting | bytes 12288
  73.2 0.0 copy-start.3
  73.2 2.2 %fusion.14 = (f32[3,512]{1,0:T(4,128)S(1)}, f32[3,512]{1,0:T(4,128)S(1)}) fusion(f32[3,512,512]{2,1,0:T(8,128)S(1)} %maximum_multiply_fusion, f32[3,512,1]{2,1,0:T(8,128)} %copy.42, f32[3,512,1]{2,1,0:T(8,128)} %copy.43), kind=kLoop, calls=%fused_computation.36 | loop fusion | flops 6144 | bytes 36864 | tf_op jit(solution)/shard_map/sub | solution.py:152
  75.5 27.3 %all_gather.7 = f32[3,32,512]{2,0,1:T(4,128)S(1)} all-gather(f32[3,2,512]{2,0,1:T(4,128)S(1)} %copy.33), channel_id=1, replica_groups=mesh['gx'=16,'gy'=16] {'gy'}, dimensions={1}, use_global_device_ids=true | all-gather | bytes 208896 | tf_op jit(solution)/shard_map/all_gather | solution.py:156
  102.9 1.0 convolution_bitcast_fusion
  103.9 0.0 copy-done.3
  103.9 0.5 multiply_add_fusion
  104.5 0.4 pad_maximum_fusion.3
  104.9 2.4 %copy.35 = f32[3,512,512]{2,1,0:T(8,128)} copy(f32[3,512,512]{1,2,0:T(8,128)S(1)} %pad_maximum_fusion.3) | data formatting | bytes 6291456 | tf_op jit(solution)/shard_map/concatenate | solution.py:161
  (17 shorter events, 0.2 us)
Async XLA Ops:
  0.0 12.7 %copy-start = (f32[3,512,512]{2,1,0:T(8,128)S(1)}, f32[3,512,512]{2,1,0:T(8,128)}, u32[]{:S(2)}) copy-start(f32[3,512,512]{2,1,0:T(8,128)} %param.11) | copy-start | bytes 9437188
  1.0 13.7 %collective-permute-start = (f32[3,3,512]{2,1,0:T(4,128)S(1)}, f32[3,3,512]{2,1,0:T(4,128)S(1)}, u32[]{:S(2)}, u32[]{:S(2)}) collective-permute-start(f32[3,3,512]{2,1,0:T(4,128)S(1)} %get-tuple-element.13), channel_id=1, source_target_pairs={{16,0},{32,16},{48,32},{64,48},{80,64},{96,80},{112,96},{128,112},... | collective-permute-start | bytes 55304 | tf_op jit(solution)/shard_map/ppermute | solution.py:24
  3.8 10.5 %copy-start.7 = (f32[512]{0:T(512)S(1)}, f32[512]{0:T(512)}, u32[]{:S(2)}) copy-start(f32[512]{0:T(512)} %param.12) | copy-start | bytes 6148
  3.8 10.5 %copy-start.8 = (f32[512]{0:T(512)S(1)}, f32[512]{0:T(512)}, u32[]{:S(2)}) copy-start(f32[512]{0:T(512)} %param.13) | copy-start | bytes 6148
  5.2 9.5 %collective-permute-start.2 = (f32[3,512,3]{1,2,0:T(4,128)S(1)}, f32[3,512,3]{1,2,0:T(4,128)S(1)}, u32[]{:S(2)}, u32[]{:S(2)}) collective-permute-start(f32[3,512,3]{1,2,0:T(4,128)S(1)} %copy.40), channel_id=1, source_target_pairs={{1,0},{2,1},{3,2},{4,3},{5,4},{6,5},{7,6},{8,7},{9,8},{10,9},{11,1... | collective-permute-start | bytes 55304 | tf_op jit(solution)/shard_map/ppermute | solution.py:24
  7.9 6.4 %copy-start.1 = (f32[3,512,512]{2,1,0:T(8,128)S(1)}, f32[3,512,512]{2,1,0:T(8,128)}, u32[]{:S(2)}) copy-start(f32[3,512,512]{2,1,0:T(8,128)} %param.11) | copy-start | bytes 9437188
  7.9 8.0 %collective-permute-start.3 = (f32[3,512,3]{1,2,0:T(4,128)S(1)}, f32[3,512,3]{1,2,0:T(4,128)S(1)}, u32[]{:S(2)}, u32[]{:S(2)}) collective-permute-start(f32[3,512,3]{1,2,0:T(4,128)S(1)} %copy.41), channel_id=1, source_target_pairs={{0,1},{1,2},{2,3},{3,4},{4,5},{5,6},{6,7},{7,8},{8,9},{9,10},{10,1... | collective-permute-start | bytes 55304 | tf_op jit(solution)/shard_map/ppermute | solution.py:22
  12.7 4.4 %collective-permute-start.1 = (f32[3,3,512]{2,1,0:T(4,128)S(1)}, f32[3,3,512]{2,1,0:T(4,128)S(1)}, u32[]{:S(2)}, u32[]{:S(2)}) collective-permute-start(f32[3,3,512]{2,1,0:T(4,128)S(1)} %get-tuple-element.14), channel_id=1, source_target_pairs={{0,16},{16,32},{32,48},{48,64},{64,80},{80,96},{96,112},{112,128},... | collective-permute-start | bytes 55304 | tf_op jit(solution)/shard_map/ppermute | solution.py:22
  17.2 18.3 %copy-start.4 = (f32[510,510,1]{1,0,2:T(8,128)S(1)}, f32[510,510,1]{1,0,2:T(8,128)}, u32[]{:S(2)}) copy-start(f32[510,510,1]{1,0,2:T(8,128)} %constant.59) | copy-start | bytes 3121204
  35.5 27.2 %copy-start.5 = (f32[510]{0:T(512)S(1)}, f32[510]{0:T(512)}, u32[]{:S(2)}) copy-start(f32[510]{0:T(512)} %constant.56.clone) | copy-start | bytes 6124
  35.5 27.2 %copy-start.6 = (f32[510]{0:T(512)S(1)}, f32[510]{0:T(512)}, u32[]{:S(2)}) copy-start(f32[510]{0:T(512)} %constant.57.clone) | copy-start | bytes 6124
  69.1 1.7 %copy-start.2 = (f32[3,512,510]{1,2,0:T(8,128)}, f32[3,512,510]{1,2,0:T(8,128)S(1)}, u32[]{:S(2)}) copy-start(f32[3,512,510]{1,2,0:T(8,128)S(1)} %fusion.6) | copy-start | bytes 9400324
  73.2 30.6 %copy-start.3 = (f32[3,512,510]{1,2,0:T(8,128)S(1)}, f32[3,512,510]{1,2,0:T(8,128)}, u32[]{:S(2)}) copy-start(f32[3,512,510]{1,2,0:T(8,128)} %copy-done.2) | copy-start | bytes 9400324
where the time goes:
time: 108 us; the launch traced here: 107 us
  blocking collectives  47.8 us (44%)
  other arithmetic  24 us (22%)
  local copies, waits for them, and re-layouts  15.9 us (15%)
  matrix products  13 us (12%)
  starting transfers between devices  6.14 us (6%)
    all_gather x1, blocking collectives, local(): lax.all_gather(ends, 'gy', axis=1, tiled=True)  27.3 us
    all_gather x1, blocking collectives, partitioned_x(): lax.all_gather(ends, 'gx', axis=1, tiled=True)  20.5 us
    mul x1, other arithmetic, local(): right_side = tendency * (math.sqrt(sig_x * sig_y) / diag_x)  18.3 us
    unnamed x27, local copies, waits for them, and re-layouts  7.26 us
    dot_general x1, matrix products, partitioned_x(): jnp.einsum('cjy,ij->ciy', right_side[:, 1:-1, :], inverse, precision=HIGH...  5.63 us
    dot_general x1, matrix products, local(): jnp.einsum('cxj,ij->cxi', y_lines[..., 1:-1], inverse, precision=HIGHEST)  5.46 us
    ppermute x2, starting transfers between devices, extended(): lax.ppermute(tail, axis, [(i, (i + 1) % count) for i in range(ends)])  4.83 us
    slice x1, local copies, waits for them, and re-layouts, extended(): lax.slice_in_dim(cells, cells.shape[dim] - width, cells.shape[dim], axis=...  2.76 us
  transfers between devices with their start and end apart: 4, of which 0 were waited for; matrix products, arithmetic and copies ran while one was open for 9% of the time, Pallas kernels for 0%

commit v1 on v0

v1 whole, which is shorter than its diff:
```python
import functools
import math

import jax
import jax.numpy as jnp
import numpy as np
from jax import lax
from jax.experimental import pallas as pl
from jax.experimental.pallas import tpu as pltpu
from jax.sharding import PartitionSpec as P

VISCOSITY = 0.2
DIFFUSION = 1.0
FIRST = (45.0 / 60.0, -9.0 / 60.0, 1.0 / 60.0)
SECOND = (270.0 / 180.0, -27.0 / 180.0, 2.0 / 180.0)
CENTRE = -490.0 / 180.0
ROWS = 64
F32 = jnp.float32
BF16 = jnp.bfloat16
VMEM_LIMIT = 48 * 1024 * 1024


def coefficients(cells):
    sigma = cells / 4.0
    diag = 1.0 + 2.0 * DIFFUSION + sigma
    return (-(DIFFUSION + sigma) / diag, -DIFFUSION / diag, diag, sigma)


def line_tables(length, lower, upper, blocks, periodic):
    matrix = np.eye(length) + lower * np.eye(length, k=-1) + upper * np.eye(length, k=1)
    inverse = np.linalg.inv(matrix)
    head = -lower * inverse[:, 0]
    tail = -upper * inverse[:, -1]
    order = 2 * blocks
    before = np.zeros((blocks, order))
    after = np.zeros((blocks, order))
    for block in range(blocks):
        if periodic or block > 0:
            before[block, 2 * ((block - 1) % blocks) + 1] = 1.0
        if periodic or block < blocks - 1:
            after[block, 2 * ((block + 1) % blocks)] = 1.0
    system = np.eye(order)
    for block in range(blocks):
        system[2 * block] -= head[0] * before[block] + tail[0] * after[block]
        system[2 * block + 1] -= head[-1] * before[block] + tail[-1] * after[block]
    solved = np.linalg.inv(system)
    sides = np.stack([before @ solved, after @ solved], axis=1)
    sides = sides.reshape(blocks, 2, blocks, 2).transpose(0, 2, 1, 3)
    return inverse, head, tail, sides


def split(values):
    high = values.astype(BF16)
    return high, (values - high.astype(F32)).astype(BF16)


def split_table(table):
    high = np.asarray(table, np.float32).astype(BF16)
    low = (np.asarray(table, np.float64) - high.astype(np.float64)).astype(BF16)
    return np.stack([high, low])


def dot3(left, right, dims):
    (lh, ll), (rh, rl) = left, right
    dot = functools.partial(
        lax.dot_general, dimension_numbers=(dims, ((), ())), preferred_element_type=F32
    )
    return dot(lh, rh) + (dot(lh, rl) + dot(ll, rh))


def padded_rows(rows, count):
    return jnp.concatenate(
        rows + [jnp.zeros((count - len(rows), rows[0].shape[1]), F32)], axis=0
    )


def edges_kernel(top, bottom, left, right, x_head, x_tail, y_head, y_tail, columns):
    for comp in range(3):
        x_head[3 * comp : 3 * comp + 3, :] = top[comp, 0:3, :]
        x_tail[3 * comp : 3 * comp + 3, :] = bottom[comp, 5:8, :]
    x_head[9:16, :] = jnp.zeros((7, x_head.shape[1]), F32)
    x_tail[9:16, :] = jnp.zeros((7, x_tail.shape[1]), F32)
    lane = lax.broadcasted_iota(jnp.int32, (64, 128), 1)
    for at in range(0, left.shape[1], 64):
        packed = jnp.zeros((64, 128), F32)
        for comp in range(3):
            here = pltpu.roll(left[comp, at : at + 64, :], 3 * comp, 1) if comp else left[comp, at : at + 64, :]
            packed = jnp.where((lane >= 3 * comp) & (lane < 3 * comp + 3), here, packed)
            here = pltpu.roll(right[comp, at : at + 64, :], 19 + 3 * comp, 1)
            packed = jnp.where((lane >= 16 + 3 * comp) & (lane < 19 + 3 * comp), here, packed)
        columns[at : at + 64, :] = packed
    for at in range(0, left.shape[1], 128):
        turned = columns[at : at + 128, :].T
        y_head[:, at : at + 128] = turned[0:16, :]
        y_tail[:, at : at + 128] = turned[16:32, :]


def inner_kernel(scale, above, own, below, m1, m2, ends_y, inner, ends, ext, columns):
    step = pl.program_id(0)
    last = pl.num_programs(0) - 1
    cells = own.shape[2]
    ext[:, 0:8, :] = jnp.where(step > 0, above[...], 0.0)
    ext[:, 8 : 8 + ROWS, :] = own[...]
    ext[:, 8 + ROWS : 16 + ROWS, :] = jnp.where(step < last, below[...], 0.0)
    first_row = m1[...]
    place = lax.broadcasted_iota(jnp.int32, (1, cells), 1)
    slope = scale * first_row
    offset = (scale * VISCOSITY) * m2[...]
    curve = (scale * VISCOSITY) * first_row * first_row
    middle = CENTRE * (curve + scale * VISCOSITY)
    lane = lax.broadcasted_iota(jnp.int32, (8, 128), 1)
    for at in range(0, ROWS, 8):
        rows = slice(8 + at, 16 + at)
        bend = offset - ext[1, rows, :] * slope
        along = ext[0, rows, :] * scale
        fields = [ext[comp, rows, :] for comp in range(3)]
        totals = [middle * field for field in fields]
        for k in (1, 2, 3):
            lead = FIRST[k - 1] * along
            x_ahead = (scale * VISCOSITY * SECOND[k - 1]) - lead
            x_behind = (scale * VISCOSITY * SECOND[k - 1]) + lead
            ahead = place < cells - k
            behind = place >= k
            bow = SECOND[k - 1] * curve
            y_ahead = jnp.where(ahead, bow, 0.0) + bend * jnp.where(ahead, FIRST[k - 1], 0.0)
            y_behind = jnp.where(behind, bow, 0.0) - bend * jnp.where(behind, FIRST[k - 1], 0.0)
            for comp in range(3):
                totals[comp] = (
                    totals[comp]
                    + (x_ahead * ext[comp, 8 + at + k : 16 + at + k, :] + x_behind * ext[comp, 8 + at - k : 16 + at - k, :])
                    + (y_ahead * pltpu.roll(fields[comp], cells - k, 1) + y_behind * pltpu.roll(fields[comp], k, 1))
                )
        packed = jnp.zeros((8, 128), F32)
        for comp in range(3):
            inner[comp, at : at + 8, :] = totals[comp]
            for end in (0, 1):
                value = jnp.sum(totals[comp] * ends_y[end : end + 1, :], axis=1, keepdims=True)
                packed = jnp.where(lane == 3 * end + comp, value, packed)
        columns[pl.ds(pl.multiple_of(step * ROWS + at, 8), 8), :] = packed

    @pl.when(step == last)
    def _():
        for at in range(0, columns.shape[0], 128):
            ends[:, at : at + 128] = columns[at : at + 128, :].T[0:8, :]


def weigh(table, index, other, values, swapped, third):
    base = 4 * other
    straight = jnp.where(third, table[index, base], table[index, base + 3])
    crossed = jnp.where(third, table[index, base + 1], table[index, base + 2])
    return straight * values + crossed * swapped


def swap_ends(values):
    return jnp.concatenate([values[3:6], values[0:3], values[6:8]], axis=0)


def halo_kernel(
    scale, blocks, index, table, before_x, after_x, before_y, after_y, x_head, x_tail, y_head, y_tail,
    m1, m2, ends_y, ends, shares, delta_x, delta_y,
):
    cells_x = before_y.shape[1]
    cells_y = before_x.shape[1]
    visc = scale * VISCOSITY
    x_rows = [[None] * 6 for _ in range(3)]
    y_rows = [[None] * 6 for _ in range(3)]
    for near in range(3):
        u_head = scale * x_head[near : near + 1, :]
        u_tail = scale * x_tail[2 - near : 3 - near, :]
        v_head = y_head[3 + near : 4 + near, :]
        v_tail = y_tail[5 - near : 6 - near, :]
        last = cells_y - 1 - near
        m1_head, m2_head = m1[0:1, near : near + 1], m2[0:1, near : near + 1]
        m1_tail, m2_tail = m1[0:1, last : last + 1], m2[0:1, last : last + 1]
        bend_head = visc * m2_head - v_head * (scale * m1_head)
        bend_tail = visc * m2_tail - v_tail * (scale * m1_tail)
        curve_head = visc * m1_head * m1_head
        curve_tail = visc * m1_tail * m1_tail
        for comp in range(3):
            x_low = x_high = y_low = y_high = None
            for k in range(near + 1, 4):
                a, b = FIRST[k - 1], SECOND[k - 1]
                low = 3 * comp + 3 + near - k
                high = 3 * comp + k - near - 1
                terms = (
                    (visc * b + a * u_head) * before_x[low : low + 1, :],
                    (visc * b - a * u_tail) * after_x[high : high + 1, :],
                    (b * curve_head - a * bend_head) * before_y[low : low + 1, :],
                    (b * curve_tail + a * bend_tail) * after_y[high : high + 1, :],
                )
                if x_low is None:
                    x_low, x_high, y_low, y_high = terms
                else:
                    x_low, x_high, y_low, y_high = (
                        x_low + terms[0], x_high + terms[1], y_low + terms[2], y_high + terms[3]
                    )
            x_rows[comp][near], x_rows[comp][5 - near] = x_low, x_high
            y_rows[comp][near], y_rows[comp][5 - near] = y_low, y_high
    zero_y = jnp.zeros((2, cells_y), F32)
    zero_x = jnp.zeros((2, cells_x), F32)
    for comp in range(3):
        delta_x[8 * comp : 8 * comp + 8, :] = jnp.concatenate(x_rows[comp] + [zero_y], axis=0)
        delta_y[8 * comp : 8 * comp + 8, :] = jnp.concatenate(y_rows[comp] + [zero_x], axis=0)
    row = lax.broadcasted_iota(jnp.int32, (8, 128), 0)
    lane = lax.broadcasted_iota(jnp.int32, (8, 128), 1)
    at_head = (row < 3) & (lane == row)
    at_tail = (row >= 3) & (row < 6) & (lane == row + 122)
    extra = [[], []]
    for comp in range(3):
        strip = delta_x[8 * comp : 8 * comp + 8, :]
        for end in (0, 1):
            value = jnp.sum(strip * ends_y[end : end + 1, :], axis=1, keepdims=True)
            total = jnp.concatenate(
                [
                    jnp.sum(jnp.where(at_head, value, 0.0), axis=0, keepdims=True),
                    jnp.zeros((1, cells_x - 256), F32),
                    jnp.sum(jnp.where(at_tail, value, 0.0), axis=0, keepdims=True),
                ],
                axis=1,
            )
            for j in range(3):
                last = cells_y - 1 - j
                total = total + (
                    y_rows[comp][j] * ends_y[end : end + 1, j : j + 1]
                    + y_rows[comp][5 - j] * ends_y[end : end + 1, last : last + 1]
                )
            extra[end].append(total)
    values = ends[...] + padded_rows(extra[0] + extra[1], 8)
    swapped = swap_ends(values)
    third = lax.broadcasted_iota(jnp.int32, (8, cells_x), 0) < 3
    for other in range(blocks):
        shares[other] = weigh(table, index[0], other, values, swapped, third)


def solve_kernel(inner, delta_x, delta_y, inverse_x, inverse_y, solved, edges, work, work2, columns):
    comp = pl.program_id(0)
    cells_x, cells_y = inner.shape[1], inner.shape[2]
    work[...] = inner[0]
    work[0:8, :] += jnp.concatenate([delta_x[0:3, :], jnp.zeros((5, cells_y), F32)], axis=0)
    work[cells_x - 8 : cells_x, :] += jnp.concatenate([jnp.zeros((5, cells_y), F32), delta_x[3:6, :]], axis=0)
    lane = lax.broadcasted_iota(jnp.int32, (128, 128), 1)
    for at in range(0, cells_x, 128):
        tile = jnp.concatenate([delta_y[:, at : at + 128], jnp.zeros((120, 128), F32)], axis=0).T
        work[at : at + 128, 0:128] += jnp.where(lane < 3, tile, 0.0)
        work[at : at + 128, cells_y - 128 : cells_y] += jnp.where(lane >= 125, pltpu.roll(tile, 122, 1), 0.0)
    right = (inverse_y[0], inverse_y[1])
    left = (inverse_x[0], inverse_x[1])
    half = cells_x // 2
    for at in (0, half):
        work2[at : at + half, :] = dot3(split(work[at : at + half, :]), right, ((1,), (1,)))
    for at in (0, half):
        lines = split(work2[:, at : at + half])
        solved[0, :, at : at + half] = dot3(left, lines, ((1,), (0,)))
    edges[pl.ds(comp, 1), :] = solved[0, 0:1, :]
    edges[pl.ds(comp + 3, 1), :] = solved[0, cells_x - 1 : cells_x, :]

    @pl.when(comp == 0)
    def _():
        edges[6:8, :] = jnp.zeros((2, cells_y), F32)


def ends_kernel(shares, edges, ends_x, sides_y, out, beside):
    total = shares[0]
    for block in range(1, shares.shape[0]):
        total = total + shares[block]
    beside[...] = total
    rows = []
    for end in (0, 1):
        value = jnp.sum(total * ends_x[end : end + 1, :], axis=1, keepdims=True)
        for comp in range(3):
            rows.append(
                value[comp : comp + 1] * sides_y[0:1, :] + value[comp + 3 : comp + 4] * sides_y[1:2, :]
            )
    out[...] = edges[...] + padded_rows(rows, 8)


def final_kernel(blocks, index, table, gathered, beside, inverse_x, sides_x, sides_y, solved, out, beyond, columns):
    step = pl.program_id(0)
    cells_x, cells_y = beside.shape[1], gathered.shape[2]

    @pl.when(step == 0)
    def _():
        third = lax.broadcasted_iota(jnp.int32, (8, cells_y), 0) < 3
        straight = jnp.zeros((8, cells_y), F32)
        crossed = jnp.zeros((8, cells_y), F32)
        for block in range(blocks):
            base = 4 * block
            values = gathered[block]
            straight += jnp.where(third, table[index[0], base], table[index[0], base + 3]) * values
            crossed += jnp.where(third, table[index[0], base + 2], table[index[0], base + 1]) * values
        beyond[...] = straight + swap_ends(crossed)
        lines = dot3(split(beside[...]), (inverse_x[0], inverse_x[1]), ((1,), (1,)))
        rows = jnp.concatenate([lines[0:6], sides_x[0:2], jnp.zeros((120, cells_x), F32)], axis=0)
        for at in range(0, cells_x, 128):
            columns[at : at + 128, :] = rows[:, at : at + 128].T

    for at in range(0, ROWS, 8):
        here = columns[pl.ds(pl.multiple_of(step * ROWS + at, 8), 8), :]
        head, tail = here[:, 6:7], here[:, 7:8]
        for comp in range(3):
            out[comp, at : at + 8, :] = (
                solved[comp, at : at + 8, :]
                + (here[:, comp : comp + 1] * sides_y[0:1, :] + here[:, comp + 3 : comp + 4] * sides_y[1:2, :])
                + (head * beyond[comp : comp + 1, :] + tail * beyond[comp + 3 : comp + 4, :])
            )


def whole(shape):
    return pl.BlockSpec(shape, lambda *_: (0,) * len(shape))


def call(kernel, grid, in_specs, out_specs, out_shape, scratch, flops, nbytes):
    return pl.pallas_call(
        kernel,
        grid=grid,
        in_specs=in_specs,
        out_specs=out_specs,
        out_shape=out_shape,
        scratch_shapes=scratch,
        compiler_params=pltpu.CompilerParams(vmem_limit_bytes=VMEM_LIMIT),
        cost_estimate=pl.CostEstimate(flops=flops, bytes_accessed=nbytes, transcendentals=0),
    )


def local(velocity, metric_first, metric_second):
    _, nx, ny = velocity.shape
    blocks_x, blocks_y = lax.axis_size("gx"), lax.axis_size("gy")
    low_x, up_x, diag_x, sig_x = coefficients(blocks_x * nx)
    low_y, up_y, diag_y, sig_y = coefficients(blocks_y * ny)
    scale = math.sqrt(sig_x * sig_y) / (diag_x * diag_y)
    inverse_x, head_x, tail_x, among_x = line_tables(nx, low_x, up_x, blocks_x, True)
    inverse_y, head_y, tail_y, among_y = line_tables(ny, low_y, up_y, blocks_y, False)
    table_x = jnp.asarray(among_x.reshape(blocks_x, 4 * blocks_x), F32)
    table_y = jnp.asarray(among_y.transpose(1, 0, 2, 3).reshape(blocks_y, 4 * blocks_y), F32)
    ends_x = jnp.asarray(np.stack([inverse_x[0], inverse_x[-1]]), F32)
    ends_y = jnp.asarray(np.stack([inverse_y[0], inverse_y[-1]]), F32)
    sides_x = jnp.asarray(np.stack([head_x, tail_x]), F32)
    sides_y = jnp.asarray(np.stack([head_y, tail_y]), F32)
    parts_x = jnp.asarray(split_table(inverse_x))
    parts_y = jnp.asarray(split_table(inverse_y))
    index_x = lax.axis_index("gx").astype(jnp.int32).reshape(1)
    index_y = lax.axis_index("gy").astype(jnp.int32).reshape(1)
    m1 = metric_first.reshape(1, ny)
    m2 = metric_second.reshape(1, ny)
    smem = pl.BlockSpec(memory_space=pltpu.SMEM)
    struct = jax.ShapeDtypeStruct
    field = struct((3, nx, ny), F32)

    with jax.named_scope("edges"):
        x_head, x_tail, y_head, y_tail = call(
            edges_kernel,
            (1,),
            [
                pl.BlockSpec((3, 8, ny), lambda i: (0, 0, 0)),
                pl.BlockSpec((3, 8, ny), lambda i: (0, nx // 8 - 1, 0)),
                pl.BlockSpec((3, nx, 128), lambda i: (0, 0, 0)),
                pl.BlockSpec((3, nx, 128), lambda i: (0, 0, ny // 128 - 1)),
            ],
            [whole((16, ny)), whole((16, ny)), whole((16, nx)), whole((16, nx))],
            [struct((16, ny), F32)] * 2 + [struct((16, nx), F32)] * 2,
            [pltpu.VMEM((nx, 128), F32)],
            10 * nx * 128,
            8 * 3 * nx * 128,
        )(velocity, velocity, velocity, velocity)
    with jax.named_scope("halos"):
        round_x = [(i, (i + 1) % blocks_x) for i in range(blocks_x)]
        along_y = [(i, i + 1) for i in range(blocks_y - 1)]
        before_y = lax.ppermute(y_tail, "gy", along_y)
        after_y = lax.ppermute(y_head, "gy", [(b, a) for a, b in along_y])
        before_x = lax.ppermute(x_tail, "gx", round_x)
        after_x = lax.ppermute(x_head, "gx", [(b, a) for a, b in round_x])
    with jax.named_scope("inner"):
        strips = ROWS // 8
        inner, ends = call(
            functools.partial(inner_kernel, scale),
            (nx // ROWS,),
            [
                pl.BlockSpec((3, 8, ny), lambda i: (0, jnp.maximum(i * strips - 1, 0), 0)),
                pl.BlockSpec((3, ROWS, ny), lambda i: (0, i, 0)),
                pl.BlockSpec((3, 8, ny), lambda i: (0, jnp.minimum((i + 1) * strips, nx // 8 - 1), 0)),
                whole((1, ny)),
                whole((1, ny)),
                whole((2, ny)),
            ],
            [pl.BlockSpec((3, ROWS, ny), lambda i: (0, i, 0)), whole((8, nx))],
            [field, struct((8, nx), F32)],
            [pltpu.VMEM((3, ROWS + 16, ny), F32), pltpu.VMEM((nx, 128), F32)],
            40 * 3 * nx * ny,
            8 * 3 * nx * ny,
        )(velocity, velocity, velocity, m1, m2, ends_y)
    with jax.named_scope("halo_part"):
        shares, delta_x, delta_y = call(
            functools.partial(halo_kernel, scale, blocks_y),
            (1,),
            [smem, smem]
            + [whole((16, ny))] * 2
            + [whole((16, nx))] * 2
            + [whole((16, ny))] * 2
            + [whole((16, nx))] * 2
            + [whole((1, ny)), whole((1, ny)), whole((2, ny)), whole((8, nx))],
            [whole((blocks_y, 8, nx)), whole((24, ny)), whole((24, nx))],
            [struct((blocks_y, 8, nx), F32), struct((24, ny), F32), struct((24, nx), F32)],
            [],
            1000 * nx,
            500 * nx,
        )(index_y, table_y, before_x, after_x, before_y, after_y, x_head, x_tail, y_head, y_tail, m1, m2, ends_y, ends)
    with jax.named_scope("across_y"):
        got_y = lax.all_to_all(shares, "gy", 0, 0, tiled=True)
    with jax.named_scope("solve"):
        solved, edges = call(
            solve_kernel,
            (3,),
            [
                pl.BlockSpec((1, nx, ny), lambda c: (c, 0, 0)),
                pl.BlockSpec((8, ny), lambda c: (c, 0)),
                pl.BlockSpec((8, nx), lambda c: (c, 0)),
                whole((2, nx, nx)),
                whole((2, ny, ny)),
            ],
            [pl.BlockSpec((1, nx, ny), lambda c: (c, 0, 0)), whole((8, ny))],
            [field, struct((8, ny), F32)],
            [pltpu.VMEM((nx, ny), F32), pltpu.VMEM((nx, ny), F32), pltpu.VMEM((nx, 128), F32)],
            3 * 6 * nx * ny * (nx + ny),
            8 * 3 * nx * ny,
        )(inner, delta_x, delta_y, parts_x, parts_y)
    with jax.named_scope("ends_x"):
        own_ends, beside = call(
            ends_kernel,
            (1,),
            [whole((blocks_y, 8, nx)), whole((8, ny)), whole((2, nx)), whole((2, ny))],
            [whole((8, ny)), whole((8, nx))],
            [struct((8, ny), F32), struct((8, nx), F32)],
            [],
            100 * nx,
            500 * nx,
        )(got_y, edges, ends_x, sides_y)
    with jax.named_scope("across_x"):
        gathered = lax.all_gather(own_ends, "gx", axis=0)
    with jax.named_scope("final"):
        return call(
            functools.partial(final_kernel, blocks_x),
            (nx // ROWS,),
            [
                smem,
                smem,
                whole((blocks_x, 8, ny)),
                whole((8, nx)),
                whole((2, nx, nx)),
                whole((2, nx)),
                whole((2, ny)),
                pl.BlockSpec((3, ROWS, ny), lambda i: (0, i, 0)),
            ],
            pl.BlockSpec((3, ROWS, ny), lambda i: (0, i, 0)),
            field,
            [pltpu.VMEM((8, ny), F32), pltpu.VMEM((nx, 128), F32)],
            8 * 3 * nx * ny,
            8 * 3 * nx * ny,
        )(index_x, table_x, gathered, beside, parts_x, sides_x, sides_y, solved)


def solution(mesh):
    in_specs = (P(None, "gx", "gy"), P("gy"), P("gy"))
    out_specs = P(None, "gx", "gy")
    return jax.shard_map(local, mesh=mesh, in_specs=in_specs, out_specs=out_specs, check_vma=False)
```

time: 108 us -> 71.2 us (0.66)
  the two profiles are of different devices: /device:TPU:32 before, /device:TPU:1 now
where the time goes in v1:
time: 71.2 us; the launch traced here: 70.8 us
  Pallas kernels  27.6 us (39%)
  blocking collectives  21.9 us (31%)
  starting transfers between devices  15.1 us (21%)
  local copies, waits for them, and re-layouts  6.02 us (8%)
    all_gather x1, blocking collectives, local(): gathered = lax.all_gather(own_ends, 'gx', axis=0)  21.9 us
    pallas_call x1, Pallas kernels, local(): call(functools.partial(inner_kernel, scale), (nx // ROWS,), [pl.BlockSpec...  13.1 us
    all_to_all x1, starting transfers between devices, local(): got_y = lax.all_to_all(shares, 'gy', 0, 0, tiled=True)  7.54 us
    pallas_call x1, Pallas kernels, local(): call(solve_kernel, (3,), [pl.BlockSpec((1, nx, ny), lambda c: (c, 0, 0)),...  6.85 us
    unnamed x20, local copies, waits for them, and re-layouts  6.02 us
    pallas_call x1, Pallas kernels, local(): call(functools.partial(final_kernel, blocks_x), (nx // ROWS,), [smem, sme...  5.48 us
    ppermute x1, starting transfers between devices, local(): before_x = lax.ppermute(x_tail, 'gx', round_x)  3.03 us
    ppermute x1, starting transfers between devices, local(): before_y = lax.ppermute(y_tail, 'gy', along_y)  2.96 us
  transfers between devices with their start and end apart: 5, of which 0 were waited for; matrix products, arithmetic and copies ran while one was open for 0% of the time, Pallas kernels for 28%

profile of v1, /device:TPU:1, one launch (start us, length us, event | category | flops | bytes accessed | tf_op | source)
XLA Modules:
  0.0 70.8 jit_solution(9765922100804474419)
XLA Ops:
  0.0 0.0 copy-start
  0.0 1.9 %copy-done = f32[3,512,512]{2,1,0:T(8,128)S(1)} copy-done((f32[3,512,512]{2,1,0:T(8,128)S(1)}, f32[3,512,512]{2,1,0:T(8,128)}, u32[]{:S(2)}) %copy-start) | copy-done | bytes 3145752
  1.9 0.0 copy-start.4
  1.9 0.0 copy-start.7
  1.9 0.0 copy-start.8
  1.9 0.5 edges.1
  2.4 3.0 %collective-permute-start = (f32[16,512]{1,0:T(8,128)S(1)}, f32[16,512]{1,0:T(8,128)S(1)}, u32[]{:S(2)}, u32[]{:S(2)}) collective-permute-start(f32[16,512]{1,0:T(8,128)S(1)} %get-tuple-element.18.x_tail), channel_id=1, source_target_pairs={{0,16},{16,32},{32,48},{48,64},{64,80},{80,96},{96,112},{112,128},... | collective-permute-start | bytes 98312 | tf_op jit(solution)/shard_map/halos/ppermute | solution.py:370
  5.4 0.2 collective-permute-start.1
  5.6 3.0 %collective-permute-start.2 = (f32[16,512]{1,0:T(8,128)S(1)}, f32[16,512]{1,0:T(8,128)S(1)}, u32[]{:S(2)}, u32[]{:S(2)}) collective-permute-start(f32[16,512]{1,0:T(8,128)S(1)} %get-tuple-element.20.y_tail), channel_id=1, source_target_pairs={{0,1},{1,2},{2,3},{3,4},{4,5},{5,6},{6,7},{7,8},{8,9},{9,10},{10,1... | collective-permute-start | bytes 98312 | tf_op jit(solution)/shard_map/halos/ppermute | solution.py:368
  8.6 1.3 %collective-permute-start.3 = (f32[16,512]{1,0:T(8,128)S(1)}, f32[16,512]{1,0:T(8,128)S(1)}, u32[]{:S(2)}, u32[]{:S(2)}) collective-permute-start(f32[16,512]{1,0:T(8,128)S(1)} %get-tuple-element.21.y_head), channel_id=1, source_target_pairs={{1,0},{2,1},{3,2},{4,3},{5,4},{6,5},{7,6},{8,7},{9,8},{10,9},{11,1... | collective-permute-start | bytes 98312 | tf_op jit(solution)/shard_map/halos/ppermute | solution.py:369
  9.9 0.0 copy-done.4
  9.9 0.0 copy-done.7
  9.9 0.0 copy-done.8
  9.9 0.0 copy-start.5
  9.9 13.1 %inner.1 = (f32[3,512,512]{2,1,0:T(8,128)S(1)}, f32[8,512]{1,0:T(8,128)S(1)}) custom-call(f32[3,512,512]{2,1,0:T(8,128)} %below.1, f32[3,512,512]{2,1,0:T(8,128)} %below.1, f32[3,512,512]{2,1,0:T(8,128)} %below.1, f32[1,512]{1,0:T(1,128)S(1)} %bitcast.6, f32[1,512]{1,0:T(1,128)S(1)} %bitcast.8, f32[2,512]{1,0:T(2,128)S(1)} %copy-done.4), custom_call_target="tpu_custom_call" | custom-call | flops 31457280 | bytes 6291456 | tf_op jit(solution)/shard_map/inner/pallas_call | solution.py:374
  23.1 0.0 copy-start.9
  23.1 1.7 %copy-done.9 = f32[3,512,512]{2,1,0:T(8,128)} copy-done((f32[3,512,512]{2,1,0:T(8,128)}, f32[3,512,512]{2,1,0:T(8,128)S(1)}, u32[]{:S(2)}) %copy-start.9) | copy-done | bytes 3145752
  24.7 0.0 collective-permute-done.before_x
  24.7 0.0 collective-permute-done.1.after_x
  24.7 0.0 collective-permute-done.2.before_y
  24.7 0.0 collective-permute-done.3.after_y
  24.7 0.0 copy-done.5
  24.8 1.6 %halo_part.1 = (f32[16,8,512]{2,1,0:T(8,128)}, f32[24,512]{1,0:T(8,128)S(1)}, f32[24,512]{1,0:T(8,128)S(1)}) custom-call(s32[1]{0:T(128)} %bitcast.1.index, f32[16,64]{1,0:T(8,128)S(1)} %copy-done.5, f32[16,512]{1,0:T(8,128)S(1)} %collective-permute-done.before_x, f32[16,512]{1,0:T(8,128)S(1)} %collective-permute-done.1.after_x, ...), custom_call_target="tpu_custom_call" | custom-call | flops 512000 | bytes 256000 | tf_op jit(solution)/shard_map/halo_part/pallas_call | solution.py:392
  26.4 7.5 %all-to-all-start = ((f32[16,8,512]{2,1,0:T(8,128)}), f32[16,8,512]{2,1,0:T(8,128)S(1)}, u32[]{:S(2)}, u32[]{:S(2)}) async-start(f32[16,8,512]{2,1,0:T(8,128)} %get-tuple-element.23), calls=%async_computation | async-start | bytes 524288 | tf_op jit(solution)/shard_map/across_y/all_to_all | solution.py:408
  33.9 0.0 copy-start.1
  33.9 1.2 %copy-done.1 = bf16[2,512,512]{2,1,0:T(8,128)(2,1)S(1)} copy-done((bf16[2,512,512]{2,1,0:T(8,128)(2,1)S(1)}, bf16[2,512,512]{2,1,0:T(8,128)(2,1)}, u32[]{:S(2)}) %copy-start.1) | copy-done | bytes 1048600
  35.1 0.0 copy-start.3
  35.1 0.0 copy-start.6
  35.1 6.8 %solve.1 = (f32[3,512,512]{2,1,0:T(8,128)S(1)}, f32[8,512]{1,0:T(8,128)S(1)}) custom-call(f32[3,512,512]{2,1,0:T(8,128)} %copy-done.9, f32[24,512]{1,0:T(8,128)S(1)} %get-tuple-element.25.delta_x, f32[24,512]{1,0:T(8,128)S(1)} %get-tuple-element.26.delta_y, bf16[2,512,512]{2,1,0:T(8,128)(2,1)S(1)} %copy-done.1, bf16[2,512,512]{2,1,0:T(8,128)(2,1)S(1)} %copy-done.1), custom_call_target="tpu_custom_call" | custom-call | flops 4831838208 | bytes 6291456 | tf_op jit(solution)/shard_map/solve/pallas_call | solution.py:410
  42.0 0.0 all-to-all-done.shares
  42.0 0.0 copy-done.3
  42.0 0.1 ends_x.2
  42.1 21.9 %all-gather = f32[128,512]{1,0:T(8,128)S(1)} all-gather(f32[8,512]{1,0:T(8,128)S(1)} %get-tuple-element.28), channel_id=2, replica_groups=mesh['gx'=16,'gy'=16] {'gx'}, dimensions={0}, use_global_device_ids=true | all-gather | bytes 278528 | tf_op jit(solution)/shard_map/across_x/all_gather | solution.py:438
  64.1 0.0 copy-done.6
  64.1 0.0 copy-start.2
  64.1 1.2 %copy-done.2 = bf16[2,512,512]{2,1,0:T(8,128)(2,1)S(1)} copy-done((bf16[2,512,512]{2,1,0:T(8,128)(2,1)S(1)}, bf16[2,512,512]{2,1,0:T(8,128)(2,1)}, u32[]{:S(2)}) %copy-start.2) | copy-done | bytes 1048600
  65.3 5.5 %final.1 = f32[3,512,512]{2,1,0:T(8,128)} custom-call(s32[1]{0:T(128)} %bitcast.index, f32[16,64]{1,0:T(8,128)S(1)} %copy-done.6, f32[16,8,512]{2,1,0:T(8,128)S(1)} %bitcast.5, f32[8,512]{1,0:T(8,128)S(1)} %get-tuple-element.29.beside, bf16[2,512,512]{2,1,0:T(8,128)(2,1)S(1)} %copy-done.2, f32[2,512]{1,0:T(2,128)S(1)} %copy-done.3, f32[2,512]{1,0:T(2,128)S(1)} %copy-done.3, ...), custom_call_target="tpu_custom_call" | custom-call | flops 6291456 | bytes 6291456 | tf_op jit(solution)/shard_map/final/pallas_call | solution.py:440
Async XLA Ops:
  0.0 1.9 %copy-start = (f32[3,512,512]{2,1,0:T(8,128)S(1)}, f32[3,512,512]{2,1,0:T(8,128)}, u32[]{:S(2)}) copy-start(f32[3,512,512]{2,1,0:T(8,128)} %below.1) | copy-start | bytes 9437188
  1.9 8.0 %copy-start.4 = (f32[2,512]{1,0:T(2,128)S(1)}, f32[2,512]{1,0:T(2,128)}, u32[]{:S(2)}) copy-start(f32[2,512]{1,0:T(2,128)} %constant.19.clone.ends_y.ends_x) | copy-start | bytes 12292
  1.9 8.0 %copy-start.7 = (f32[512]{0:T(512)S(1)}, f32[512]{0:T(512)}, u32[]{:S(2)}) copy-start(f32[512]{0:T(512)} %param.12) | copy-start | bytes 6148
  1.9 8.0 %copy-start.8 = (f32[512]{0:T(512)S(1)}, f32[512]{0:T(512)}, u32[]{:S(2)}) copy-start(f32[512]{0:T(512)} %param.13) | copy-start | bytes 6148
  2.4 22.4 %collective-permute-start = (f32[16,512]{1,0:T(8,128)S(1)}, f32[16,512]{1,0:T(8,128)S(1)}, u32[]{:S(2)}, u32[]{:S(2)}) collective-permute-start(f32[16,512]{1,0:T(8,128)S(1)} %get-tuple-element.18.x_tail), channel_id=1, source_target_pairs={{0,16},{16,32},{32,48},{48,64},{64,80},{80,96},{96,112},{112,128},... | collective-permute-start | bytes 98312 | tf_op jit(solution)/shard_map/halos/ppermute | solution.py:370
  5.4 19.3 %collective-permute-start.1 = (f32[16,512]{1,0:T(8,128)S(1)}, f32[16,512]{1,0:T(8,128)S(1)}, u32[]{:S(2)}, u32[]{:S(2)}) collective-permute-start(f32[16,512]{1,0:T(8,128)S(1)} %get-tuple-element.19.x_head), channel_id=1, source_target_pairs={{16,0},{32,16},{48,32},{64,48},{80,64},{96,80},{112,96},{128,112},... | collective-permute-start | bytes 98312 | tf_op jit(solution)/shard_map/halos/ppermute | solution.py:371
  5.6 19.1 %collective-permute-start.2 = (f32[16,512]{1,0:T(8,128)S(1)}, f32[16,512]{1,0:T(8,128)S(1)}, u32[]{:S(2)}, u32[]{:S(2)}) collective-permute-start(f32[16,512]{1,0:T(8,128)S(1)} %get-tuple-element.20.y_tail), channel_id=1, source_target_pairs={{0,1},{1,2},{2,3},{3,4},{4,5},{5,6},{6,7},{7,8},{8,9},{9,10},{10,1... | collective-permute-start | bytes 98312 | tf_op jit(solution)/shard_map/halos/ppermute | solution.py:368
  8.6 16.1 %collective-permute-start.3 = (f32[16,512]{1,0:T(8,128)S(1)}, f32[16,512]{1,0:T(8,128)S(1)}, u32[]{:S(2)}, u32[]{:S(2)}) collective-permute-start(f32[16,512]{1,0:T(8,128)S(1)} %get-tuple-element.21.y_head), channel_id=1, source_target_pairs={{1,0},{2,1},{3,2},{4,3},{5,4},{6,5},{7,6},{8,7},{9,8},{10,9},{11,1... | collective-permute-start | bytes 98312 | tf_op jit(solution)/shard_map/halos/ppermute | solution.py:369
  9.9 14.8 %copy-start.5 = (f32[16,64]{1,0:T(8,128)S(1)}, f32[16,64]{1,0:T(8,128)}, u32[]{:S(2)}) copy-start(f32[16,64]{1,0:T(8,128)} %constant.18.clone.table) | copy-start | bytes 12292
  23.1 1.7 %copy-start.9 = (f32[3,512,512]{2,1,0:T(8,128)}, f32[3,512,512]{2,1,0:T(8,128)S(1)}, u32[]{:S(2)}) copy-start(f32[3,512,512]{2,1,0:T(8,128)S(1)} %get-tuple-element.24.inner) | copy-start | bytes 9437188
  26.4 15.6 %all-to-all-start = ((f32[16,8,512]{2,1,0:T(8,128)}), f32[16,8,512]{2,1,0:T(8,128)S(1)}, u32[]{:S(2)}, u32[]{:S(2)}) async-start(f32[16,8,512]{2,1,0:T(8,128)} %get-tuple-element.23), calls=%async_computation | async-start | bytes 524288 | tf_op jit(solution)/shard_map/across_y/all_to_all | solution.py:408
  33.9 1.2 %copy-start.1 = (bf16[2,512,512]{2,1,0:T(8,128)(2,1)S(1)}, bf16[2,512,512]{2,1,0:T(8,128)(2,1)}, u32[]{:S(2)}) copy-start(bf16[2,512,512]{2,1,0:T(8,128)(2,1)} %constant.21.clone.inverse_x.inverse_y) | copy-start | bytes 3145732
  35.1 6.9 %copy-start.3 = (f32[2,512]{1,0:T(2,128)S(1)}, f32[2,512]{1,0:T(2,128)}, u32[]{:S(2)}) copy-start(f32[2,512]{1,0:T(2,128)} %constant.20.clone.sides_y.sides_x) | copy-start | bytes 12292
  35.1 28.9 %copy-start.6 = (f32[16,64]{1,0:T(8,128)S(1)}, f32[16,64]{1,0:T(8,128)}, u32[]{:S(2)}) copy-start(f32[16,64]{1,0:T(8,128)} %constant.17.clone.table) | copy-start | bytes 12292
  64.1 1.2 %copy-start.2 = (bf16[2,512,512]{2,1,0:T(8,128)(2,1)S(1)}, bf16[2,512,512]{2,1,0:T(8,128)(2,1)}, u32[]{:S(2)}) copy-start(bf16[2,512,512]{2,1,0:T(8,128)(2,1)} %constant.21.clone.inverse_x.inverse_y) | copy-start | bytes 3145732

commit v2 on v0

v2 whole, which is shorter than its diff:
```python
import functools
import math

import jax
import jax.numpy as jnp
import numpy as np
from jax import lax
from jax.experimental import pallas as pl
from jax.experimental.pallas import tpu as pltpu
from jax.sharding import PartitionSpec as P

VISCOSITY = 0.2
DIFFUSION = 1.0
FIRST = (45.0 / 60.0, -9.0 / 60.0, 1.0 / 60.0)
SECOND = (270.0 / 180.0, -27.0 / 180.0, 2.0 / 180.0)
CENTRE = -490.0 / 180.0
CUTS = (0, 8, 24, 56, 64)
UNROLL = 8
F32 = jnp.float32
BF16 = jnp.bfloat16
VMEM_LIMIT = 24 * 1024 * 1024


def coefficients(cells):
    sigma = cells / 4.0
    diag = 1.0 + 2.0 * DIFFUSION + sigma
    return (-(DIFFUSION + sigma) / diag, -DIFFUSION / diag, diag, sigma)


def line_tables(length, lower, upper, blocks, periodic):
    matrix = np.eye(length) + lower * np.eye(length, k=-1) + upper * np.eye(length, k=1)
    inverse = np.linalg.inv(matrix)
    head = -lower * inverse[:, 0]
    tail = -upper * inverse[:, -1]
    order = 2 * blocks
    before = np.zeros((blocks, order))
    after = np.zeros((blocks, order))
    for block in range(blocks):
        if periodic or block > 0:
            before[block, 2 * ((block - 1) % blocks) + 1] = 1.0
        if periodic or block < blocks - 1:
            after[block, 2 * ((block + 1) % blocks)] = 1.0
    system = np.eye(order)
    for block in range(blocks):
        system[2 * block] -= head[0] * before[block] + tail[0] * after[block]
        system[2 * block + 1] -= head[-1] * before[block] + tail[-1] * after[block]
    solved = np.linalg.inv(system)
    sides = np.stack([before @ solved, after @ solved], axis=1)
    sides = sides.reshape(blocks, 2, blocks, 2).transpose(0, 2, 1, 3)
    return inverse, head, tail, sides


def split(values):
    high = values.astype(BF16)
    return high, (values - high.astype(F32)).astype(BF16)


def split_table(table, axis):
    high = np.asarray(table, np.float32).astype(BF16)
    low = (np.asarray(table, np.float64) - high.astype(np.float64)).astype(BF16)
    return np.concatenate([high, high, low], axis=axis)


def padded_rows(rows, count):
    filled = sum(row.shape[0] for row in rows)
    return jnp.concatenate(rows + [jnp.zeros((count - filled, rows[0].shape[1]), F32)], axis=0)


def lane_blocks(cells):
    return [slice(at, at + 128) for at in range(0, cells, 128)]


def edges_kernel(field, x_head, x_tail, y_head, y_tail, top, bottom, left, right, columns, sems):
    rows, cells = field.shape[1], field.shape[2]
    copies = [
        pltpu.make_async_copy(field.at[:, 0:8, :], top, sems.at[0]),
        pltpu.make_async_copy(field.at[:, rows - 8 : rows, :], bottom, sems.at[1]),
        pltpu.make_async_copy(field.at[:, :, 0:128], left, sems.at[2]),
        pltpu.make_async_copy(field.at[:, :, cells - 128 : cells], right, sems.at[3]),
    ]
    for copy in copies:
        copy.start()
    x_head[...] = jnp.zeros(x_head.shape, F32)
    x_tail[...] = jnp.zeros(x_tail.shape, F32)
    for copy in copies[:2]:
        copy.wait()
    for comp in range(3):
        x_head[3 * comp : 3 * comp + 3, :] = top[comp, 0:3, :]
        x_tail[3 * comp : 3 * comp + 3, :] = bottom[comp, 5:8, :]
    for copy in copies[2:]:
        copy.wait()
    edge_columns(left, right, y_head, y_tail, columns)


def edge_columns(left, right, y_head, y_tail, columns):
    cells_x = left.shape[1]
    lane = lax.broadcasted_iota(jnp.int32, (64, 128), 1)
    for at in range(0, cells_x, 64):
        packed = jnp.zeros((64, 128), F32)
        for comp in range(3):
            here = left[comp, at : at + 64, :]
            here = pltpu.roll(here, 3 * comp, 1) if comp else here
            packed = jnp.where((lane >= 3 * comp) & (lane < 3 * comp + 3), here, packed)
            here = pltpu.roll(right[comp, at : at + 64, :], 19 + 3 * comp, 1)
            packed = jnp.where((lane >= 16 + 3 * comp) & (lane < 19 + 3 * comp), here, packed)
        columns[at : at + 64, :] = packed
    for block in lane_blocks(cells_x):
        turned = columns[block, :].T
        y_head[:, block] = turned[0:16, :]
        y_tail[:, block] = turned[16:32, :]


def inner_kernel(scale, field, m1, m2, ends_y, inner, ends, padded, result, along_rows, sums, load_sems, store_sems):
    rows, cells = result.shape[1], result.shape[2]
    blocks = lane_blocks(cells)
    count = len(blocks)
    visc = scale * VISCOSITY
    zero = jnp.zeros((8, 128), F32)
    bounds = [rows * at // 64 for at in CUTS]
    spans = list(zip(bounds[:-1], bounds[1:]))
    loads = []
    for which, (first, final) in enumerate(spans):
        low, high = (first + 8 if first else 0), min(final + 8, rows)
        loads.append(
            [
                pltpu.make_async_copy(
                    field.at[:, low:high, block], padded.at[:, at, low + 8 : high + 8, :], load_sems.at[which, at]
                )
                for at, block in enumerate(blocks)
            ]
        )
    for group in loads:
        for copy in group:
            copy.start()
    for comp in range(3):
        for at in range(count):
            padded[comp, at, 0:8, :] = zero
            padded[comp, at, 8 + rows : 16 + rows, :] = zero
    slope = m1[...]
    curve = visc * slope * slope
    for at, row in enumerate(
        [scale * slope, visc * m2[...], SECOND[0] * curve, SECOND[1] * curve, SECOND[2] * curve]
        + [CENTRE * (curve + visc), ends_y[0:1, :], ends_y[1:2, :]]
    ):
        wide = jnp.broadcast_to(row, (8, cells))
        for place, block in enumerate(blocks):
            along_rows[at, place] = wide[:, block]
    lane = lax.broadcasted_iota(jnp.int32, (8, 128), 1)

    def step(index, carry):
        row = pl.multiple_of(index * 8, 8)
        fields = [[padded[comp, at, pl.ds(row + 8, 8), :] for at in range(count)] for comp in range(3)]
        along = [scale * part for part in fields[0]]
        bend = [along_rows[1, at] - fields[1][at] * along_rows[0, at] for at in range(count)]
        totals = [[along_rows[5, at] * fields[comp][at] for at in range(count)] for comp in range(3)]
        for k in (1, 2, 3):
            lead = [FIRST[k - 1] * part for part in along]
            lean = [FIRST[k - 1] * part for part in bend]
            x_ahead = [visc * SECOND[k - 1] - part for part in lead]
            x_behind = [visc * SECOND[k - 1] + part for part in lead]
            y_ahead = [along_rows[1 + k, at] + lean[at] for at in range(count)]
            y_behind = [along_rows[1 + k, at] - lean[at] for at in range(count)]
            for comp in range(3):
                left = [pltpu.roll(part, 128 - k, 1) for part in fields[comp]] + [zero]
                right = [zero] + [pltpu.roll(part, k, 1) for part in fields[comp]]
                for at in range(count):
                    totals[comp][at] = (
                        totals[comp][at]
                        + (
                            x_ahead[at] * padded[comp, at, pl.ds(row + 8 + k, 8), :]
                            + x_behind[at] * padded[comp, at, pl.ds(row + 8 - k, 8), :]
                        )
                        + (
                            y_ahead[at] * jnp.where(lane < 128 - k, left[at], left[at + 1])
                            + y_behind[at] * jnp.where(lane >= k, right[at + 1], right[at])
                        )
                    )
        for comp in range(3):
            for end in (0, 1):
                value = totals[comp][0] * along_rows[6 + end, 0]
                for at in range(1, count):
                    value = value + totals[comp][at] * along_rows[6 + end, at]
                sums[3 * end + comp, pl.ds(row, 8), :] = value
            for at, block in enumerate(blocks):
                result[comp, pl.ds(row, 8), block] = totals[comp][at]
        return carry

    stores = []
    for which, (first, final) in enumerate(spans):
        for copy in loads[which]:
            copy.wait()
        lax.fori_loop(first // 8, final // 8, step, 0, unroll=UNROLL)
        store = pltpu.make_async_copy(
            result.at[:, first:final, :], inner.at[:, first:final, :], store_sems.at[which]
        )
        store.start()
        stores.append(store)
    for block in lane_blocks(rows):
        values = [jnp.sum(sums[at, block, :].T, axis=0, keepdims=True) for at in range(6)]
        ends[:, block] = padded_rows(values, 8)
    for store in stores:
        store.wait()


def pack(values):
    return jnp.concatenate([values[0:6, block] for block in lane_blocks(values.shape[1])], axis=0)


def unpack(values):
    count = values.shape[0] // 6
    return jnp.concatenate([values[6 * at : 6 * at + 6, :] for at in range(count)], axis=1)


def write_shares(table, index, values, shares):
    swapped = pack(jnp.concatenate([values[3:6], values[0:3]], axis=0))
    values = pack(values)
    place = lax.broadcasted_iota(jnp.int32, values.shape, 0)
    third = jnp.zeros(values.shape, jnp.bool_)
    for at in range(0, values.shape[0], 6):
        third = third | ((place >= at) & (place < at + 3))
    for other in range(shares.shape[0]):
        base = 4 * other
        straight = jnp.where(third, table[index[0], base], table[index[0], base + 3])
        crossed = jnp.where(third, table[index[0], base + 1], table[index[0], base + 2])
        shares[other] = straight * values + crossed * swapped


def halo_sides(before, after, curves, bends_head, bends_tail):
    rows = lax.broadcasted_iota(jnp.int32, (16, 1), 0)
    line = rows - 3 * ((rows >= 3).astype(jnp.int32) + (rows >= 6).astype(jnp.int32))
    inside = rows < 9
    head = tail = None
    for k in (1, 2, 3):
        a, b = FIRST[k - 1], SECOND[k - 1]
        low = jnp.where(inside & (line < k), (b * curves[0] - a * bends_head), 0.0)
        high = jnp.where(inside & (line >= 3 - k), (b * curves[1] + a * bends_tail), 0.0)
        low = low * (pltpu.roll(before, 16 - (3 - k), 0) if k < 3 else before)
        high = high * (pltpu.roll(after, 3 - k, 0) if k < 3 else after)
        head = low if head is None else head + low
        tail = high if tail is None else tail + high
    return head, tail


def tiled_lines(lines):
    return jnp.concatenate([lines, lines, lines, jnp.zeros((7, lines.shape[1]), F32)], axis=0)


def line_column(row, first):
    rows = lax.broadcasted_iota(jnp.int32, (16, 1), 0)
    column = jnp.zeros((16, 1), F32)
    for at in range(9):
        column = jnp.where(rows == at, row[0:1, first + at % 3 : first + at % 3 + 1], column)
    return column


def halo_kernel(
    scale, index, table, before_x, after_x, before_y, after_y, x_head, x_tail, y_head, y_tail,
    m1, m2, ends_y, near_ends, ends, shares, delta_x, delta_y,
):
    cells_x = before_y.shape[1]
    cells_y = before_x.shape[1]
    visc = scale * VISCOSITY
    head_x, tail_x = halo_sides(
        before_x[...],
        after_x[...],
        (visc, visc),
        -scale * tiled_lines(x_head[0:3, :]),
        -scale * tiled_lines(x_tail[0:3, :]),
    )
    row1, row2 = m1[...], m2[...]
    ends_at = (0, cells_y - 3)
    slopes = [line_column(row1, at) for at in ends_at]
    offsets = [visc * line_column(row2, at) for at in ends_at]
    bends = [
        offsets[side] - (scale * slopes[side]) * tiled_lines(lines[3:6, :])
        for side, lines in enumerate((y_head, y_tail))
    ]
    head_y, tail_y = halo_sides(
        jnp.where(index[0] > 0, before_y[...], 0.0),
        jnp.where(index[0] < shares.shape[0] - 1, after_y[...], 0.0),
        [visc * slope * slope for slope in slopes],
        bends[0],
        bends[1],
    )
    delta_x[0:16, :] = head_x
    delta_x[16:32, :] = tail_x
    delta_y[0:16, :] = head_y
    delta_y[16:32, :] = tail_y
    values = ends[...] + lax.dot_general(
        near_ends[...],
        jnp.concatenate([head_y, tail_y], axis=0),
        (((1,), (0,)), ((), ())),
        precision=lax.Precision.HIGHEST,
        preferred_element_type=F32,
    )
    rows = lax.broadcasted_iota(jnp.int32, (16, 128), 0)
    line = rows - 3 * ((rows >= 3).astype(jnp.int32) + (rows >= 6).astype(jnp.int32))
    lane = lax.broadcasted_iota(jnp.int32, (16, 128), 1)
    extra = []
    for end in (0, 1):
        weights = ends_y[end : end + 1, :]
        first = jnp.sum(head_x * weights, axis=1, keepdims=True) * jnp.where(lane == line, 1.0, 0.0)
        final = jnp.sum(tail_x * weights, axis=1, keepdims=True) * jnp.where(lane == line + 125, 1.0, 0.0)
        for comp in range(3):
            own = (rows >= 3 * comp) & (rows < 3 * comp + 3)
            extra.append(
                jnp.concatenate(
                    [
                        jnp.sum(jnp.where(own, first, 0.0), axis=0, keepdims=True),
                        jnp.zeros((1, cells_x - 256), F32),
                        jnp.sum(jnp.where(own, final, 0.0), axis=0, keepdims=True),
                    ],
                    axis=1,
                )
            )
    write_shares(table, index, values + padded_rows(extra, 8), shares)


def turned_rows(rows, turned):
    tall = jnp.concatenate([rows, jnp.zeros((128 - rows.shape[0], rows.shape[1]), F32)], axis=0)
    for block in lane_blocks(rows.shape[1]):
        turned[block, :] = tall[:, block].T


def solve_y_kernel(
    inner, delta_x, delta_y, rows_x, table, lines, edges,
    work, result, inverse, turned, wide, sems,
):
    cells_x, cells = result.shape[1], result.shape[2]
    loads = [pltpu.make_async_copy(inner.at[comp], work.at[comp], sems.at[comp]) for comp in range(3)]
    tables = [pltpu.make_async_copy(table, inverse, sems.at[3])]
    for copy in loads[:1] + tables + loads[1:]:
        copy.start()
    turned_rows(rows_x[...], turned)
    for at in range(0, cells_x, 128):
        for end in (0, 1):
            wide[end, at : at + 128, :] = jnp.broadcast_to(turned[at : at + 128, end : end + 1], (128, 128))
    turned_rows(delta_y[...], turned)
    lane = lax.broadcasted_iota(jnp.int32, (128, 128), 1)
    found = [None] * 6
    half = cells_x // 2
    stores = []
    for comp in range(3):
        loads[comp].wait()
        for at in range(0, cells_x, 128):
            tile = turned[at : at + 128, :]
            near = pltpu.roll(tile, 128 - 3 * comp, 1) if comp else tile
            work[comp, at : at + 128, 0:128] += jnp.where(lane < 3, near, 0.0)
            far = pltpu.roll(tile, 109 - 3 * comp, 1)
            work[comp, at : at + 128, cells - 128 : cells] += jnp.where(lane >= 125, far, 0.0)
        work[comp, 0:3, :] += delta_x[3 * comp : 3 * comp + 3, :]
        work[comp, cells_x - 3 : cells_x, :] += delta_x[16 + 3 * comp : 19 + 3 * comp, :]
        if comp == 0:
            for copy in tables:
                copy.wait()
        for at in (0, half):
            high, low = split(work[comp, at : at + half, :])
            solved = jnp.dot(
                jnp.concatenate([high, low, high], axis=1), inverse[...], preferred_element_type=F32
            )
            result[comp, at : at + half, :] = solved
            for end in (0, 1):
                weights = wide[end, at : at + half, :]
                value = jnp.concatenate(
                    [
                        jnp.sum((solved[:, lanes] * weights).reshape(half // 8, 8, 128), axis=0)
                        for lanes in lane_blocks(cells)
                    ],
                    axis=1,
                )
                where = 3 * end + comp
                found[where] = value if found[where] is None else found[where] + value
        store = pltpu.make_async_copy(result.at[comp], lines.at[comp], sems.at[4 + comp])
        store.start()
        stores.append(store)
    edges[...] = padded_rows([jnp.sum(value, axis=0, keepdims=True) for value in found], 8)
    for store in stores:
        store.wait()


def ends_kernel(index, table, got, edges, ends_x, sides_y, shares, beside):
    total = got[0]
    for block in range(1, got.shape[0]):
        total = total + got[block]
    total = unpack(total)
    beside[...] = padded_rows([total], 8)
    rows = []
    for end in (0, 1):
        value = jnp.sum(total * ends_x[end : end + 1, :], axis=1, keepdims=True)
        for comp in range(3):
            rows.append(
                value[comp : comp + 1] * sides_y[0:1, :] + value[comp + 3 : comp + 4] * sides_y[1:2, :]
            )
    write_shares(table, index, edges[...] + padded_rows(rows, 8), shares)


def solve_x_kernel(lines, beside, sides_y, table, solved, work, inverse, turned, sems):
    cells_x, cells_y = solved.shape[1], solved.shape[2]
    tables = [pltpu.make_async_copy(table, inverse, sems.at[3])]
    loads = [pltpu.make_async_copy(lines.at[comp], work.at[comp], sems.at[comp]) for comp in range(3)]
    for copy in loads[:1] + tables + loads[1:]:
        copy.start()
    turned_rows(beside[...], turned)
    half = cells_y // 2
    before, after = sides_y[0:1, :], sides_y[1:2, :]
    for comp in range(3):
        loads[comp].wait()
        if comp == 0:
            for copy in tables:
                copy.wait()
        for at in (0, half):
            block = slice(at, at + half)
            full = (
                work[comp, :, block]
                + turned[:, comp : comp + 1] * before[:, block]
                + turned[:, comp + 3 : comp + 4] * after[:, block]
            )
            high, low = split(full)
            solved[comp, :, block] = jnp.dot(
                inverse[...], jnp.concatenate([high, low, high], axis=0), preferred_element_type=F32
            )


def final_kernel(got, rows_x, solved, out, beyond, turned):
    step = pl.program_id(0)
    rows = out.shape[1]
    blocks = lane_blocks(out.shape[2])

    @pl.when(step == 0)
    def _():
        turned_rows(rows_x[...], turned)
        total = got[0]
        for block in range(1, got.shape[0]):
            total = total + got[block]
        for row in range(6):
            for at in range(len(blocks)):
                beyond[row, at] = jnp.broadcast_to(total[6 * at + row : 6 * at + row + 1, :], (8, 128))

    for at in range(0, rows, 8):
        where = pl.ds(pl.multiple_of(step * rows + at, 8), 8)
        here = turned[where, :]
        head = jnp.broadcast_to(here[:, 2:3], (8, 128))
        tail = jnp.broadcast_to(here[:, 3:4], (8, 128))
        for comp in range(3):
            for place, block in enumerate(blocks):
                out[comp, at : at + 8, block] = solved[comp, where, block] + (
                    head * beyond[comp, place] + tail * beyond[comp + 3, place]
                )


VMEM = pl.BlockSpec(memory_space=pltpu.VMEM)
SMEM = pl.BlockSpec(memory_space=pltpu.SMEM)
HBM = pl.BlockSpec(memory_space=pltpu.HBM)


def in_hbm(values):
    return pltpu.with_memory_space_constraint(values, pltpu.HBM)


def struct(*shape):
    return jax.ShapeDtypeStruct(shape, F32)


def call(kernel, in_specs, out_shape, scratch, flops, nbytes, **kinds):
    if "out_specs" not in kinds:
        kinds["out_specs"] = [VMEM] * len(out_shape)
    return pl.pallas_call(
        kernel,
        in_specs=in_specs,
        out_shape=out_shape,
        scratch_shapes=scratch,
        compiler_params=pltpu.CompilerParams(vmem_limit_bytes=VMEM_LIMIT),
        cost_estimate=pl.CostEstimate(flops=flops, bytes_accessed=nbytes, transcendentals=0),
        **kinds,
    )


def local(velocity, metric_first, metric_second):
    _, nx, ny = velocity.shape
    blocks_x, blocks_y = lax.axis_size("gx"), lax.axis_size("gy")
    low_x, up_x, diag_x, sig_x = coefficients(blocks_x * nx)
    low_y, up_y, diag_y, sig_y = coefficients(blocks_y * ny)
    scale = math.sqrt(sig_x * sig_y) / (diag_x * diag_y)
    inverse_x, head_x, tail_x, among_x = line_tables(nx, low_x, up_x, blocks_x, True)
    inverse_y, head_y, tail_y, among_y = line_tables(ny, low_y, up_y, blocks_y, False)
    table_x = jnp.asarray(among_x.transpose(1, 0, 2, 3).reshape(blocks_x, 4 * blocks_x), F32)
    table_y = jnp.asarray(among_y.transpose(1, 0, 2, 3).reshape(blocks_y, 4 * blocks_y), F32)
    ends_x = jnp.asarray(np.stack([inverse_x[0], inverse_x[-1]]), F32)
    ends_y = jnp.asarray(np.stack([inverse_y[0], inverse_y[-1]]), F32)
    near = np.zeros((8, 32))
    for end, row in enumerate((inverse_y[0], inverse_y[-1])):
        for comp in range(3):
            near[3 * end + comp, 3 * comp : 3 * comp + 3] = row[:3]
            near[3 * end + comp, 16 + 3 * comp : 19 + 3 * comp] = row[-3:]
    near_ends = jnp.asarray(near, F32)
    rows_x = np.zeros((8, nx))
    rows_x[:4] = np.stack([inverse_x[0], inverse_x[-1], head_x, tail_x])
    rows_x = jnp.asarray(rows_x, F32)
    sides_y = jnp.asarray(np.stack([head_y, tail_y]), F32)
    parts_x = in_hbm(jnp.asarray(split_table(inverse_x, 1)))
    parts_y = in_hbm(jnp.asarray(split_table(inverse_y.T, 0)))
    index_x = lax.axis_index("gx").astype(jnp.int32).reshape(1)
    index_y = lax.axis_index("gy").astype(jnp.int32).reshape(1)
    m1 = metric_first.reshape(1, ny)
    m2 = metric_second.reshape(1, ny)
    cells = 3 * nx * ny
    round_x = [(i, (i + 1) % blocks_x) for i in range(blocks_x)]
    back_x = [(b, a) for a, b in round_x]
    round_y = [(i, (i + 1) % blocks_y) for i in range(blocks_y)]
    back_y = [(b, a) for a, b in round_y]

    velocity = in_hbm(velocity)
    with jax.named_scope("edges"):
        x_head, x_tail, y_head, y_tail = call(
            edges_kernel,
            [HBM],
            [struct(16, ny)] * 2 + [struct(16, nx)] * 2,
            [pltpu.VMEM((3, 8, ny), F32)] * 2
            + [pltpu.VMEM((3, nx, 128), F32)] * 2
            + [pltpu.VMEM((nx, 128), F32), pltpu.SemaphoreType.DMA((4,))],
            10 * nx * 128,
            24 * nx * 128,
        )(velocity)
    with jax.named_scope("halos"):
        before_x = lax.ppermute(x_tail, "gx", round_x)
        after_x = lax.ppermute(x_head, "gx", back_x)
        before_y = lax.ppermute(y_tail, "gy", round_y)
        after_y = lax.ppermute(y_head, "gy", back_y)
    with jax.named_scope("inner"):
        inner, ends = call(
            functools.partial(inner_kernel, scale),
            [HBM] + [VMEM] * 3,
            [pltpu.HBM((3, nx, ny), F32), struct(8, nx)],
            [
                pltpu.VMEM((3, ny // 128, nx + 16, 128), F32),
                pltpu.VMEM((3, nx, ny), F32),
                pltpu.VMEM((8, ny // 128, 8, 128), F32),
                pltpu.VMEM((6, nx, 128), F32),
                pltpu.SemaphoreType.DMA((len(CUTS) - 1, ny // 128)),
                pltpu.SemaphoreType.DMA((len(CUTS) - 1,)),
            ],
            40 * cells,
            8 * cells,
            out_specs=[HBM, VMEM],
        )(velocity, m1, m2, ends_y)
    with jax.named_scope("halo_part"):
        shares_y, delta_x, delta_y = call(
            functools.partial(halo_kernel, scale),
            [SMEM, SMEM] + [VMEM] * 13,
            [struct(blocks_y, 6 * (nx // 128), 128), struct(32, ny), struct(32, nx)],
            [],
            1000 * nx,
            500 * nx,
        )(
            index_y, table_y, before_x, after_x, before_y, after_y, x_head, x_tail, y_head, y_tail,
            m1, m2, ends_y, near_ends, ends,
        )
    with jax.named_scope("across_y"):
        got_y = lax.all_to_all(shares_y, "gy", 0, 0, tiled=True)
    with jax.named_scope("solve_y"):
        lines, edges = call(
            solve_y_kernel,
            [HBM] + [VMEM] * 3 + [HBM],
            [pltpu.HBM((3, nx, ny), F32), struct(8, ny)],
            [pltpu.VMEM((3, nx, ny), F32)] * 2
            + [pltpu.VMEM((3 * ny, ny), BF16), pltpu.VMEM((nx, 128), F32), pltpu.VMEM((2, nx, 128), F32)]
            + [pltpu.SemaphoreType.DMA((7,))],
            6 * cells * ny,
            8 * cells,
            out_specs=[HBM, VMEM],
        )(in_hbm(inner), delta_x, delta_y, rows_x, parts_y)
    with jax.named_scope("ends_x"):
        shares_x, beside = call(
            ends_kernel,
            [SMEM, SMEM] + [VMEM] * 4,
            [struct(blocks_x, 6 * (ny // 128), 128), struct(8, nx)],
            [],
            100 * nx,
            500 * nx,
        )(index_x, table_x, got_y, edges, ends_x, sides_y)
    with jax.named_scope("across_x"):
        got_x = lax.all_to_all(shares_x, "gx", 0, 0, tiled=True)
    with jax.named_scope("solve_x"):
        (solved,) = call(
            solve_x_kernel,
            [HBM, VMEM, VMEM, HBM],
            [struct(3, nx, ny)],
            [pltpu.VMEM((3, nx, ny), F32), pltpu.VMEM((nx, 3 * nx), BF16), pltpu.VMEM((nx, 128), F32)]
            + [pltpu.SemaphoreType.DMA((4,))],
            6 * cells * nx,
            8 * cells,
        )(in_hbm(lines), beside, sides_y, parts_x)
    with jax.named_scope("final"):
        return call(
            final_kernel,
            [VMEM] * 3,
            struct(3, nx, ny),
            [pltpu.VMEM((6, ny // 128, 8, 128), F32), pltpu.VMEM((nx, 128), F32)],
            4 * cells,
            8 * cells,
            grid=(nx // 128,),
            out_specs=pl.BlockSpec((3, 128, ny), lambda i: (0, i, 0)),
        )(got_x, rows_x, solved)


def solution(mesh):
    in_specs = (P(None, "gx", "gy"), P("gy"), P("gy"))
    out_specs = P(None, "gx", "gy")
    return jax.shard_map(local, mesh=mesh, in_specs=in_specs, out_specs=out_specs, check_vma=False)
```

time: 108 us -> 56.8 us (0.53)
  the two profiles are of different devices: /device:TPU:32 before, /device:TPU:1 now
where the time goes in v2:
time: 56.8 us; the launch traced here: 56.5 us
  Pallas kernels  27.7 us (49%)
  starting transfers between devices  23.2 us (41%)
  waiting for transfers between devices  5.39 us (9%)
    all_to_all x1, starting transfers between devices, local(): got_x = lax.all_to_all(shares_x, 'gx', 0, 0, tiled=True)  11.6 us
    pallas_call x1, Pallas kernels, local(): call(functools.partial(inner_kernel, scale), [HBM] + [VMEM] * 3, [pltpu.H...  7.7 us
    pallas_call x1, Pallas kernels, local(): call(solve_y_kernel, [HBM] + [VMEM] * 3 + [HBM], [pltpu.HBM((3, nx, ny),...  6.18 us
    pallas_call x1, Pallas kernels, local(): call(solve_x_kernel, [HBM, VMEM, VMEM, HBM], [struct(3, nx, ny)], [pltpu....  5.61 us
    all_to_all x1, waiting for transfers between devices, local(): got_x = lax.all_to_all(shares_x, 'gx', 0, 0, tiled=True)  4.71 us
    ppermute x1, starting transfers between devices, local(): after_y = lax.ppermute(y_head, 'gy', back_y)  3.73 us
    all_to_all x1, starting transfers between devices, local(): got_y = lax.all_to_all(shares_y, 'gy', 0, 0, tiled=True)  3.52 us
    ppermute x1, starting transfers between devices, local(): before_x = lax.ppermute(x_tail, 'gx', round_x)  3.04 us
  transfers between devices with their start and end apart: 6, of which 2 were waited for; matrix products, arithmetic and copies ran while one was open for 0% of the time, Pallas kernels for 34%

profile of v2, /device:TPU:1, one launch (start us, length us, event | category | flops | bytes accessed | tf_op | source)
XLA Modules:
  0.0 56.5 jit_solution(493354434957103534)
XLA Ops:
  0.0 0.0 copy-start
  0.0 0.0 copy-start.5
  0.0 0.0 copy-start.7
  0.0 0.0 copy-start.1
  0.0 0.0 copy-start.3
  0.0 0.0 copy-start.2
  0.0 2.0 %edges.1 = (f32[16,512]{1,0:T(8,128)S(1)}, f32[16,512]{1,0:T(8,128)S(1)}, f32[16,512]{1,0:T(8,128)S(1)}, f32[16,512]{1,0:T(8,128)S(1)}) custom-call(f32[3,512,512]{2,1,0:T(8,128)} %field.3), custom_call_target="tpu_custom_call" | custom-call | flops 655360 | bytes 1572864 | tf_op jit(solution)/shard_map/edges/pallas_call | solution.py:514
  2.0 3.0 %collective-permute-start = (f32[16,512]{1,0:T(8,128)S(1)}, f32[16,512]{1,0:T(8,128)S(1)}, u32[]{:S(2)}, u32[]{:S(2)}) collective-permute-start(f32[16,512]{1,0:T(8,128)S(1)} %get-tuple-element.18.x_tail), channel_id=1, source_target_pairs={{0,16},{16,32},{32,48},{48,64},{64,80},{80,96},{96,112},{112,128},... | collective-permute-start | bytes 98312 | tf_op jit(solution)/shard_map/halos/ppermute | solution.py:525
  5.1 0.2 collective-permute-start.1
  5.3 1.1 %collective-permute-start.2 = (f32[16,512]{1,0:T(8,128)S(1)}, f32[16,512]{1,0:T(8,128)S(1)}, u32[]{:S(2)}, u32[]{:S(2)}) collective-permute-start(f32[16,512]{1,0:T(8,128)S(1)} %get-tuple-element.20.y_tail), channel_id=1, source_target_pairs={{0,1},{1,2},{2,3},{3,4},{4,5},{5,6},{6,7},{7,8},{8,9},{9,10},{10,1... | collective-permute-start | bytes 98312 | tf_op jit(solution)/shard_map/halos/ppermute | solution.py:527
  6.4 3.7 %collective-permute-start.3 = (f32[16,512]{1,0:T(8,128)S(1)}, f32[16,512]{1,0:T(8,128)S(1)}, u32[]{:S(2)}, u32[]{:S(2)}) collective-permute-start(f32[16,512]{1,0:T(8,128)S(1)} %get-tuple-element.21.y_head), channel_id=1, source_target_pairs={{1,0},{2,1},{3,2},{4,3},{5,4},{6,5},{7,6},{8,7},{9,8},{10,9},{11,1... | collective-permute-start | bytes 98312 | tf_op jit(solution)/shard_map/halos/ppermute | solution.py:528
  10.1 0.0 copy-done
  10.1 0.0 copy-done.3
  10.1 0.0 copy-done.2
  10.1 7.7 %inner.1 = (f32[3,512,512]{2,1,0:T(8,128)}, f32[8,512]{1,0:T(8,128)S(1)}) custom-call(f32[3,512,512]{2,1,0:T(8,128)} %field.3, f32[1,512]{1,0:T(1,128)S(1)} %bitcast.4, f32[1,512]{1,0:T(1,128)S(1)} %bitcast.6, f32[2,512]{1,0:T(2,128)S(1)} %copy-done), custom_call_target="tpu_custom_call" | custom-call | flops 31457280 | bytes 6291456 | tf_op jit(solution)/shard_map/inner/pallas_call | solution.py:530
  17.8 0.0 collective-permute-done.before_x
  17.8 0.0 collective-permute-done.1.after_x
  17.8 0.0 collective-permute-done.2.before_y
  17.9 0.0 collective-permute-done.3.after_y
  17.9 0.0 copy-done.5
  17.9 0.0 copy-done.7
  17.9 2.2 %halo_part.1 = (f32[16,24,128]{2,1,0:T(8,128)}, f32[32,512]{1,0:T(8,128)S(1)}, f32[32,512]{1,0:T(8,128)S(1)}) custom-call(s32[1]{0:T(128)} %bitcast.1.index, f32[16,64]{1,0:T(8,128)S(1)} %copy-done.5, f32[16,512]{1,0:T(8,128)S(1)} %collective-permute-done.before_x, f32[16,512]{1,0:T(8,128)S(1)} %collective-permute-done.1.after_x, ...), custom_call_target="tpu_custom_call" | custom-call | flops 512000 | bytes 256000 | tf_op jit(solution)/shard_map/halo_part/pallas_call | solution.py:547
  20.1 3.5 %all-to-all-start = ((f32[16,24,128]{2,1,0:T(8,128)}), f32[16,24,128]{2,1,0:T(8,128)S(1)}, u32[]{:S(2)}, u32[]{:S(2)}) async-start(f32[16,24,128]{2,1,0:T(8,128)} %get-tuple-element.23), calls=%async_computation | async-start | bytes 393216 | tf_op jit(solution)/shard_map/across_y/all_to_all | solution.py:559
  23.6 0.0 copy-done.1
  23.7 0.0 copy-start.4
  23.7 0.0 copy-start.6
  23.7 6.2 %solve_y.1 = (f32[3,512,512]{2,1,0:T(8,128)}, f32[8,512]{1,0:T(8,128)S(1)}) custom-call(f32[3,512,512]{2,1,0:T(8,128)} %get-tuple-element.24.inner, f32[32,512]{1,0:T(8,128)S(1)} %get-tuple-element.25.delta_x, f32[32,512]{1,0:T(8,128)S(1)} %get-tuple-element.26.delta_y, f32[8,512]{1,0:T(8,128)S(1)} %copy-done.1, bf16[1536,512]{1,0:T(8,128)(2,1)} %constant.30.clone.table), custom_call_target="tpu_custom_call" | custom-call | flops 2415919104 | bytes 6291456 | tf_op jit(solution)/shard_map/solve_y/pallas_call | solution.py:561
  29.9 0.7 %all-to-all-done.got = f32[16,24,128]{2,1,0:T(8,128)S(1)} async-done(((f32[16,24,128]{2,1,0:T(8,128)}), f32[16,24,128]{2,1,0:T(8,128)S(1)}, u32[]{:S(2)}, u32[]{:S(2)}) %all-to-all-start) | async-done | bytes 196640 | tf_op jit(solution)/shard_map/across_y/all_to_all | solution.py:559
  30.5 0.0 copy-done.4
  30.5 0.0 copy-done.6
  30.5 1.5 %ends_x.2 = (f32[16,24,128]{2,1,0:T(8,128)}, f32[8,512]{1,0:T(8,128)S(1)}) custom-call(s32[1]{0:T(128)} %bitcast.index, f32[16,64]{1,0:T(8,128)S(1)} %copy-done.4, f32[16,24,128]{2,1,0:T(8,128)S(1)} %all-to-all-done.got, f32[8,512]{1,0:T(8,128)S(1)} %get-tuple-element.27.edges, f32[2,512]{1,0:T(2,128)S(1)} %copy-done, f32[2,512]{1,0:T(2,128)S(1)} %copy-done.6), custom_call_target="tpu_custom_call" | custom-call | flops 51200 | bytes 256000 | tf_op jit(solution)/shard_map/ends_x/pallas_call | solution.py:573
  32.0 11.6 %all-to-all-start.1 = ((f32[16,24,128]{2,1,0:T(8,128)}), f32[16,24,128]{2,1,0:T(8,128)S(1)}, u32[]{:S(2)}, u32[]{:S(2)}) async-start(f32[16,24,128]{2,1,0:T(8,128)} %get-tuple-element.28), calls=%async_computation.1 | async-start | bytes 393216 | tf_op jit(solution)/shard_map/across_x/all_to_all | solution.py:582
  43.6 5.6 %solve_x.1.solved = f32[3,512,512]{2,1,0:T(8,128)S(1)} custom-call(f32[3,512,512]{2,1,0:T(8,128)} %get-tuple-element.29.lines, f32[8,512]{1,0:T(8,128)S(1)} %get-tuple-element.30.beside, f32[2,512]{1,0:T(2,128)S(1)} %copy-done.6, bf16[512,1536]{1,0:T(8,128)(2,1)} %constant.29.clone.table), custom_call_target="tpu_custom_call" | custom-call | flops 2415919104 | bytes 6291456 | tf_op jit(solution)/shard_map/solve_x/pallas_call | solution.py:584
  49.3 4.7 %all-to-all-done.1.got = f32[16,24,128]{2,1,0:T(8,128)S(1)} async-done(((f32[16,24,128]{2,1,0:T(8,128)}), f32[16,24,128]{2,1,0:T(8,128)S(1)}, u32[]{:S(2)}, u32[]{:S(2)}) %all-to-all-start.1) | async-done | bytes 196640 | tf_op jit(solution)/shard_map/across_x/all_to_all | solution.py:582
  54.0 2.5 %final.1 = f32[3,512,512]{2,1,0:T(8,128)} custom-call(f32[16,24,128]{2,1,0:T(8,128)S(1)} %all-to-all-done.1.got, f32[8,512]{1,0:T(8,128)S(1)} %copy-done.1, f32[3,512,512]{2,1,0:T(8,128)S(1)} %solve_x.1.solved), custom_call_target="tpu_custom_call" | custom-call | flops 3145728 | bytes 6291456 | tf_op jit(solution)/shard_map/final/pallas_call | solution.py:594
Async XLA Ops:
  0.0 10.1 %copy-start = (f32[2,512]{1,0:T(2,128)S(1)}, f32[2,512]{1,0:T(2,128)}, u32[]{:S(2)}) copy-start(f32[2,512]{1,0:T(2,128)} %constant.25.clone.ends_y.ends_x) | copy-start | bytes 12292
  0.0 17.9 %copy-start.5 = (f32[16,64]{1,0:T(8,128)S(1)}, f32[16,64]{1,0:T(8,128)}, u32[]{:S(2)}) copy-start(f32[16,64]{1,0:T(8,128)} %constant.24.clone.table) | copy-start | bytes 12292
  0.0 17.9 %copy-start.7 = (f32[8,32]{1,0:T(8,128)S(1)}, f32[8,32]{1,0:T(8,128)}, u32[]{:S(2)}) copy-start(f32[8,32]{1,0:T(8,128)} %constant.26.clone.near_ends) | copy-start | bytes 3076
  0.0 23.6 %copy-start.1 = (f32[8,512]{1,0:T(8,128)S(1)}, f32[8,512]{1,0:T(8,128)}, u32[]{:S(2)}) copy-start(f32[8,512]{1,0:T(8,128)} %constant.27.clone.rows_x) | copy-start | bytes 49156
  0.0 10.1 %copy-start.3 = (f32[512]{0:T(512)S(1)}, f32[512]{0:T(512)}, u32[]{:S(2)}) copy-start(f32[512]{0:T(512)} %param.14) | copy-start | bytes 6148
  0.0 10.1 %copy-start.2 = (f32[512]{0:T(512)S(1)}, f32[512]{0:T(512)}, u32[]{:S(2)}) copy-start(f32[512]{0:T(512)} %param.13) | copy-start | bytes 6148
  2.0 15.8 %collective-permute-start = (f32[16,512]{1,0:T(8,128)S(1)}, f32[16,512]{1,0:T(8,128)S(1)}, u32[]{:S(2)}, u32[]{:S(2)}) collective-permute-start(f32[16,512]{1,0:T(8,128)S(1)} %get-tuple-element.18.x_tail), channel_id=1, source_target_pairs={{0,16},{16,32},{32,48},{48,64},{64,80},{80,96},{96,112},{112,128},... | collective-permute-start | bytes 98312 | tf_op jit(solution)/shard_map/halos/ppermute | solution.py:525
  5.1 12.8 %collective-permute-start.1 = (f32[16,512]{1,0:T(8,128)S(1)}, f32[16,512]{1,0:T(8,128)S(1)}, u32[]{:S(2)}, u32[]{:S(2)}) collective-permute-start(f32[16,512]{1,0:T(8,128)S(1)} %get-tuple-element.19.x_head), channel_id=1, source_target_pairs={{16,0},{32,16},{48,32},{64,48},{80,64},{96,80},{112,96},{128,112},... | collective-permute-start | bytes 98312 | tf_op jit(solution)/shard_map/halos/ppermute | solution.py:526
  5.3 12.5 %collective-permute-start.2 = (f32[16,512]{1,0:T(8,128)S(1)}, f32[16,512]{1,0:T(8,128)S(1)}, u32[]{:S(2)}, u32[]{:S(2)}) collective-permute-start(f32[16,512]{1,0:T(8,128)S(1)} %get-tuple-element.20.y_tail), channel_id=1, source_target_pairs={{0,1},{1,2},{2,3},{3,4},{4,5},{5,6},{6,7},{7,8},{8,9},{9,10},{10,1... | collective-permute-start | bytes 98312 | tf_op jit(solution)/shard_map/halos/ppermute | solution.py:527
  6.4 11.5 %collective-permute-start.3 = (f32[16,512]{1,0:T(8,128)S(1)}, f32[16,512]{1,0:T(8,128)S(1)}, u32[]{:S(2)}, u32[]{:S(2)}) collective-permute-start(f32[16,512]{1,0:T(8,128)S(1)} %get-tuple-element.21.y_head), channel_id=1, source_target_pairs={{1,0},{2,1},{3,2},{4,3},{5,4},{6,5},{7,6},{8,7},{9,8},{10,9},{11,1... | collective-permute-start | bytes 98312 | tf_op jit(solution)/shard_map/halos/ppermute | solution.py:528
  20.1 10.4 %all-to-all-start = ((f32[16,24,128]{2,1,0:T(8,128)}), f32[16,24,128]{2,1,0:T(8,128)S(1)}, u32[]{:S(2)}, u32[]{:S(2)}) async-start(f32[16,24,128]{2,1,0:T(8,128)} %get-tuple-element.23), calls=%async_computation | async-start | bytes 393216 | tf_op jit(solution)/shard_map/across_y/all_to_all | solution.py:559
  23.7 6.9 %copy-start.4 = (f32[16,64]{1,0:T(8,128)S(1)}, f32[16,64]{1,0:T(8,128)}, u32[]{:S(2)}) copy-start(f32[16,64]{1,0:T(8,128)} %constant.23.clone.table) | copy-start | bytes 12292
  23.7 6.9 %copy-start.6 = (f32[2,512]{1,0:T(2,128)S(1)}, f32[2,512]{1,0:T(2,128)}, u32[]{:S(2)}) copy-start(f32[2,512]{1,0:T(2,128)} %constant.28.clone.sides_y) | copy-start | bytes 12292
  32.0 21.9 %all-to-all-start.1 = ((f32[16,24,128]{2,1,0:T(8,128)}), f32[16,24,128]{2,1,0:T(8,128)S(1)}, u32[]{:S(2)}, u32[]{:S(2)}) async-start(f32[16,24,128]{2,1,0:T(8,128)} %get-tuple-element.28), calls=%async_computation.1 | async-start | bytes 393216 | tf_op jit(solution)/shard_map/across_x/all_to_all | solution.py:582

commit v3 on v2

--- a/solution.py
+++ b/solution.py
@@ -55,10 +55,10 @@
     return high, (values - high.astype(F32)).astype(BF16)
 
 
-def split_table(table, axis):
+def split_table(table):
     high = np.asarray(table, np.float32).astype(BF16)
     low = (np.asarray(table, np.float64) - high.astype(np.float64)).astype(BF16)
-    return np.concatenate([high, high, low], axis=axis)
+    return np.stack([high, low])
 
 
 def padded_rows(rows, count):
@@ -70,44 +70,45 @@
     return [slice(at, at + 128) for at in range(0, cells, 128)]
 
 
-def edges_kernel(field, x_head, x_tail, y_head, y_tail, top, bottom, left, right, columns, sems):
+def edges_kernel(field, x_head, x_tail, y_head, y_tail, top, bottom, left, right, sems):
     rows, cells = field.shape[1], field.shape[2]
-    copies = [
+    ends = [
         pltpu.make_async_copy(field.at[:, 0:8, :], top, sems.at[0]),
         pltpu.make_async_copy(field.at[:, rows - 8 : rows, :], bottom, sems.at[1]),
-        pltpu.make_async_copy(field.at[:, :, 0:128], left, sems.at[2]),
-        pltpu.make_async_copy(field.at[:, :, cells - 128 : cells], right, sems.at[3]),
     ]
-    for copy in copies:
-        copy.start()
-    x_head[...] = jnp.zeros(x_head.shape, F32)
-    x_tail[...] = jnp.zeros(x_tail.shape, F32)
-    for copy in copies[:2]:
+    blocks = lane_blocks(rows)
+    sides = [
+        [
+            pltpu.make_async_copy(field.at[:, block, 0:128], left.at[:, block, :], sems.at[2 + 2 * at]),
+            pltpu.make_async_copy(field.at[:, block, cells - 128 : cells], right.at[:, block, :], sems.at[3 + 2 * at]),
+        ]
+        for at, block in enumerate(blocks)
+    ]
+    for group in sides + [ends]:
+        for copy in group:
+            copy.start()
+    x_head[9:16, :] = jnp.zeros((7, cells), F32)
+    x_tail[9:16, :] = jnp.zeros((7, cells), F32)
+    lane = lax.broadcasted_iota(jnp.int32, (128, 128), 1)
+    for group, block in zip(sides, blocks):
+        for copy in group:
+            copy.wait()
+        packed = left[0, block, :]
+        for comp in range(3):
+            if comp:
+                packed = jnp.where(lane < 3 * comp, packed, pltpu.roll(left[comp, block, :], 3 * comp, 1))
+        packed = jnp.where(lane < 9, packed, 0.0)
+        for comp in range(3):
+            here = pltpu.roll(right[comp, block, :], 19 + 3 * comp, 1)
+            packed = jnp.where((lane >= 16 + 3 * comp) & (lane < 19 + 3 * comp), here, packed)
+        turned = packed.T
+        y_head[:, block] = turned[0:16, :]
+        y_tail[:, block] = turned[16:32, :]
+    for copy in ends:
         copy.wait()
     for comp in range(3):
         x_head[3 * comp : 3 * comp + 3, :] = top[comp, 0:3, :]
         x_tail[3 * comp : 3 * comp + 3, :] = bottom[comp, 5:8, :]
-    for copy in copies[2:]:
-        copy.wait()
-    edge_columns(left, right, y_head, y_tail, columns)
-
-
-def edge_columns(left, right, y_head, y_tail, columns):
-    cells_x = left.shape[1]
-    lane = lax.broadcasted_iota(jnp.int32, (64, 128), 1)
-    for at in range(0, cells_x, 64):
-        packed = jnp.zeros((64, 128), F32)
-        for comp in range(3):
-            here = left[comp, at : at + 64, :]
-            here = pltpu.roll(here, 3 * comp, 1) if comp else here
-            packed = jnp.where((lane >= 3 * comp) & (lane < 3 * comp + 3), here, packed)
-            here = pltpu.roll(right[comp, at : at + 64, :], 19 + 3 * comp, 1)
-            packed = jnp.where((lane >= 16 + 3 * comp) & (lane < 19 + 3 * comp), here, packed)
-        columns[at : at + 64, :] = packed
-    for block in lane_blocks(cells_x):
-        turned = columns[block, :].T
-        y_head[:, block] = turned[0:16, :]
-        y_tail[:, block] = turned[16:32, :]
 
 
 def inner_kernel(scale, field, m1, m2, ends_y, inner, ends, padded, result, along_rows, sums, load_sems, store_sems):
@@ -225,15 +226,19 @@
         shares[other] = straight * values + crossed * swapped
 
 
+def edge_lines(shape):
+    rows = lax.broadcasted_iota(jnp.int32, shape, 0)
+    line = rows - 3 * ((rows >= 3).astype(jnp.int32) + (rows >= 6).astype(jnp.int32))
+    return rows, jnp.where(rows < 9, line, 3)
+
+
 def halo_sides(before, after, curves, bends_head, bends_tail):
-    rows = lax.broadcasted_iota(jnp.int32, (16, 1), 0)
-    line = rows - 3 * ((rows >= 3).astype(jnp.int32) + (rows >= 6).astype(jnp.int32))
-    inside = rows < 9
+    _, line = edge_lines(before.shape)
     head = tail = None
     for k in (1, 2, 3):
         a, b = FIRST[k - 1], SECOND[k - 1]
-        low = jnp.where(inside & (line < k), (b * curves[0] - a * bends_head), 0.0)
-        high = jnp.where(inside & (line >= 3 - k), (b * curves[1] + a * bends_tail), 0.0)
+        low = jnp.where(line < k, b * curves[0] - a * bends_head, 0.0)
+        high = jnp.where((line >= 3 - k) & (line < 3), b * curves[1] + a * bends_tail, 0.0)
         low = low * (pltpu.roll(before, 16 - (3 - k), 0) if k < 3 else before)
         high = high * (pltpu.roll(after, 3 - k, 0) if k < 3 else after)
         head = low if head is None else head + low
@@ -243,14 +248,6 @@
 
 def tiled_lines(lines):
     return jnp.concatenate([lines, lines, lines, jnp.zeros((7, lines.shape[1]), F32)], axis=0)
-
-
-def line_column(row, first):
-    rows = lax.broadcasted_iota(jnp.int32, (16, 1), 0)
-    column = jnp.zeros((16, 1), F32)
-    for at in range(9):
-        column = jnp.where(rows == at, row[0:1, first + at % 3 : first + at % 3 + 1], column)
-    return column
 
 
 def halo_kernel(
@@ -267,10 +264,14 @@
         -scale * tiled_lines(x_head[0:3, :]),
         -scale * tiled_lines(x_tail[0:3, :]),
     )
-    row1, row2 = m1[...], m2[...]
-    ends_at = (0, cells_y - 3)
-    slopes = [line_column(row1, at) for at in ends_at]
-    offsets = [visc * line_column(row2, at) for at in ends_at]
+    first, last = slice(0, 128), slice(cells_y - 128, cells_y)
+    near = padded_rows([m1[:, first], m1[:, last], m2[:, first], m2[:, last]], 128).T
+    spread = [
+        tiled_lines(jnp.broadcast_to(near[lines, at : at + 1], (3, cells_x)))
+        for at, lines in enumerate((slice(0, 3), slice(125, 128), slice(0, 3), slice(125, 128)))
+    ]
+    slopes = spread[0:2]
+    offsets = [visc * offset for offset in spread[2:4]]
     bends = [
         offsets[side] - (scale * slopes[side]) * tiled_lines(lines[3:6, :])
         for side, lines in enumerate((y_head, y_tail))
@@ -293,8 +294,7 @@
         precision=lax.Precision.HIGHEST,
         preferred_element_type=F32,
     )
-    rows = lax.broadcasted_iota(jnp.int32, (16, 128), 0)
-    line = rows - 3 * ((rows >= 3).astype(jnp.int32) + (rows >= 6).astype(jnp.int32))
+    rows, line = edge_lines((16, 128))
     lane = lax.broadcasted_iota(jnp.int32, (16, 128), 1)
     extra = []
     for end in (0, 1):
@@ -322,63 +322,61 @@
         turned[block, :] = tall[:, block].T
 
 
-def solve_y_kernel(
-    inner, delta_x, delta_y, rows_x, table, lines, edges,
-    work, result, inverse, turned, wide, sems,
+def solve_kernel(
+    inner, delta_x, delta_y, table_y, table_x, solved, edges,
+    work, inverse_y, inverse_x, high, low, turned, sems,
 ):
-    cells_x, cells = result.shape[1], result.shape[2]
+    cells_x, cells = solved.shape[1], solved.shape[2]
     loads = [pltpu.make_async_copy(inner.at[comp], work.at[comp], sems.at[comp]) for comp in range(3)]
-    tables = [pltpu.make_async_copy(table, inverse, sems.at[3])]
-    for copy in loads[:1] + tables + loads[1:]:
+    tables_y = [pltpu.make_async_copy(table_y.at[at], inverse_y.at[at], sems.at[3 + at]) for at in (0, 1)]
+    tables_x = [pltpu.make_async_copy(table_x.at[at], inverse_x.at[at], sems.at[5 + at]) for at in (0, 1)]
+    for copy in loads[:1] + tables_y + tables_x + loads[1:]:
         copy.start()
-    turned_rows(rows_x[...], turned)
-    for at in range(0, cells_x, 128):
-        for end in (0, 1):
-            wide[end, at : at + 128, :] = jnp.broadcast_to(turned[at : at + 128, end : end + 1], (128, 128))
     turned_rows(delta_y[...], turned)
     lane = lax.broadcasted_iota(jnp.int32, (128, 128), 1)
-    found = [None] * 6
     half = cells_x // 2
-    stores = []
+    halves = (slice(0, half), slice(half, cells_x))
     for comp in range(3):
         loads[comp].wait()
-        for at in range(0, cells_x, 128):
-            tile = turned[at : at + 128, :]
+        for block in lane_blocks(cells_x):
+            tile = turned[block, :]
             near = pltpu.roll(tile, 128 - 3 * comp, 1) if comp else tile
-            work[comp, at : at + 128, 0:128] += jnp.where(lane < 3, near, 0.0)
+            work[comp, block, 0:128] += jnp.where(lane < 3, near, 0.0)
             far = pltpu.roll(tile, 109 - 3 * comp, 1)
-            work[comp, at : at + 128, cells - 128 : cells] += jnp.where(lane >= 125, far, 0.0)
+            work[comp, block, cells - 128 : cells] += jnp.where(lane >= 125, far, 0.0)
         work[comp, 0:3, :] += delta_x[3 * comp : 3 * comp + 3, :]
         work[comp, cells_x - 3 : cells_x, :] += delta_x[16 + 3 * comp : 19 + 3 * comp, :]
         if comp == 0:
-            for copy in tables:
+            for copy in tables_y:
                 copy.wait()
-        for at in (0, half):
-            high, low = split(work[comp, at : at + half, :])
-            solved = jnp.dot(
-                jnp.concatenate([high, low, high], axis=1), inverse[...], preferred_element_type=F32
+        for rows in halves:
+            above, below = split(work[comp, rows, :])
+            high[rows, :], low[rows, :] = split(
+                jnp.dot(above, inverse_y[0], preferred_element_type=F32)
+                + jnp.dot(below, inverse_y[0], preferred_element_type=F32)
+                + jnp.dot(above, inverse_y[1], preferred_element_type=F32)
             )
-            result[comp, at : at + half, :] = solved
-            for end in (0, 1):
-                weights = wide[end, at : at + half, :]
-                value = jnp.concatenate(
-                    [
-                        jnp.sum((solved[:, lanes] * weights).reshape(half // 8, 8, 128), axis=0)
-                        for lanes in lane_blocks(cells)
-                    ],
-                    axis=1,
-                )
-                where = 3 * end + comp
-                found[where] = value if found[where] is None else found[where] + value
-        store = pltpu.make_async_copy(result.at[comp], lines.at[comp], sems.at[4 + comp])
-        store.start()
-        stores.append(store)
-    edges[...] = padded_rows([jnp.sum(value, axis=0, keepdims=True) for value in found], 8)
-    for store in stores:
-        store.wait()
-
-
-def ends_kernel(index, table, got, edges, ends_x, sides_y, shares, beside):
+        if comp == 0:
+            for copy in tables_x:
+                copy.wait()
+        for rows in halves:
+            solved[comp, rows, :] = (
+                jnp.dot(inverse_x[0, rows, :], high[...], preferred_element_type=F32)
+                + jnp.dot(inverse_x[0, rows, :], low[...], preferred_element_type=F32)
+                + jnp.dot(inverse_x[1, rows, :], high[...], preferred_element_type=F32)
+            )
+    edges[...] = padded_rows(
+        [solved[comp, 0:1, :] for comp in range(3)] + [solved[comp, cells_x - 1 : cells_x, :] for comp in range(3)], 8
+    )
+
+
+def chain_numbers(head, tail):
+    gain = 1.0 / (1.0 - tail[-1] * head[0])
+    return float(gain), float(gain * head[-1]), float(tail[-1]), float(head[0])
+
+
+def ends_kernel(chain, got, edges, ends_x, sides_y, out, beside):
+    gain, ratio, behind, _ = chain
     total = got[0]
     for block in range(1, got.shape[0]):
         total = total + got[block]
@@ -391,50 +389,80 @@
             rows.append(
                 value[comp : comp + 1] * sides_y[0:1, :] + value[comp + 3 : comp + 4] * sides_y[1:2, :]
             )
-    write_shares(table, index, edges[...] + padded_rows(rows, 8), shares)
-
-
-def solve_x_kernel(lines, beside, sides_y, table, solved, work, inverse, turned, sems):
+    values = edges[...] + padded_rows(rows, 8)
+    links = gain * values[3:6] + (gain * ratio * behind) * values[0:3]
+    out[...] = padded_rows([links, values[0:3]], 8)
+
+
+def pair_kernel(chain, index, own, other, out):
+    even = index[0] % 2 == 0
+    first = jnp.where(even, own[...], other[...])
+    second = jnp.where(even, other[...], own[...])
+    out[...] = padded_rows([second[0:3] + chain[1] * first[0:3], first[3:6]], 8)
+
+
+def window_kernel(chain, own, below, above, out):
+    step = chain[1] * chain[1]
+    out[...] = above[...] + step * own[...] + (step * step) * below[...]
+
+
+def beside_kernel(solved, beside, sides_y, table, token, updated, inverse, turned, sems):
     cells_x, cells_y = solved.shape[1], solved.shape[2]
-    tables = [pltpu.make_async_copy(table, inverse, sems.at[3])]
-    loads = [pltpu.make_async_copy(lines.at[comp], work.at[comp], sems.at[comp]) for comp in range(3)]
-    for copy in loads[:1] + tables + loads[1:]:
+    copies = [pltpu.make_async_copy(table.at[at], inverse.at[at], sems.at[at]) for at in (0, 1)]
+    for copy in copies:
         copy.start()
-    turned_rows(beside[...], turned)
-    half = cells_y // 2
-    before, after = sides_y[0:1, :], sides_y[1:2, :]
-    for comp in range(3):
-        loads[comp].wait()
-        if comp == 0:
-            for copy in tables:
-                copy.wait()
-        for at in (0, half):
-            block = slice(at, at + half)
-            full = (
-                work[comp, :, block]
-                + turned[:, comp : comp + 1] * before[:, block]
-                + turned[:, comp + 3 : comp + 4] * after[:, block]
+    high, low = split(padded_rows([beside[...]], 16))
+    for copy in copies:
+        copy.wait()
+    turned_rows(
+        jnp.dot(high, inverse[0], preferred_element_type=F32)
+        + jnp.dot(low, inverse[0], preferred_element_type=F32)
+        + jnp.dot(high, inverse[1], preferred_element_type=F32),
+        turned,
+    )
+    before = jnp.broadcast_to(sides_y[0:1, :], (8, cells_y))
+    after = jnp.broadcast_to(sides_y[1:2, :], (8, cells_y))
+
+    def step(index, carry):
+        rows = pl.ds(pl.multiple_of(index * 8, 8), 8)
+        here = turned[rows, :]
+        for comp in range(3):
+            updated[comp, rows, :] = solved[comp, rows, :] + (
+                here[:, comp : comp + 1] * before + here[:, comp + 3 : comp + 4] * after
             )
-            high, low = split(full)
-            solved[comp, :, block] = jnp.dot(
-                inverse[...], jnp.concatenate([high, low, high], axis=0), preferred_element_type=F32
-            )
-
-
-def final_kernel(got, rows_x, solved, out, beyond, turned):
+        return carry
+
+    lax.fori_loop(0, cells_x // 8, step, 0, unroll=4)
+
+
+def final_kernel(
+    chain, chips, index, own, other, pair, pair_above, far_below, far_above, rows_x, solved,
+    out, beyond, turned,
+):
     step = pl.program_id(0)
     rows = out.shape[1]
     blocks = lane_blocks(out.shape[2])
+    gain, ratio, behind, ahead = chain
+    link = ratio * ratio
 
     @pl.when(step == 0)
     def _():
         turned_rows(rows_x[...], turned)
-        total = got[0]
-        for block in range(1, got.shape[0]):
-            total = total + got[block]
-        for row in range(6):
-            for at in range(len(blocks)):
-                beyond[row, at] = jnp.broadcast_to(total[6 * at + row : 6 * at + row + 1, :], (8, 128))
+        even = index[0] % 2 == 0
+        chip = (
+            far_below[0:3, :]
+            + link**3 * far_above[0:3, :]
+            + (link**6 * pair_above[0:3, :] + link**7 * pair[0:3, :])
+        ) * (1.0 / (1.0 - link**chips))
+        before = jnp.where(even, chip, other[0:3, :] + ratio * chip)
+        following = jnp.where(even, other[3:6, :], pair_above[3:6, :])
+        first = (gain * behind) * own[3:6, :] + before
+        last = gain * following + ahead * (own[0:3, :] + ratio * before)
+        for comp in range(3):
+            for side, values in enumerate((first, last)):
+                wide = jnp.broadcast_to(values[comp : comp + 1, :], (8, values.shape[1]))
+                for at, block in enumerate(blocks):
+                    beyond[3 * side + comp, at] = wide[:, block]
 
     for at in range(0, rows, 8):
         where = pl.ds(pl.multiple_of(step * rows + at, 8), 8)
@@ -481,9 +509,8 @@
     low_x, up_x, diag_x, sig_x = coefficients(blocks_x * nx)
     low_y, up_y, diag_y, sig_y = coefficients(blocks_y * ny)
     scale = math.sqrt(sig_x * sig_y) / (diag_x * diag_y)
-    inverse_x, head_x, tail_x, among_x = line_tables(nx, low_x, up_x, blocks_x, True)
+    inverse_x, head_x, tail_x, _ = line_tables(nx, low_x, up_x, blocks_x, True)
     inverse_y, head_y, tail_y, among_y = line_tables(ny, low_y, up_y, blocks_y, False)
-    table_x = jnp.asarray(among_x.transpose(1, 0, 2, 3).reshape(blocks_x, 4 * blocks_x), F32)
     table_y = jnp.asarray(among_y.transpose(1, 0, 2, 3).reshape(blocks_y, 4 * blocks_y), F32)
     ends_x = jnp.asarray(np.stack([inverse_x[0], inverse_x[-1]]), F32)
     ends_y = jnp.asarray(np.stack([inverse_y[0], inverse_y[-1]]), F32)
@@ -497,8 +524,9 @@
     rows_x[:4] = np.stack([inverse_x[0], inverse_x[-1], head_x, tail_x])
     rows_x = jnp.asarray(rows_x, F32)
     sides_y = jnp.asarray(np.stack([head_y, tail_y]), F32)
-    parts_x = in_hbm(jnp.asarray(split_table(inverse_x, 1)))
-    parts_y = in_hbm(jnp.asarray(split_table(inverse_y.T, 0)))
+    parts_x = in_hbm(jnp.asarray(split_table(inverse_x)))
+    turned_x = in_hbm(jnp.asarray(split_table(inverse_x.T)))
+    parts_y = in_hbm(jnp.asarray(split_table(inverse_y.T)))
     index_x = lax.axis_index("gx").astype(jnp.int32).reshape(1)
     index_y = lax.axis_index("gy").astype(jnp.int32).reshape(1)
     m1 = metric_first.reshape(1, ny)
@@ -517,7 +545,7 @@
             [struct(16, ny)] * 2 + [struct(16, nx)] * 2,
             [pltpu.VMEM((3, 8, ny), F32)] * 2
             + [pltpu.VMEM((3, nx, 128), F32)] * 2
-            + [pltpu.VMEM((nx, 128), F32), pltpu.SemaphoreType.DMA((4,))],
+            + [pltpu.SemaphoreType.DMA((2 + nx // 64,))],
             10 * nx * 128,
             24 * nx * 128,
         )(velocity)
@@ -557,50 +585,64 @@
         )
     with jax.named_scope("across_y"):
         got_y = lax.all_to_all(shares_y, "gy", 0, 0, tiled=True)
-    with jax.named_scope("solve_y"):
-        lines, edges = call(
-            solve_y_kernel,
-            [HBM] + [VMEM] * 3 + [HBM],
-            [pltpu.HBM((3, nx, ny), F32), struct(8, ny)],
-            [pltpu.VMEM((3, nx, ny), F32)] * 2
-            + [pltpu.VMEM((3 * ny, ny), BF16), pltpu.VMEM((nx, 128), F32), pltpu.VMEM((2, nx, 128), F32)]
-            + [pltpu.SemaphoreType.DMA((7,))],
-            6 * cells * ny,
+    with jax.named_scope("solve"):
+        solved, edges = call(
+            solve_kernel,
+            [HBM] + [VMEM] * 2 + [HBM] * 2,
+            [struct(3, nx, ny), struct(8, ny)],
+            [pltpu.VMEM((3, nx, ny), F32), pltpu.VMEM((2, ny, ny), BF16), pltpu.VMEM((2, nx, nx), BF16)]
+            + [pltpu.VMEM((nx, ny), BF16)] * 2
+            + [pltpu.VMEM((nx, 128), F32), pltpu.SemaphoreType.DMA((7,))],
+            6 * cells * (nx + ny),
             8 * cells,
-            out_specs=[HBM, VMEM],
-        )(in_hbm(inner), delta_x, delta_y, rows_x, parts_y)
+        )(in_hbm(inner), delta_x, delta_y, parts_y, parts_x)
+    chain = chain_numbers(head_x, tail_x)
+    link = struct(8, ny)
     with jax.named_scope("ends_x"):
-        shares_x, beside = call(
-            ends_kernel,
-            [SMEM, SMEM] + [VMEM] * 4,
-            [struct(blocks_x, 6 * (ny // 128), 128), struct(8, nx)],
+        own, beside = call(
+            functools.partial(ends_kernel, chain),
+            [VMEM] * 4,
+            [link, struct(8, nx)],
             [],
             100 * nx,
             500 * nx,
-        )(index_x, table_x, got_y, edges, ends_x, sides_y)
+        )(got_y, edges, ends_x, sides_y)
+
+    def along(values, shift):
+        return lax.ppermute(values, "gx", [(i, (i + shift) % blocks_x) for i in range(blocks_x)])
+
     with jax.named_scope("across_x"):
-        got_x = lax.all_to_all(shares_x, "gx", 0, 0, tiled=True)
-    with jax.named_scope("solve_x"):
+        other = lax.ppermute(own, "gx", [(i, i ^ 1) for i in range(blocks_x)])
+        (pair,) = call(
+            functools.partial(pair_kernel, chain), [SMEM, VMEM, VMEM], [link], [], 10 * nx, 100 * nx
+        )(index_x, own, other)
+        pair_below = along(pair, 2)
+        pair_above = along(pair, -2)
+        (window,) = call(functools.partial(window_kernel, chain), [VMEM] * 3, [link], [], 10 * nx, 100 * nx)(
+            pair, pair_below, pair_above
+        )
+        far_below = along(window, 4)
+        far_above = along(window, -6)
         (solved,) = call(
-            solve_x_kernel,
-            [HBM, VMEM, VMEM, HBM],
+            beside_kernel,
+            [VMEM] * 3 + [HBM, VMEM],
             [struct(3, nx, ny)],
-            [pltpu.VMEM((3, nx, ny), F32), pltpu.VMEM((nx, 3 * nx), BF16), pltpu.VMEM((nx, 128), F32)]
-            + [pltpu.SemaphoreType.DMA((4,))],
-            6 * cells * nx,
+            [pltpu.VMEM((2, nx, nx), BF16), pltpu.VMEM((nx, 128), F32), pltpu.SemaphoreType.DMA((2,))],
+            6 * cells,
             8 * cells,
-        )(in_hbm(lines), beside, sides_y, parts_x)
+            input_output_aliases={0: 0},
+        )(solved, beside, sides_y, turned_x, window)
     with jax.named_scope("final"):
         return call(
-            final_kernel,
-            [VMEM] * 3,
+            functools.partial(final_kernel, chain, blocks_x // 2),
+            [SMEM] + [VMEM] * 8,
             struct(3, nx, ny),
             [pltpu.VMEM((6, ny // 128, 8, 128), F32), pltpu.VMEM((nx, 128), F32)],
             4 * cells,
             8 * cells,
             grid=(nx // 128,),
             out_specs=pl.BlockSpec((3, 128, ny), lambda i: (0, i, 0)),
-        )(got_x, rows_x, solved)
+        )(index_x, own, other, pair, pair_above, far_below, far_above, rows_x, solved)
 
 
 def solution(mesh):

time: 56.8 us -> 52.9 us (0.931)
  the two profiles are of different devices: /device:TPU:1 before, /device:TPU:2 now
where the time goes in v3:
time: 52.9 us; the launch traced here: 52.7 us
  Pallas kernels  25.1 us (47%)
  starting transfers between devices  23.9 us (45%)
  waiting for transfers between devices  3.51 us (7%)
    ppermute x4, starting transfers between devices, along(): lax.ppermute(values, 'gx', [(i, (i + shift) % blocks_x) for i in range(bl...  8.97 us
    pallas_call x1, Pallas kernels, local(): call(functools.partial(inner_kernel, scale), [HBM] + [VMEM] * 3, [pltpu.H...  7.7 us
    pallas_call x1, Pallas kernels, local(): call(solve_kernel, [HBM] + [VMEM] * 2 + [HBM] * 2, [struct(3, nx, ny), st...  7.41 us
    all_to_all x1, starting transfers between devices, local(): got_y = lax.all_to_all(shares_y, 'gy', 0, 0, tiled=True)  5.37 us
    ppermute x1, starting transfers between devices, local(): after_x = lax.ppermute(x_head, 'gx', back_x)  5.31 us
    pallas_call x1, Pallas kernels, local(): call(beside_kernel, [VMEM] * 3 + [HBM, VMEM], [struct(3, nx, ny)], [pltpu...  3.58 us
    ppermute x1, starting transfers between devices, local(): after_y = lax.ppermute(y_head, 'gy', back_y)  2.56 us
    pallas_call x1, Pallas kernels, local(): call(functools.partial(final_kernel, chain, blocks_x // 2), [SMEM] + [VME...  2.52 us
  transfers between devices with their start and end apart: 10, of which 3 were waited for; matrix products, arithmetic and copies ran while one was open for 0% of the time, Pallas kernels for 35%

profile of v3, /device:TPU:2, one launch (start us, length us, event | category | flops | bytes accessed | tf_op | source)
XLA Modules:
  0.0 52.7 jit_solution(15529731509797508436)
XLA Ops:
  0.0 0.0 copy-start
  0.0 0.0 copy-start.5
  0.0 0.0 copy-start.6
  0.0 0.0 copy-start.4
  0.0 0.0 copy-start.3
  0.0 2.0 %edges.1 = (f32[16,512]{1,0:T(8,128)S(1)}, f32[16,512]{1,0:T(8,128)S(1)}, f32[16,512]{1,0:T(8,128)S(1)}, f32[16,512]{1,0:T(8,128)S(1)}) custom-call(f32[3,512,512]{2,1,0:T(8,128)} %field.3), custom_call_target="tpu_custom_call" | custom-call | flops 655360 | bytes 1572864 | tf_op jit(solution)/shard_map/edges/pallas_call | solution.py:542
  2.0 0.0 collective-permute-start
  2.0 5.3 %collective-permute-start.1 = (f32[16,512]{1,0:T(8,128)S(1)}, f32[16,512]{1,0:T(8,128)S(1)}, u32[]{:S(2)}, u32[]{:S(2)}) collective-permute-start(f32[16,512]{1,0:T(8,128)S(1)} %get-tuple-element.19.x_head), channel_id=1, source_target_pairs={{16,0},{32,16},{48,32},{64,48},{80,64},{96,80},{112,96},{128,112},... | collective-permute-start | bytes 98312 | tf_op jit(solution)/shard_map/halos/ppermute | solution.py:554
  7.3 1.6 %collective-permute-start.2 = (f32[16,512]{1,0:T(8,128)S(1)}, f32[16,512]{1,0:T(8,128)S(1)}, u32[]{:S(2)}, u32[]{:S(2)}) collective-permute-start(f32[16,512]{1,0:T(8,128)S(1)} %get-tuple-element.20.y_tail), channel_id=1, source_target_pairs={{0,1},{1,2},{2,3},{3,4},{4,5},{5,6},{6,7},{7,8},{8,9},{9,10},{10,1... | collective-permute-start | bytes 98312 | tf_op jit(solution)/shard_map/halos/ppermute | solution.py:555
  8.9 2.6 %collective-permute-start.3 = (f32[16,512]{1,0:T(8,128)S(1)}, f32[16,512]{1,0:T(8,128)S(1)}, u32[]{:S(2)}, u32[]{:S(2)}) collective-permute-start(f32[16,512]{1,0:T(8,128)S(1)} %get-tuple-element.21.y_head), channel_id=1, source_target_pairs={{1,0},{2,1},{3,2},{4,3},{5,4},{6,5},{7,6},{8,7},{9,8},{10,9},{11,1... | collective-permute-start | bytes 98312 | tf_op jit(solution)/shard_map/halos/ppermute | solution.py:556
  11.5 0.0 copy-done
  11.5 0.0 copy-done.4
  11.5 0.0 copy-done.3
  11.5 7.7 %inner.1 = (f32[3,512,512]{2,1,0:T(8,128)}, f32[8,512]{1,0:T(8,128)S(1)}) custom-call(f32[3,512,512]{2,1,0:T(8,128)} %field.3, f32[1,512]{1,0:T(1,128)S(1)} %bitcast.4, f32[1,512]{1,0:T(1,128)S(1)} %bitcast.6, f32[2,512]{1,0:T(2,128)S(1)} %copy-done), custom_call_target="tpu_custom_call" | custom-call | flops 31457280 | bytes 6291456 | tf_op jit(solution)/shard_map/inner/pallas_call | solution.py:558
  19.2 0.0 collective-permute-done.before_x
  19.2 0.0 collective-permute-done.1.after_x
  19.2 0.0 collective-permute-done.2.before_y
  19.2 0.0 collective-permute-done.3.after_y
  19.2 0.0 copy-done.5
  19.2 0.0 copy-done.6
  19.2 1.7 %halo_part.1 = (f32[16,24,128]{2,1,0:T(8,128)}, f32[32,512]{1,0:T(8,128)S(1)}, f32[32,512]{1,0:T(8,128)S(1)}) custom-call(s32[1]{0:T(128)} %bitcast.1.index, f32[16,64]{1,0:T(8,128)S(1)} %copy-done.5, f32[16,512]{1,0:T(8,128)S(1)} %collective-permute-done.before_x, f32[16,512]{1,0:T(8,128)S(1)} %collective-permute-done.1.after_x, ...), custom_call_target="tpu_custom_call" | custom-call | flops 512000 | bytes 256000 | tf_op jit(solution)/shard_map/halo_part/pallas_call | solution.py:575
  21.0 5.4 %all-to-all-start = ((f32[16,24,128]{2,1,0:T(8,128)}), f32[16,24,128]{2,1,0:T(8,128)S(1)}, u32[]{:S(2)}, u32[]{:S(2)}) async-start(f32[16,24,128]{2,1,0:T(8,128)} %get-tuple-element.23), calls=%async_computation | async-start | bytes 393216 | tf_op jit(solution)/shard_map/across_y/all_to_all | solution.py:587
  26.4 0.0 copy-start.2
  26.4 7.4 %solve.1 = (f32[3,512,512]{2,1,0:T(8,128)S(1)}, f32[8,512]{1,0:T(8,128)S(1)}) custom-call(f32[3,512,512]{2,1,0:T(8,128)} %get-tuple-element.24.inner, f32[32,512]{1,0:T(8,128)S(1)} %get-tuple-element.25.delta_x, f32[32,512]{1,0:T(8,128)S(1)} %get-tuple-element.26.delta_y, bf16[2,512,512]{2,1,0:T(8,128)(2,1)} %constant.27.clone.table_y.table, ...), custom_call_target="tpu_custom_call" | custom-call | flops 4831838208 | bytes 6291456 | tf_op jit(solution)/shard_map/solve/pallas_call | solution.py:589
  33.8 0.0 all-to-all-done.got
  33.8 0.0 copy-done.2
  33.8 0.1 ends_x.2
  33.9 0.1 collective-permute-start.4
  34.0 1.2 %collective-permute-done.4.other = f32[8,512]{1,0:T(8,128)S(1)} collective-permute-done((f32[8,512]{1,0:T(8,128)S(1)}, f32[8,512]{1,0:T(8,128)S(1)}, u32[]{:S(2)}, u32[]{:S(2)}) %collective-permute-start.4) | collective-permute-done | bytes 16416 | tf_op jit(solution)/shard_map/across_x/ppermute | solution.py:615
  35.2 0.1 collective-permute-start.6
  35.3 3.2 %collective-permute-start.5 = (f32[8,512]{1,0:T(8,128)S(1)}, f32[8,512]{1,0:T(8,128)S(1)}, u32[]{:S(2)}, u32[]{:S(2)}) collective-permute-start(f32[8,512]{1,0:T(8,128)S(1)} %across_x.3.own.pair), channel_id=1, source_target_pairs={{0,224},{16,240},{32,0},{48,16},{64,32},{80,48},{96,64},{112,80},{... | collective-permute-start | bytes 49160 | tf_op jit(solution)/shard_map/across_x/ppermute | solution.py:612
  38.5 1.7 %collective-permute-done.6.below = f32[8,512]{1,0:T(8,128)S(1)} collective-permute-done((f32[8,512]{1,0:T(8,128)S(1)}, f32[8,512]{1,0:T(8,128)S(1)}, u32[]{:S(2)}, u32[]{:S(2)}) %collective-permute-start.6) | collective-permute-done | bytes 16416 | tf_op jit(solution)/shard_map/across_x/ppermute | solution.py:612
  40.2 0.0 collective-permute-done.5.above.pair_above
  40.3 3.0 %collective-permute-start.8 = (f32[8,512]{1,0:T(8,128)S(1)}, f32[8,512]{1,0:T(8,128)S(1)}, u32[]{:S(2)}, u32[]{:S(2)}) collective-permute-start(f32[8,512]{1,0:T(8,128)S(1)} %across_x.4.token), channel_id=1, source_target_pairs={{0,160},{16,176},{32,192},{48,208},{64,224},{80,240},{96,0},{112,1... | collective-permute-start | bytes 49160 | tf_op jit(solution)/shard_map/across_x/ppermute | solution.py:612
  43.3 2.6 %collective-permute-start.7 = (f32[8,512]{1,0:T(8,128)S(1)}, f32[8,512]{1,0:T(8,128)S(1)}, u32[]{:S(2)}, u32[]{:S(2)}) collective-permute-start(f32[8,512]{1,0:T(8,128)S(1)} %across_x.4.token), channel_id=1, source_target_pairs={{0,64},{16,80},{32,96},{48,112},{64,128},{80,144},{96,160},{112,17... | collective-permute-start | bytes 49160 | tf_op jit(solution)/shard_map/across_x/ppermute | solution.py:612
  45.9 0.0 copy-start.1
  45.9 3.6 %across_x.5.solved = f32[3,512,512]{2,1,0:T(8,128)S(1)} custom-call(f32[3,512,512]{2,1,0:T(8,128)S(1)} %get-tuple-element.29.solved, f32[8,512]{1,0:T(8,128)S(1)} %get-tuple-element.30.beside, f32[2,512]{1,0:T(2,128)S(1)} %copy-done.2, bf16[2,512,512]{2,1,0:T(8,128)(2,1)} %constant.27.clone.table_y.table, ...), custom_call_target="tpu_custom_call", output_to_operand_aliasing={{}: (0, {})} | custom-call | flops 4718592 | bytes 6291456 | tf_op jit(solution)/shard_map/across_x/pallas_call | solution.py:626
  49.5 0.0 collective-permute-done.8.far_above
  49.5 0.6 %collective-permute-done.7.far_below = f32[8,512]{1,0:T(8,128)S(1)} collective-permute-done((f32[8,512]{1,0:T(8,128)S(1)}, f32[8,512]{1,0:T(8,128)S(1)}, u32[]{:S(2)}, u32[]{:S(2)}) %collective-permute-start.7) | collective-permute-done | bytes 16416 | tf_op jit(solution)/shard_map/across_x/ppermute | solution.py:612
  50.1 0.0 copy-done.1
  50.1 2.5 %final.1 = f32[3,512,512]{2,1,0:T(8,128)} custom-call(s32[1]{0:T(128)} %bitcast.index, f32[8,512]{1,0:T(8,128)S(1)} %get-tuple-element.28.own, f32[8,512]{1,0:T(8,128)S(1)} %collective-permute-done.4.other, f32[8,512]{1,0:T(8,128)S(1)} %across_x.3.own.pair, f32[8,512]{1,0:T(8,128)S(1)} %collective-permute-done.5.above.pair_above, ...), custom_call_target="tpu_custom_call" | custom-call | flops 3145728 | bytes 6291456 | tf_op jit(solution)/shard_map/final/pallas_call | solution.py:636
  (2 shorter events, 0.0 us)
Async XLA Ops:
  0.0 11.5 %copy-start = (f32[2,512]{1,0:T(2,128)S(1)}, f32[2,512]{1,0:T(2,128)}, u32[]{:S(2)}) copy-start(f32[2,512]{1,0:T(2,128)} %constant.22.clone.ends_y.ends_x) | copy-start | bytes 12292
  0.0 19.2 %copy-start.5 = (f32[16,64]{1,0:T(8,128)S(1)}, f32[16,64]{1,0:T(8,128)}, u32[]{:S(2)}) copy-start(f32[16,64]{1,0:T(8,128)} %constant.21.clone.table) | copy-start | bytes 12292
  0.0 19.2 %copy-start.6 = (f32[8,32]{1,0:T(8,128)S(1)}, f32[8,32]{1,0:T(8,128)}, u32[]{:S(2)}) copy-start(f32[8,32]{1,0:T(8,128)} %constant.23.clone.near_ends) | copy-start | bytes 3076
  0.0 11.5 %copy-start.4 = (f32[512]{0:T(512)S(1)}, f32[512]{0:T(512)}, u32[]{:S(2)}) copy-start(f32[512]{0:T(512)} %param.14) | copy-start | bytes 6148
  0.0 11.5 %copy-start.3 = (f32[512]{0:T(512)S(1)}, f32[512]{0:T(512)}, u32[]{:S(2)}) copy-start(f32[512]{0:T(512)} %param.13) | copy-start | bytes 6148
  2.0 17.2 %collective-permute-start = (f32[16,512]{1,0:T(8,128)S(1)}, f32[16,512]{1,0:T(8,128)S(1)}, u32[]{:S(2)}, u32[]{:S(2)}) collective-permute-start(f32[16,512]{1,0:T(8,128)S(1)} %get-tuple-element.18.x_tail), channel_id=1, source_target_pairs={{0,16},{16,32},{32,48},{48,64},{64,80},{80,96},{96,112},{112,128},... | collective-permute-start | bytes 98312 | tf_op jit(solution)/shard_map/halos/ppermute | solution.py:553
  2.0 17.2 %collective-permute-start.1 = (f32[16,512]{1,0:T(8,128)S(1)}, f32[16,512]{1,0:T(8,128)S(1)}, u32[]{:S(2)}, u32[]{:S(2)}) collective-permute-start(f32[16,512]{1,0:T(8,128)S(1)} %get-tuple-element.19.x_head), channel_id=1, source_target_pairs={{16,0},{32,16},{48,32},{64,48},{80,64},{96,80},{112,96},{128,112},... | collective-permute-start | bytes 98312 | tf_op jit(solution)/shard_map/halos/ppermute | solution.py:554
  7.3 11.9 %collective-permute-start.2 = (f32[16,512]{1,0:T(8,128)S(1)}, f32[16,512]{1,0:T(8,128)S(1)}, u32[]{:S(2)}, u32[]{:S(2)}) collective-permute-start(f32[16,512]{1,0:T(8,128)S(1)} %get-tuple-element.20.y_tail), channel_id=1, source_target_pairs={{0,1},{1,2},{2,3},{3,4},{4,5},{5,6},{6,7},{7,8},{8,9},{9,10},{10,1... | collective-permute-start | bytes 98312 | tf_op jit(solution)/shard_map/halos/ppermute | solution.py:555
  8.9 10.3 %collective-permute-start.3 = (f32[16,512]{1,0:T(8,128)S(1)}, f32[16,512]{1,0:T(8,128)S(1)}, u32[]{:S(2)}, u32[]{:S(2)}) collective-permute-start(f32[16,512]{1,0:T(8,128)S(1)} %get-tuple-element.21.y_head), channel_id=1, source_target_pairs={{1,0},{2,1},{3,2},{4,3},{5,4},{6,5},{7,6},{8,7},{9,8},{10,9},{11,1... | collective-permute-start | bytes 98312 | tf_op jit(solution)/shard_map/halos/ppermute | solution.py:556
  21.0 12.8 %all-to-all-start = ((f32[16,24,128]{2,1,0:T(8,128)}), f32[16,24,128]{2,1,0:T(8,128)S(1)}, u32[]{:S(2)}, u32[]{:S(2)}) async-start(f32[16,24,128]{2,1,0:T(8,128)} %get-tuple-element.23), calls=%async_computation | async-start | bytes 393216 | tf_op jit(solution)/shard_map/across_y/all_to_all | solution.py:587
  26.4 7.4 %copy-start.2 = (f32[2,512]{1,0:T(2,128)S(1)}, f32[2,512]{1,0:T(2,128)}, u32[]{:S(2)}) copy-start(f32[2,512]{1,0:T(2,128)} %constant.25.clone.sides_y) | copy-start | bytes 12292
  33.9 1.3 %collective-permute-start.4 = (f32[8,512]{1,0:T(8,128)S(1)}, f32[8,512]{1,0:T(8,128)S(1)}, u32[]{:S(2)}, u32[]{:S(2)}) collective-permute-start(f32[8,512]{1,0:T(8,128)S(1)} %get-tuple-element.28.own), channel_id=1, source_target_pairs={{0,16},{16,0},{32,48},{48,32},{64,80},{80,64},{96,112},{112,96},{1... | collective-permute-start | bytes 49160 | tf_op jit(solution)/shard_map/across_x/ppermute | solution.py:615
  35.2 5.0 %collective-permute-start.6 = (f32[8,512]{1,0:T(8,128)S(1)}, f32[8,512]{1,0:T(8,128)S(1)}, u32[]{:S(2)}, u32[]{:S(2)}) collective-permute-start(f32[8,512]{1,0:T(8,128)S(1)} %across_x.3.own.pair), channel_id=1, source_target_pairs={{0,32},{16,48},{32,64},{48,80},{64,96},{80,112},{96,128},{112,144}... | collective-permute-start | bytes 49160 | tf_op jit(solution)/shard_map/across_x/ppermute | solution.py:612
  35.3 4.9 %collective-permute-start.5 = (f32[8,512]{1,0:T(8,128)S(1)}, f32[8,512]{1,0:T(8,128)S(1)}, u32[]{:S(2)}, u32[]{:S(2)}) collective-permute-start(f32[8,512]{1,0:T(8,128)S(1)} %across_x.3.own.pair), channel_id=1, source_target_pairs={{0,224},{16,240},{32,0},{48,16},{64,32},{80,48},{96,64},{112,80},{... | collective-permute-start | bytes 49160 | tf_op jit(solution)/shard_map/across_x/ppermute | solution.py:612
  40.3 9.3 %collective-permute-start.8 = (f32[8,512]{1,0:T(8,128)S(1)}, f32[8,512]{1,0:T(8,128)S(1)}, u32[]{:S(2)}, u32[]{:S(2)}) collective-permute-start(f32[8,512]{1,0:T(8,128)S(1)} %across_x.4.token), channel_id=1, source_target_pairs={{0,160},{16,176},{32,192},{48,208},{64,224},{80,240},{96,0},{112,1... | collective-permute-start | bytes 49160 | tf_op jit(solution)/shard_map/across_x/ppermute | solution.py:612
  43.3 6.8 %collective-permute-start.7 = (f32[8,512]{1,0:T(8,128)S(1)}, f32[8,512]{1,0:T(8,128)S(1)}, u32[]{:S(2)}, u32[]{:S(2)}) collective-permute-start(f32[8,512]{1,0:T(8,128)S(1)} %across_x.4.token), channel_id=1, source_target_pairs={{0,64},{16,80},{32,96},{48,112},{64,128},{80,144},{96,160},{112,17... | collective-permute-start | bytes 49160 | tf_op jit(solution)/shard_map/across_x/ppermute | solution.py:612
  45.9 4.2 %copy-start.1 = (f32[8,512]{1,0:T(8,128)S(1)}, f32[8,512]{1,0:T(8,128)}, u32[]{:S(2)}) copy-start(f32[8,512]{1,0:T(8,128)} %constant.24.clone.rows_x) | copy-start | bytes 49156

commit v4 on v3

--- a/solution.py
+++ b/solution.py
@@ -14,8 +14,9 @@
 FIRST = (45.0 / 60.0, -9.0 / 60.0, 1.0 / 60.0)
 SECOND = (270.0 / 180.0, -27.0 / 180.0, 2.0 / 180.0)
 CENTRE = -490.0 / 180.0
-CUTS = (0, 8, 24, 56, 64)
-UNROLL = 8
+CUTS = (0, 4, 16, 64)
+UNROLL = 16
+OUT_CUTS = (0, 4, 16, 32, 48, 64)
 F32 = jnp.float32
 BF16 = jnp.bfloat16
 VMEM_LIMIT = 24 * 1024 * 1024
@@ -111,7 +112,7 @@
         x_tail[3 * comp : 3 * comp + 3, :] = bottom[comp, 5:8, :]
 
 
-def inner_kernel(scale, field, m1, m2, ends_y, inner, ends, padded, result, along_rows, sums, load_sems, store_sems):
+def inner_kernel(scale, field, m1, m2, ends_y, result, ends, padded, along_rows, sums, load_sems):
     rows, cells = result.shape[1], result.shape[2]
     blocks = lane_blocks(cells)
     count = len(blocks)
@@ -186,21 +187,13 @@
                 result[comp, pl.ds(row, 8), block] = totals[comp][at]
         return carry
 
-    stores = []
     for which, (first, final) in enumerate(spans):
         for copy in loads[which]:
             copy.wait()
-        lax.fori_loop(first // 8, final // 8, step, 0, unroll=UNROLL)
-        store = pltpu.make_async_copy(
-            result.at[:, first:final, :], inner.at[:, first:final, :], store_sems.at[which]
-        )
-        store.start()
-        stores.append(store)
+        lax.fori_loop(first // 8, final // 8, step, 0, unroll=min(UNROLL, (final - first) // 8))
     for block in lane_blocks(rows):
         values = [jnp.sum(sums[at, block, :].T, axis=0, keepdims=True) for at in range(6)]
         ends[:, block] = padded_rows(values, 8)
-    for store in stores:
-        store.wait()
 
 
 def pack(values):
@@ -252,7 +245,7 @@
 
 def halo_kernel(
     scale, index, table, before_x, after_x, before_y, after_y, x_head, x_tail, y_head, y_tail,
-    m1, m2, ends_y, near_ends, ends, shares, delta_x, delta_y,
+    m1, m2, ends_y, near_ends, ends, inner, shares, delta, kept, near_shares, near_delta, sems,
 ):
     cells_x = before_y.shape[1]
     cells_y = before_x.shape[1]
@@ -283,10 +276,10 @@
         bends[0],
         bends[1],
     )
-    delta_x[0:16, :] = head_x
-    delta_x[16:32, :] = tail_x
-    delta_y[0:16, :] = head_y
-    delta_y[16:32, :] = tail_y
+    for at, part in enumerate((head_x, tail_x, head_y, tail_y)):
+        near_delta[16 * at : 16 * at + 16, :] = part
+    store = pltpu.make_async_copy(near_delta, delta, sems.at[0])
+    store.start()
     values = ends[...] + lax.dot_general(
         near_ends[...],
         jnp.concatenate([head_y, tail_y], axis=0),
@@ -313,7 +306,11 @@
                     axis=1,
                 )
             )
-    write_shares(table, index, values + padded_rows(extra, 8), shares)
+    write_shares(table, index, values + padded_rows(extra, 8), near_shares)
+    leave = pltpu.make_async_copy(near_shares, shares, sems.at[1])
+    leave.start()
+    store.wait()
+    leave.wait()
 
 
 def turned_rows(rows, turned):
@@ -323,38 +320,48 @@
 
 
 def solve_kernel(
-    inner, delta_x, delta_y, table_y, table_x, solved, edges,
-    work, inverse_y, inverse_x, high, low, turned, sems,
+    inner, delta, table_y, table_x, solved, edges,
+    near_delta, inverse_y, inverse_x, above, below, high, low, turned, sems,
 ):
     cells_x, cells = solved.shape[1], solved.shape[2]
-    loads = [pltpu.make_async_copy(inner.at[comp], work.at[comp], sems.at[comp]) for comp in range(3)]
-    tables_y = [pltpu.make_async_copy(table_y.at[at], inverse_y.at[at], sems.at[3 + at]) for at in (0, 1)]
-    tables_x = [pltpu.make_async_copy(table_x.at[at], inverse_x.at[at], sems.at[5 + at]) for at in (0, 1)]
-    for copy in loads[:1] + tables_y + tables_x + loads[1:]:
+    tables_y = [pltpu.make_async_copy(table_y.at[at], inverse_y.at[at], sems.at[at]) for at in (0, 1)]
+    tables_x = [pltpu.make_async_copy(table_x.at[at], inverse_x.at[at], sems.at[2 + at]) for at in (0, 1)]
+    sides = pltpu.make_async_copy(delta, near_delta, sems.at[4])
+    for copy in [sides] + tables_y + tables_x:
         copy.start()
-    turned_rows(delta_y[...], turned)
+    sides.wait()
+    turned_rows(near_delta[32:64, :], turned)
     lane = lax.broadcasted_iota(jnp.int32, (128, 128), 1)
     half = cells_x // 2
     halves = (slice(0, half), slice(half, cells_x))
     for comp in range(3):
-        loads[comp].wait()
         for block in lane_blocks(cells_x):
             tile = turned[block, :]
             near = pltpu.roll(tile, 128 - 3 * comp, 1) if comp else tile
-            work[comp, block, 0:128] += jnp.where(lane < 3, near, 0.0)
             far = pltpu.roll(tile, 109 - 3 * comp, 1)
-            work[comp, block, cells - 128 : cells] += jnp.where(lane >= 125, far, 0.0)
-        work[comp, 0:3, :] += delta_x[3 * comp : 3 * comp + 3, :]
-        work[comp, cells_x - 3 : cells_x, :] += delta_x[16 + 3 * comp : 19 + 3 * comp, :]
+            full = jnp.concatenate(
+                [
+                    inner[comp, block, 0:128] + jnp.where(lane < 3, near, 0.0),
+                    inner[comp, block, 128 : cells - 128],
+                    inner[comp, block, cells - 128 : cells] + jnp.where(lane >= 125, far, 0.0),
+                ],
+                axis=1,
+            )
+            if block.start == 0:
+                full = full + padded_rows([near_delta[3 * comp : 3 * comp + 3, :]], 128)
+            if block.stop == cells_x:
+                full = full + jnp.concatenate(
+                    [jnp.zeros((125, cells), F32), near_delta[16 + 3 * comp : 19 + 3 * comp, :]], axis=0
+                )
+            above[block, :], below[block, :] = split(full)
         if comp == 0:
             for copy in tables_y:
                 copy.wait()
         for rows in halves:
-            above, below = split(work[comp, rows, :])
             high[rows, :], low[rows, :] = split(
-                jnp.dot(above, inverse_y[0], preferred_element_type=F32)
-                + jnp.dot(below, inverse_y[0], preferred_element_type=F32)
-                + jnp.dot(above, inverse_y[1], preferred_element_type=F32)
+                jnp.dot(above[rows, :], inverse_y[0], preferred_element_type=F32)
+                + jnp.dot(below[rows, :], inverse_y[0], preferred_element_type=F32)
+                + jnp.dot(above[rows, :], inverse_y[1], preferred_element_type=F32)
             )
         if comp == 0:
             for copy in tables_x:
@@ -406,20 +413,23 @@
     out[...] = above[...] + step * own[...] + (step * step) * below[...]
 
 
-def beside_kernel(solved, beside, sides_y, table, token, updated, inverse, turned, sems):
-    cells_x, cells_y = solved.shape[1], solved.shape[2]
+def columns_kernel(beside, table, sides_x, token, turned, inverse, sems):
     copies = [pltpu.make_async_copy(table.at[at], inverse.at[at], sems.at[at]) for at in (0, 1)]
     for copy in copies:
         copy.start()
     high, low = split(padded_rows([beside[...]], 16))
     for copy in copies:
         copy.wait()
-    turned_rows(
+    lines = (
         jnp.dot(high, inverse[0], preferred_element_type=F32)
         + jnp.dot(low, inverse[0], preferred_element_type=F32)
-        + jnp.dot(high, inverse[1], preferred_element_type=F32),
-        turned,
+        + jnp.dot(high, inverse[1], preferred_element_type=F32)
     )
+    turned_rows(jnp.concatenate([lines[0:6], sides_x[...]], axis=0), turned)
+
+
+def beside_kernel(solved, turned, sides_y, token, updated):
+    cells_x, cells_y = solved.shape[1], solved.shape[2]
     before = jnp.broadcast_to(sides_y[0:1, :], (8, cells_y))
     after = jnp.broadcast_to(sides_y[1:2, :], (8, cells_y))
 
@@ -436,49 +446,57 @@
 
 
 def final_kernel(
-    chain, chips, index, own, other, pair, pair_above, far_below, far_above, rows_x, solved,
-    out, beyond, turned,
+    chain, chips, index, own, other, pair, pair_above, far_below, far_above, turned, solved,
+    out, beyond, result, sems,
 ):
-    step = pl.program_id(0)
     rows = out.shape[1]
     blocks = lane_blocks(out.shape[2])
     gain, ratio, behind, ahead = chain
     link = ratio * ratio
 
-    @pl.when(step == 0)
-    def _():
-        turned_rows(rows_x[...], turned)
-        even = index[0] % 2 == 0
-        chip = (
-            far_below[0:3, :]
-            + link**3 * far_above[0:3, :]
-            + (link**6 * pair_above[0:3, :] + link**7 * pair[0:3, :])
-        ) * (1.0 / (1.0 - link**chips))
-        before = jnp.where(even, chip, other[0:3, :] + ratio * chip)
-        following = jnp.where(even, other[3:6, :], pair_above[3:6, :])
-        first = (gain * behind) * own[3:6, :] + before
-        last = gain * following + ahead * (own[0:3, :] + ratio * before)
-        for comp in range(3):
-            for side, values in enumerate((first, last)):
-                wide = jnp.broadcast_to(values[comp : comp + 1, :], (8, values.shape[1]))
-                for at, block in enumerate(blocks):
-                    beyond[3 * side + comp, at] = wide[:, block]
-
-    for at in range(0, rows, 8):
-        where = pl.ds(pl.multiple_of(step * rows + at, 8), 8)
+    even = index[0] % 2 == 0
+    chip = (
+        far_below[0:3, :]
+        + link**3 * far_above[0:3, :]
+        + (link**6 * pair_above[0:3, :] + link**7 * pair[0:3, :])
+    ) * (1.0 / (1.0 - link**chips))
+    before = jnp.where(even, chip, other[0:3, :] + ratio * chip)
+    following = jnp.where(even, other[3:6, :], pair_above[3:6, :])
+    first = (gain * behind) * own[3:6, :] + before
+    last = gain * following + ahead * (own[0:3, :] + ratio * before)
+    for comp in range(3):
+        for side, values in enumerate((first, last)):
+            wide = jnp.broadcast_to(values[comp : comp + 1, :], (8, values.shape[1]))
+            for at, block in enumerate(blocks):
+                beyond[3 * side + comp, at] = wide[:, block]
+
+    def step(index, carry):
+        where = pl.ds(pl.multiple_of(index * 8, 8), 8)
         here = turned[where, :]
-        head = jnp.broadcast_to(here[:, 2:3], (8, 128))
-        tail = jnp.broadcast_to(here[:, 3:4], (8, 128))
+        head = jnp.broadcast_to(here[:, 6:7], (8, 128))
+        tail = jnp.broadcast_to(here[:, 7:8], (8, 128))
         for comp in range(3):
             for place, block in enumerate(blocks):
-                out[comp, at : at + 8, block] = solved[comp, where, block] + (
+                result[comp, where, block] = solved[comp, where, block] + (
                     head * beyond[comp, place] + tail * beyond[comp + 3, place]
                 )
+        return carry
+
+    stores = []
+    bounds = [rows * at // 64 for at in OUT_CUTS]
+    for which, (low, high) in enumerate(zip(bounds[:-1], bounds[1:])):
+        lax.fori_loop(low // 8, high // 8, step, 0, unroll=4)
+        store = pltpu.make_async_copy(result.at[:, low:high, :], out.at[:, low:high, :], sems.at[which])
+        store.start()
+        stores.append(store)
+    for store in stores:
+        store.wait()
 
 
 VMEM = pl.BlockSpec(memory_space=pltpu.VMEM)
 SMEM = pl.BlockSpec(memory_space=pltpu.SMEM)
 HBM = pl.BlockSpec(memory_space=pltpu.HBM)
+ANY = pl.BlockSpec(memory_space=pl.ANY)
 
 
 def in_hbm(values):
@@ -520,9 +538,7 @@
             near[3 * end + comp, 3 * comp : 3 * comp + 3] = row[:3]
             near[3 * end + comp, 16 + 3 * comp : 19 + 3 * comp] = row[-3:]
     near_ends = jnp.asarray(near, F32)
-    rows_x = np.zeros((8, nx))
-    rows_x[:4] = np.stack([inverse_x[0], inverse_x[-1], head_x, tail_x])
-    rows_x = jnp.asarray(rows_x, F32)
+    sides_x = jnp.asarray(np.stack([head_x, tail_x]), F32)
     sides_y = jnp.asarray(np.stack([head_y, tail_y]), F32)
     parts_x = in_hbm(jnp.asarray(split_table(inverse_x)))
     turned_x = in_hbm(jnp.asarray(split_table(inverse_x.T)))
@@ -558,44 +574,45 @@
         inner, ends = call(
             functools.partial(inner_kernel, scale),
             [HBM] + [VMEM] * 3,
-            [pltpu.HBM((3, nx, ny), F32), struct(8, nx)],
+            [struct(3, nx, ny), struct(8, nx)],
             [
                 pltpu.VMEM((3, ny // 128, nx + 16, 128), F32),
-                pltpu.VMEM((3, nx, ny), F32),
                 pltpu.VMEM((8, ny // 128, 8, 128), F32),
                 pltpu.VMEM((6, nx, 128), F32),
                 pltpu.SemaphoreType.DMA((len(CUTS) - 1, ny // 128)),
-                pltpu.SemaphoreType.DMA((len(CUTS) - 1,)),
             ],
             40 * cells,
             8 * cells,
-            out_specs=[HBM, VMEM],
         )(velocity, m1, m2, ends_y)
     with jax.named_scope("halo_part"):
-        shares_y, delta_x, delta_y = call(
+        shares_y, delta, inner = call(
             functools.partial(halo_kernel, scale),
-            [SMEM, SMEM] + [VMEM] * 13,
-            [struct(blocks_y, 6 * (nx // 128), 128), struct(32, ny), struct(32, nx)],
-            [],
+            [SMEM, SMEM] + [VMEM] * 13 + [ANY],
+            [pltpu.HBM((blocks_y, 6 * (nx // 128), 128), F32), pltpu.HBM((64, ny), F32), struct(3, nx, ny)],
+            [pltpu.VMEM((blocks_y, 6 * (nx // 128), 128), F32), pltpu.VMEM((64, ny), F32)]
+            + [pltpu.SemaphoreType.DMA((2,))],
             1000 * nx,
             500 * nx,
+            input_output_aliases={15: 2},
+            out_specs=[HBM, HBM, ANY],
         )(
             index_y, table_y, before_x, after_x, before_y, after_y, x_head, x_tail, y_head, y_tail,
-            m1, m2, ends_y, near_ends, ends,
+            m1, m2, ends_y, near_ends, ends, inner,
         )
     with jax.named_scope("across_y"):
         got_y = lax.all_to_all(shares_y, "gy", 0, 0, tiled=True)
     with jax.named_scope("solve"):
         solved, edges = call(
             solve_kernel,
-            [HBM] + [VMEM] * 2 + [HBM] * 2,
+            [VMEM] + [HBM] * 3,
             [struct(3, nx, ny), struct(8, ny)],
-            [pltpu.VMEM((3, nx, ny), F32), pltpu.VMEM((2, ny, ny), BF16), pltpu.VMEM((2, nx, nx), BF16)]
-            + [pltpu.VMEM((nx, ny), BF16)] * 2
-            + [pltpu.VMEM((nx, 128), F32), pltpu.SemaphoreType.DMA((7,))],
+            [pltpu.VMEM((64, ny), F32), pltpu.VMEM((2, ny, ny), BF16), pltpu.VMEM((2, nx, nx), BF16)]
+            + [pltpu.VMEM((nx, ny), BF16)] * 4
+            + [pltpu.VMEM((nx, 128), F32), pltpu.SemaphoreType.DMA((5,))],
             6 * cells * (nx + ny),
             8 * cells,
-        )(in_hbm(inner), delta_x, delta_y, parts_y, parts_x)
+            input_output_aliases={0: 0},
+        )(inner, in_hbm(delta), parts_y, parts_x)
     chain = chain_numbers(head_x, tail_x)
     link = struct(8, ny)
     with jax.named_scope("ends_x"):
@@ -618,6 +635,14 @@
         )(index_x, own, other)
         pair_below = along(pair, 2)
         pair_above = along(pair, -2)
+        (turned,) = call(
+            columns_kernel,
+            [VMEM, HBM, VMEM, VMEM],
+            [struct(nx, 128)],
+            [pltpu.VMEM((2, nx, nx), BF16), pltpu.SemaphoreType.DMA((2,))],
+            48 * nx * nx,
+            4 * nx * nx,
+        )(beside, turned_x, sides_x, pair)
         (window,) = call(functools.partial(window_kernel, chain), [VMEM] * 3, [link], [], 10 * nx, 100 * nx)(
             pair, pair_below, pair_above
         )
@@ -625,24 +650,24 @@
         far_above = along(window, -6)
         (solved,) = call(
             beside_kernel,
-            [VMEM] * 3 + [HBM, VMEM],
+            [VMEM] * 4,
             [struct(3, nx, ny)],
-            [pltpu.VMEM((2, nx, nx), BF16), pltpu.VMEM((nx, 128), F32), pltpu.SemaphoreType.DMA((2,))],
+            [],
             6 * cells,
             8 * cells,
             input_output_aliases={0: 0},
-        )(solved, beside, sides_y, turned_x, window)
+        )(solved, turned, sides_y, window)
     with jax.named_scope("final"):
         return call(
             functools.partial(final_kernel, chain, blocks_x // 2),
             [SMEM] + [VMEM] * 8,
             struct(3, nx, ny),
-            [pltpu.VMEM((6, ny // 128, 8, 128), F32), pltpu.VMEM((nx, 128), F32)],
+            [pltpu.VMEM((6, ny // 128, 8, 128), F32), pltpu.VMEM((3, nx, ny), F32)]
+            + [pltpu.SemaphoreType.DMA((len(OUT_CUTS) - 1,))],
             4 * cells,
             8 * cells,
-            grid=(nx // 128,),
-            out_specs=pl.BlockSpec((3, 128, ny), lambda i: (0, i, 0)),
-        )(index_x, own, other, pair, pair_above, far_below, far_above, rows_x, solved)
+            out_specs=ANY,
+        )(index_x, own, other, pair, pair_above, far_below, far_above, turned, solved)
 
 
 def solution(mesh):

time: 52.9 us -> 52.1 us (0.985)
  the two profiles are of different devices: /device:TPU:2 before, /device:TPU:1 now
where the time goes in v4:
time: 52.1 us; the launch traced here: 51.1 us
  starting transfers between devices  24.7 us (47%)
  Pallas kernels  24.2 us (46%)
  waiting for transfers between devices  2 us (4%)
    ppermute x4, starting transfers between devices, along(): lax.ppermute(values, 'gx', [(i, (i + shift) % blocks_x) for i in range(bl...  7.57 us
    pallas_call x1, Pallas kernels, local(): call(functools.partial(inner_kernel, scale), [HBM] + [VMEM] * 3, [struct(...  7.36 us
    pallas_call x1, Pallas kernels, local(): call(solve_kernel, [VMEM] + [HBM] * 3, [struct(3, nx, ny), struct(8, ny)]...  6.86 us
    ppermute x1, starting transfers between devices, local(): other = lax.ppermute(own, 'gx', [(i, i ^ 1) for i in range(blocks_x)])  5.57 us
    ppermute x1, starting transfers between devices, local(): after_y = lax.ppermute(y_head, 'gy', back_y)  3.73 us
    all_to_all x1, starting transfers between devices, local(): got_y = lax.all_to_all(shares_y, 'gy', 0, 0, tiled=True)  3.53 us
    ppermute x1, starting transfers between devices, local(): before_x = lax.ppermute(x_tail, 'gx', round_x)  3.04 us
    pallas_call x1, Pallas kernels, local(): call(functools.partial(final_kernel, chain, blocks_x // 2), [SMEM] + [VME...  2.57 us
  transfers between devices with their start and end apart: 10, of which 2 were waited for; matrix products, arithmetic and copies ran while one was open for 0% of the time, Pallas kernels for 35%

profile of v4, /device:TPU:1, one launch (start us, length us, event | category | flops | bytes accessed | tf_op | source)
XLA Modules:
  0.0 51.1 jit_solution(16334630461397704908)
XLA Ops:
  0.0 0.0 copy-start
  0.0 0.0 copy-start.2
  0.0 0.0 copy-start.5
  0.0 0.0 copy-start.4
  0.0 0.0 copy-start.3
  0.0 2.0 %edges.1 = (f32[16,512]{1,0:T(8,128)S(1)}, f32[16,512]{1,0:T(8,128)S(1)}, f32[16,512]{1,0:T(8,128)S(1)}, f32[16,512]{1,0:T(8,128)S(1)}) custom-call(f32[3,512,512]{2,1,0:T(8,128)} %field.3), custom_call_target="tpu_custom_call" | custom-call | flops 655360 | bytes 1572864 | tf_op jit(solution)/shard_map/edges/pallas_call | solution.py:558
  2.0 3.0 %collective-permute-start = (f32[16,512]{1,0:T(8,128)S(1)}, f32[16,512]{1,0:T(8,128)S(1)}, u32[]{:S(2)}, u32[]{:S(2)}) collective-permute-start(f32[16,512]{1,0:T(8,128)S(1)} %get-tuple-element.18.x_tail), channel_id=1, source_target_pairs={{0,16},{16,32},{32,48},{48,64},{64,80},{80,96},{96,112},{112,128},... | collective-permute-start | bytes 98312 | tf_op jit(solution)/shard_map/halos/ppermute | solution.py:569
  5.0 0.2 collective-permute-start.1
  5.3 1.1 %collective-permute-start.2 = (f32[16,512]{1,0:T(8,128)S(1)}, f32[16,512]{1,0:T(8,128)S(1)}, u32[]{:S(2)}, u32[]{:S(2)}) collective-permute-start(f32[16,512]{1,0:T(8,128)S(1)} %get-tuple-element.20.y_tail), channel_id=1, source_target_pairs={{0,1},{1,2},{2,3},{3,4},{4,5},{5,6},{6,7},{7,8},{8,9},{9,10},{10,1... | collective-permute-start | bytes 98312 | tf_op jit(solution)/shard_map/halos/ppermute | solution.py:571
  6.3 3.7 %collective-permute-start.3 = (f32[16,512]{1,0:T(8,128)S(1)}, f32[16,512]{1,0:T(8,128)S(1)}, u32[]{:S(2)}, u32[]{:S(2)}) collective-permute-start(f32[16,512]{1,0:T(8,128)S(1)} %get-tuple-element.21.y_head), channel_id=1, source_target_pairs={{1,0},{2,1},{3,2},{4,3},{5,4},{6,5},{7,6},{8,7},{9,8},{10,9},{11,1... | collective-permute-start | bytes 98312 | tf_op jit(solution)/shard_map/halos/ppermute | solution.py:572
  10.1 0.0 copy-done
  10.1 0.0 copy-done.4
  10.1 0.0 copy-done.3
  10.1 7.4 %inner.1 = (f32[3,512,512]{2,1,0:T(8,128)S(1)}, f32[8,512]{1,0:T(8,128)S(1)}) custom-call(f32[3,512,512]{2,1,0:T(8,128)} %field.3, f32[1,512]{1,0:T(1,128)S(1)} %bitcast.4, f32[1,512]{1,0:T(1,128)S(1)} %bitcast.6, f32[2,512]{1,0:T(2,128)S(1)} %copy-done), custom_call_target="tpu_custom_call" | custom-call | flops 31457280 | bytes 6291456 | tf_op jit(solution)/shard_map/inner/pallas_call | solution.py:574
  17.4 0.0 collective-permute-done.before_x
  17.5 0.0 collective-permute-done.1.after_x
  17.5 0.0 collective-permute-done.2.before_y
  17.5 0.0 collective-permute-done.3.after_y
  17.5 0.0 copy-done.2
  17.5 0.0 copy-done.5
  17.5 1.8 %halo_part.1 = (f32[16,24,128]{2,1,0:T(8,128)}, f32[64,512]{1,0:T(8,128)}, f32[3,512,512]{2,1,0:T(8,128)S(1)}) custom-call(s32[1]{0:T(128)} %bitcast.1.index, f32[16,64]{1,0:T(8,128)S(1)} %copy-done.2, f32[16,512]{1,0:T(8,128)S(1)} %collective-permute-done.before_x, f32[16,512]{1,0:T(8,128)S(1)} %collective-permute-done.1.after_x, ...), custom_call_target="tpu_custom_call", output_to_operand_aliasing={{2}: (15, {})} | custom-call | flops 512000 | bytes 256000 | tf_op jit(solution)/shard_map/halo_part/pallas_call | solution.py:588
  19.3 3.5 %all-to-all-start = ((f32[16,24,128]{2,1,0:T(8,128)}), f32[16,24,128]{2,1,0:T(8,128)S(1)}, u32[]{:S(2)}, u32[]{:S(2)}) async-start(f32[16,24,128]{2,1,0:T(8,128)} %get-tuple-element.24), calls=%async_computation | async-start | bytes 393216 | tf_op jit(solution)/shard_map/across_y/all_to_all | solution.py:603
  22.8 0.0 copy-start.1
  22.8 6.9 %solve.1 = (f32[3,512,512]{2,1,0:T(8,128)S(1)}, f32[8,512]{1,0:T(8,128)S(1)}) custom-call(f32[3,512,512]{2,1,0:T(8,128)S(1)} %get-tuple-element.25.inner, f32[64,512]{1,0:T(8,128)} %get-tuple-element.26.delta, bf16[2,512,512]{2,1,0:T(8,128)(2,1)} %constant.24.clone.table_y.table, ...), custom_call_target="tpu_custom_call", output_to_operand_aliasing={{0}: (0, {})} | custom-call | flops 4831838208 | bytes 6291456 | tf_op jit(solution)/shard_map/solve/pallas_call | solution.py:605
  29.7 0.0 all-to-all-done.got
  29.7 0.0 copy-done.1
  29.7 0.1 ends_x.2
  29.8 5.6 %collective-permute-start.4 = (f32[8,512]{1,0:T(8,128)S(1)}, f32[8,512]{1,0:T(8,128)S(1)}, u32[]{:S(2)}, u32[]{:S(2)}) collective-permute-start(f32[8,512]{1,0:T(8,128)S(1)} %get-tuple-element.28.own), channel_id=1, source_target_pairs={{0,16},{16,0},{32,48},{48,32},{64,80},{80,64},{96,112},{112,96},{1... | collective-permute-start | bytes 49160 | tf_op jit(solution)/shard_map/across_x/ppermute | solution.py:632
  35.4 0.8 %collective-permute-done.4.other = f32[8,512]{1,0:T(8,128)S(1)} collective-permute-done((f32[8,512]{1,0:T(8,128)S(1)}, f32[8,512]{1,0:T(8,128)S(1)}, u32[]{:S(2)}, u32[]{:S(2)}) %collective-permute-start.4) | collective-permute-done | bytes 16416 | tf_op jit(solution)/shard_map/across_x/ppermute | solution.py:632
  36.3 0.1 collective-permute-start.6
  36.4 2.7 %collective-permute-start.5 = (f32[8,512]{1,0:T(8,128)S(1)}, f32[8,512]{1,0:T(8,128)S(1)}, u32[]{:S(2)}, u32[]{:S(2)}) collective-permute-start(f32[8,512]{1,0:T(8,128)S(1)} %across_x.4.own.token.pair), channel_id=1, source_target_pairs={{0,224},{16,240},{32,0},{48,16},{64,32},{80,48},{96,64},{112,80},{... | collective-permute-start | bytes 49160 | tf_op jit(solution)/shard_map/across_x/ppermute | solution.py:629
  39.0 1.1 %collective-permute-done.6.below = f32[8,512]{1,0:T(8,128)S(1)} collective-permute-done((f32[8,512]{1,0:T(8,128)S(1)}, f32[8,512]{1,0:T(8,128)S(1)}, u32[]{:S(2)}, u32[]{:S(2)}) %collective-permute-start.6) | collective-permute-done | bytes 16416 | tf_op jit(solution)/shard_map/across_x/ppermute | solution.py:629
  40.1 0.0 collective-permute-done.5.above.pair_above
  40.2 2.5 %collective-permute-start.8 = (f32[8,512]{1,0:T(8,128)S(1)}, f32[8,512]{1,0:T(8,128)S(1)}, u32[]{:S(2)}, u32[]{:S(2)}) collective-permute-start(f32[8,512]{1,0:T(8,128)S(1)} %across_x.5.token), channel_id=1, source_target_pairs={{0,160},{16,176},{32,192},{48,208},{64,224},{80,240},{96,0},{112,1... | collective-permute-start | bytes 49160 | tf_op jit(solution)/shard_map/across_x/ppermute | solution.py:629
  42.6 2.3 %collective-permute-start.7 = (f32[8,512]{1,0:T(8,128)S(1)}, f32[8,512]{1,0:T(8,128)S(1)}, u32[]{:S(2)}, u32[]{:S(2)}) collective-permute-start(f32[8,512]{1,0:T(8,128)S(1)} %across_x.5.token), channel_id=1, source_target_pairs={{0,64},{16,80},{32,96},{48,112},{64,128},{80,144},{96,160},{112,17... | collective-permute-start | bytes 49160 | tf_op jit(solution)/shard_map/across_x/ppermute | solution.py:629
  45.0 1.7 %across_x.6.turned = f32[512,128]{1,0:T(8,128)S(1)} custom-call(f32[8,512]{1,0:T(8,128)S(1)} %get-tuple-element.29.beside, bf16[2,512,512]{2,1,0:T(8,128)(2,1)} %constant.24.clone.table_y.table, f32[2,512]{1,0:T(2,128)S(1)} %copy-done.1, f32[8,512]{1,0:T(8,128)S(1)} %across_x.4.own.token.pair), custom_call_target="tpu_custom_call" | custom-call | flops 12582912 | bytes 1048576 | tf_op jit(solution)/shard_map/across_x/pallas_call | solution.py:638
  46.7 1.9 %across_x.7.solved = f32[3,512,512]{2,1,0:T(8,128)S(1)} custom-call(f32[3,512,512]{2,1,0:T(8,128)S(1)} %get-tuple-element.30.solved, f32[512,128]{1,0:T(8,128)S(1)} %across_x.6.turned, f32[2,512]{1,0:T(2,128)S(1)} %copy-done.1, f32[8,512]{1,0:T(8,128)S(1)} %across_x.5.token), custom_call_target="tpu_custom_call", output_to_operand_aliasing={{}: (0, {})} | custom-call | flops 4718592 | bytes 6291456 | tf_op jit(solution)/shard_map/across_x/pallas_call | solution.py:651
  48.6 0.0 collective-permute-done.8.far_above
  48.6 0.0 collective-permute-done.7.far_below
  48.6 2.6 %final.1 = f32[3,512,512]{2,1,0:T(8,128)} custom-call(s32[1]{0:T(128)} %bitcast.index, f32[8,512]{1,0:T(8,128)S(1)} %get-tuple-element.28.own, f32[8,512]{1,0:T(8,128)S(1)} %collective-permute-done.4.other, f32[8,512]{1,0:T(8,128)S(1)} %across_x.4.own.token.pair, f32[8,512]{1,0:T(8,128)S(1)} %collective-permute-done.5.above.pair_above, ...), custom_call_target="tpu_custom_call" | custom-call | flops 3145728 | bytes 6291456 | tf_op jit(solution)/shard_map/final/pallas_call | solution.py:661
  (2 shorter events, 0.0 us)
Async XLA Ops:
  0.0 10.1 %copy-start = (f32[2,512]{1,0:T(2,128)S(1)}, f32[2,512]{1,0:T(2,128)}, u32[]{:S(2)}) copy-start(f32[2,512]{1,0:T(2,128)} %constant.20.clone.ends_y.ends_x) | copy-start | bytes 12292
  0.0 17.5 %copy-start.2 = (f32[16,64]{1,0:T(8,128)S(1)}, f32[16,64]{1,0:T(8,128)}, u32[]{:S(2)}) copy-start(f32[16,64]{1,0:T(8,128)} %constant.19.clone.table) | copy-start | bytes 12292
  0.0 17.5 %copy-start.5 = (f32[8,32]{1,0:T(8,128)S(1)}, f32[8,32]{1,0:T(8,128)}, u32[]{:S(2)}) copy-start(f32[8,32]{1,0:T(8,128)} %constant.21.clone.near_ends) | copy-start | bytes 3076
  0.0 10.1 %copy-start.4 = (f32[512]{0:T(512)S(1)}, f32[512]{0:T(512)}, u32[]{:S(2)}) copy-start(f32[512]{0:T(512)} %param.14) | copy-start | bytes 6148
  0.0 10.1 %copy-start.3 = (f32[512]{0:T(512)S(1)}, f32[512]{0:T(512)}, u32[]{:S(2)}) copy-start(f32[512]{0:T(512)} %param.13) | copy-start | bytes 6148
  2.0 15.4 %collective-permute-start = (f32[16,512]{1,0:T(8,128)S(1)}, f32[16,512]{1,0:T(8,128)S(1)}, u32[]{:S(2)}, u32[]{:S(2)}) collective-permute-start(f32[16,512]{1,0:T(8,128)S(1)} %get-tuple-element.18.x_tail), channel_id=1, source_target_pairs={{0,16},{16,32},{32,48},{48,64},{64,80},{80,96},{96,112},{112,128},... | collective-permute-start | bytes 98312 | tf_op jit(solution)/shard_map/halos/ppermute | solution.py:569
  5.0 12.4 %collective-permute-start.1 = (f32[16,512]{1,0:T(8,128)S(1)}, f32[16,512]{1,0:T(8,128)S(1)}, u32[]{:S(2)}, u32[]{:S(2)}) collective-permute-start(f32[16,512]{1,0:T(8,128)S(1)} %get-tuple-element.19.x_head), channel_id=1, source_target_pairs={{16,0},{32,16},{48,32},{64,48},{80,64},{96,80},{112,96},{128,112},... | collective-permute-start | bytes 98312 | tf_op jit(solution)/shard_map/halos/ppermute | solution.py:570
  5.3 12.2 %collective-permute-start.2 = (f32[16,512]{1,0:T(8,128)S(1)}, f32[16,512]{1,0:T(8,128)S(1)}, u32[]{:S(2)}, u32[]{:S(2)}) collective-permute-start(f32[16,512]{1,0:T(8,128)S(1)} %get-tuple-element.20.y_tail), channel_id=1, source_target_pairs={{0,1},{1,2},{2,3},{3,4},{4,5},{5,6},{6,7},{7,8},{8,9},{9,10},{10,1... | collective-permute-start | bytes 98312 | tf_op jit(solution)/shard_map/halos/ppermute | solution.py:571
  6.3 11.1 %collective-permute-start.3 = (f32[16,512]{1,0:T(8,128)S(1)}, f32[16,512]{1,0:T(8,128)S(1)}, u32[]{:S(2)}, u32[]{:S(2)}) collective-permute-start(f32[16,512]{1,0:T(8,128)S(1)} %get-tuple-element.21.y_head), channel_id=1, source_target_pairs={{1,0},{2,1},{3,2},{4,3},{5,4},{6,5},{7,6},{8,7},{9,8},{10,9},{11,1... | collective-permute-start | bytes 98312 | tf_op jit(solution)/shard_map/halos/ppermute | solution.py:572
  19.3 10.4 %all-to-all-start = ((f32[16,24,128]{2,1,0:T(8,128)}), f32[16,24,128]{2,1,0:T(8,128)S(1)}, u32[]{:S(2)}, u32[]{:S(2)}) async-start(f32[16,24,128]{2,1,0:T(8,128)} %get-tuple-element.24), calls=%async_computation | async-start | bytes 393216 | tf_op jit(solution)/shard_map/across_y/all_to_all | solution.py:603
  22.8 6.9 %copy-start.1 = (f32[2,512]{1,0:T(2,128)S(1)}, f32[2,512]{1,0:T(2,128)}, u32[]{:S(2)}) copy-start(f32[2,512]{1,0:T(2,128)} %constant.22.clone.sides_y.sides_x) | copy-start | bytes 12292
  29.8 6.4 %collective-permute-start.4 = (f32[8,512]{1,0:T(8,128)S(1)}, f32[8,512]{1,0:T(8,128)S(1)}, u32[]{:S(2)}, u32[]{:S(2)}) collective-permute-start(f32[8,512]{1,0:T(8,128)S(1)} %get-tuple-element.28.own), channel_id=1, source_target_pairs={{0,16},{16,0},{32,48},{48,32},{64,80},{80,64},{96,112},{112,96},{1... | collective-permute-start | bytes 49160 | tf_op jit(solution)/shard_map/across_x/ppermute | solution.py:632
  36.3 3.9 %collective-permute-start.6 = (f32[8,512]{1,0:T(8,128)S(1)}, f32[8,512]{1,0:T(8,128)S(1)}, u32[]{:S(2)}, u32[]{:S(2)}) collective-permute-start(f32[8,512]{1,0:T(8,128)S(1)} %across_x.4.own.token.pair), channel_id=1, source_target_pairs={{0,32},{16,48},{32,64},{48,80},{64,96},{80,112},{96,128},{112,144}... | collective-permute-start | bytes 49160 | tf_op jit(solution)/shard_map/across_x/ppermute | solution.py:629
  36.4 3.8 %collective-permute-start.5 = (f32[8,512]{1,0:T(8,128)S(1)}, f32[8,512]{1,0:T(8,128)S(1)}, u32[]{:S(2)}, u32[]{:S(2)}) collective-permute-start(f32[8,512]{1,0:T(8,128)S(1)} %across_x.4.own.token.pair), channel_id=1, source_target_pairs={{0,224},{16,240},{32,0},{48,16},{64,32},{80,48},{96,64},{112,80},{... | collective-permute-start | bytes 49160 | tf_op jit(solution)/shard_map/across_x/ppermute | solution.py:629
  40.2 8.4 %collective-permute-start.8 = (f32[8,512]{1,0:T(8,128)S(1)}, f32[8,512]{1,0:T(8,128)S(1)}, u32[]{:S(2)}, u32[]{:S(2)}) collective-permute-start(f32[8,512]{1,0:T(8,128)S(1)} %across_x.5.token), channel_id=1, source_target_pairs={{0,160},{16,176},{32,192},{48,208},{64,224},{80,240},{96,0},{112,1... | collective-permute-start | bytes 49160 | tf_op jit(solution)/shard_map/across_x/ppermute | solution.py:629
  42.6 5.9 %collective-permute-start.7 = (f32[8,512]{1,0:T(8,128)S(1)}, f32[8,512]{1,0:T(8,128)S(1)}, u32[]{:S(2)}, u32[]{:S(2)}) collective-permute-start(f32[8,512]{1,0:T(8,128)S(1)} %across_x.5.token), channel_id=1, source_target_pairs={{0,64},{16,80},{32,96},{48,112},{64,128},{80,144},{96,160},{112,17... | collective-permute-start | bytes 49160 | tf_op jit(solution)/shard_map/across_x/ppermute | solution.py:629

commit v5 on v4

--- a/solution.py
+++ b/solution.py
@@ -16,6 +16,7 @@
 CENTRE = -490.0 / 180.0
 CUTS = (0, 4, 16, 64)
 UNROLL = 16
+LATER = 2
 OUT_CUTS = (0, 4, 16, 32, 48, 64)
 F32 = jnp.float32
 BF16 = jnp.bfloat16
@@ -358,23 +359,39 @@
             for copy in tables_y:
                 copy.wait()
         for rows in halves:
-            high[rows, :], low[rows, :] = split(
+            found = (
                 jnp.dot(above[rows, :], inverse_y[0], preferred_element_type=F32)
                 + jnp.dot(below[rows, :], inverse_y[0], preferred_element_type=F32)
                 + jnp.dot(above[rows, :], inverse_y[1], preferred_element_type=F32)
             )
+            high[rows, :], low[rows, :] = split(found)
+            if comp == LATER:
+                solved[comp, rows, :] = found
         if comp == 0:
             for copy in tables_x:
                 copy.wait()
-        for rows in halves:
-            solved[comp, rows, :] = (
-                jnp.dot(inverse_x[0, rows, :], high[...], preferred_element_type=F32)
-                + jnp.dot(inverse_x[0, rows, :], low[...], preferred_element_type=F32)
-                + jnp.dot(inverse_x[1, rows, :], high[...], preferred_element_type=F32)
+        if comp == LATER:
+            main, rest = [
+                jnp.concatenate([inverse_x[at, 0:16, :], inverse_x[at, cells_x - 16 : cells_x, :]], axis=0)
+                for at in (0, 1)
+            ]
+            found = (
+                jnp.dot(main, high[...], preferred_element_type=F32)
+                + jnp.dot(main, low[...], preferred_element_type=F32)
+                + jnp.dot(rest, high[...], preferred_element_type=F32)
             )
-    edges[...] = padded_rows(
-        [solved[comp, 0:1, :] for comp in range(3)] + [solved[comp, cells_x - 1 : cells_x, :] for comp in range(3)], 8
-    )
+            first, last = found[0:1], found[31:32]
+        else:
+            for rows in halves:
+                solved[comp, rows, :] = (
+                    jnp.dot(inverse_x[0, rows, :], high[...], preferred_element_type=F32)
+                    + jnp.dot(inverse_x[0, rows, :], low[...], preferred_element_type=F32)
+                    + jnp.dot(inverse_x[1, rows, :], high[...], preferred_element_type=F32)
+                )
+            first, last = solved[comp, 0:1, :], solved[comp, cells_x - 1 : cells_x, :]
+        edges[comp : comp + 1, :] = first
+        edges[comp + 3 : comp + 4, :] = last
+    edges[6:8, :] = jnp.zeros((2, cells), F32)
 
 
 def chain_numbers(head, tail):
@@ -408,7 +425,7 @@
     out[...] = padded_rows([second[0:3] + chain[1] * first[0:3], first[3:6]], 8)
 
 
-def window_kernel(chain, own, below, above, out):
+def window_kernel(chain, own, below, above, token, out):
     step = chain[1] * chain[1]
     out[...] = above[...] + step * own[...] + (step * step) * below[...]
 
@@ -428,8 +445,12 @@
     turned_rows(jnp.concatenate([lines[0:6], sides_x[...]], axis=0), turned)
 
 
-def beside_kernel(solved, turned, sides_y, token, updated):
+def beside_kernel(solved, turned, sides_y, table, token, updated, inverse, high, low, sems):
     cells_x, cells_y = solved.shape[1], solved.shape[2]
+    copies = [pltpu.make_async_copy(table.at[at], inverse.at[at], sems.at[at]) for at in (0, 1)]
+    for copy in copies:
+        copy.start()
+    high[...], low[...] = split(solved[LATER])
     before = jnp.broadcast_to(sides_y[0:1, :], (8, cells_y))
     after = jnp.broadcast_to(sides_y[1:2, :], (8, cells_y))
 
@@ -437,11 +458,21 @@
         rows = pl.ds(pl.multiple_of(index * 8, 8), 8)
         here = turned[rows, :]
         for comp in range(3):
-            updated[comp, rows, :] = solved[comp, rows, :] + (
+            source = updated if comp == LATER else solved
+            updated[comp, rows, :] = source[comp, rows, :] + (
                 here[:, comp : comp + 1] * before + here[:, comp + 3 : comp + 4] * after
             )
         return carry
 
+    for copy in copies:
+        copy.wait()
+    half = cells_x // 2
+    for rows in (slice(0, half), slice(half, cells_x)):
+        updated[LATER, rows, :] = (
+            jnp.dot(inverse[0, rows, :], high[...], preferred_element_type=F32)
+            + jnp.dot(inverse[0, rows, :], low[...], preferred_element_type=F32)
+            + jnp.dot(inverse[1, rows, :], high[...], preferred_element_type=F32)
+        )
     lax.fori_loop(0, cells_x // 8, step, 0, unroll=4)
 
 
@@ -643,20 +674,22 @@
             48 * nx * nx,
             4 * nx * nx,
         )(beside, turned_x, sides_x, pair)
-        (window,) = call(functools.partial(window_kernel, chain), [VMEM] * 3, [link], [], 10 * nx, 100 * nx)(
-            pair, pair_below, pair_above
+        (window,) = call(functools.partial(window_kernel, chain), [VMEM] * 4, [link], [], 10 * nx, 100 * nx)(
+            pair, pair_below, pair_above, turned
         )
         far_below = along(window, 4)
         far_above = along(window, -6)
         (solved,) = call(
             beside_kernel,
-            [VMEM] * 4,
+            [VMEM] * 3 + [HBM, VMEM],
             [struct(3, nx, ny)],
-            [],
-            6 * cells,
+            [pltpu.VMEM((2, nx, nx), BF16)]
+            + [pltpu.VMEM((nx, ny), BF16)] * 2
+            + [pltpu.SemaphoreType.DMA((2,))],
+            2 * cells * nx,
             8 * cells,
             input_output_aliases={0: 0},
-        )(solved, turned, sides_y, window)
+        )(solved, turned, sides_y, parts_x, window)
     with jax.named_scope("final"):
         return call(
             functools.partial(final_kernel, chain, blocks_x // 2),

time: 52.1 us -> 51.9 us (level); the launches traced: 51.1 us -> 51.6 us
  Pallas kernels: 24.2 us -> 25.8 us
  waiting for transfers between devices: 2 us -> 1.4 us
    pallas_call x2, Pallas kernels: 1.9 us -> 4.02 us  [the longest x1 4.01 us: local(): call(beside_kernel, [VMEM] * 3 + [HBM, VMEM], [struct(3, nx, ny)], [pltpu...]
    ppermute x4, waiting for transfers between devices: 1.14 us -> 0.01 us  [along(): lax.ppermute(values, 'gx', [(i, (i + shift) % blocks_x) for i in range(bl...]
    ppermute x4, starting transfers between devices: 7.57 us -> 7 us  [along(): lax.ppermute(values, 'gx', [(i, (i + shift) % blocks_x) for i in range(bl...]
    pallas_call x1, Pallas kernels: 6.86 us -> 6.34 us  [local(): call(solve_kernel, [VMEM] + [HBM] * 3, [struct(3, nx, ny), struct(8, ny)]...]
    all_to_all x1, waiting for transfers between devices: 0.01 us -> 0.54 us  [local(): got_y = lax.all_to_all(shares_y, 'gy', 0, 0, tiled=True)]
  transfers between devices with their start and end apart: 10 -> 10, of which waited for: 2 -> 2; matrix products, arithmetic and copies ran while one was open for 0% -> 0% of each run, Pallas kernels for 35% -> 38%
where the time goes in v5:
time: 51.9 us; the launch traced here: 51.6 us
  Pallas kernels  25.8 us (50%)
  starting transfers between devices  24.2 us (47%)
  waiting for transfers between devices  1.4 us (3%)
    pallas_call x1, Pallas kernels, local(): call(functools.partial(inner_kernel, scale), [HBM] + [VMEM] * 3, [struct(...  7.36 us
    ppermute x4, starting transfers between devices, along(): lax.ppermute(values, 'gx', [(i, (i + shift) % blocks_x) for i in range(bl...  7 us
    pallas_call x1, Pallas kernels, local(): call(solve_kernel, [VMEM] + [HBM] * 3, [struct(3, nx, ny), struct(8, ny)]...  6.34 us
    ppermute x1, starting transfers between devices, local(): other = lax.ppermute(own, 'gx', [(i, i ^ 1) for i in range(blocks_x)])  5.58 us
    pallas_call x1, Pallas kernels, local(): call(beside_kernel, [VMEM] * 3 + [HBM, VMEM], [struct(3, nx, ny)], [pltpu...  4.01 us
    ppermute x1, starting transfers between devices, local(): after_y = lax.ppermute(y_head, 'gy', back_y)  3.73 us
    all_to_all x1, starting transfers between devices, local(): got_y = lax.all_to_all(shares_y, 'gy', 0, 0, tiled=True)  3.53 us
    ppermute x1, starting transfers between devices, local(): before_x = lax.ppermute(x_tail, 'gx', round_x)  3.04 us
  transfers between devices with their start and end apart: 10, of which 2 were waited for; matrix products, arithmetic and copies ran while one was open for 0% of the time, Pallas kernels for 38%

profile of v5, /device:TPU:1, one launch (start us, length us, event | category | flops | bytes accessed | tf_op | source)
XLA Modules:
  0.0 51.6 jit_solution(7299003972070966090)
XLA Ops:
  0.0 0.0 copy-start.1
  0.0 0.0 copy-start.2
  0.0 0.0 copy-start.5
  0.0 0.0 copy-start.4
  0.0 0.0 copy-start.3
  0.0 2.0 %edges.1 = (f32[16,512]{1,0:T(8,128)S(1)}, f32[16,512]{1,0:T(8,128)S(1)}, f32[16,512]{1,0:T(8,128)S(1)}, f32[16,512]{1,0:T(8,128)S(1)}) custom-call(f32[3,512,512]{2,1,0:T(8,128)} %field.3), custom_call_target="tpu_custom_call" | custom-call | flops 655360 | bytes 1572864 | tf_op jit(solution)/shard_map/edges/pallas_call | solution.py:589
  2.0 3.0 %collective-permute-start = (f32[16,512]{1,0:T(8,128)S(1)}, f32[16,512]{1,0:T(8,128)S(1)}, u32[]{:S(2)}, u32[]{:S(2)}) collective-permute-start(f32[16,512]{1,0:T(8,128)S(1)} %get-tuple-element.18.x_tail), channel_id=1, source_target_pairs={{0,16},{16,32},{32,48},{48,64},{64,80},{80,96},{96,112},{112,128},... | collective-permute-start | bytes 98312 | tf_op jit(solution)/shard_map/halos/ppermute | solution.py:600
  5.0 0.2 collective-permute-start.1
  5.3 1.1 %collective-permute-start.2 = (f32[16,512]{1,0:T(8,128)S(1)}, f32[16,512]{1,0:T(8,128)S(1)}, u32[]{:S(2)}, u32[]{:S(2)}) collective-permute-start(f32[16,512]{1,0:T(8,128)S(1)} %get-tuple-element.20.y_tail), channel_id=1, source_target_pairs={{0,1},{1,2},{2,3},{3,4},{4,5},{5,6},{6,7},{7,8},{8,9},{9,10},{10,1... | collective-permute-start | bytes 98312 | tf_op jit(solution)/shard_map/halos/ppermute | solution.py:602
  6.3 3.7 %collective-permute-start.3 = (f32[16,512]{1,0:T(8,128)S(1)}, f32[16,512]{1,0:T(8,128)S(1)}, u32[]{:S(2)}, u32[]{:S(2)}) collective-permute-start(f32[16,512]{1,0:T(8,128)S(1)} %get-tuple-element.21.y_head), channel_id=1, source_target_pairs={{1,0},{2,1},{3,2},{4,3},{5,4},{6,5},{7,6},{8,7},{9,8},{10,9},{11,1... | collective-permute-start | bytes 98312 | tf_op jit(solution)/shard_map/halos/ppermute | solution.py:603
  10.1 0.0 copy-done.1
  10.1 0.0 copy-done.4
  10.1 0.0 copy-done.3
  10.1 7.4 %inner.1 = (f32[3,512,512]{2,1,0:T(8,128)S(1)}, f32[8,512]{1,0:T(8,128)S(1)}) custom-call(f32[3,512,512]{2,1,0:T(8,128)} %field.3, f32[1,512]{1,0:T(1,128)S(1)} %bitcast.4, f32[1,512]{1,0:T(1,128)S(1)} %bitcast.6, f32[2,512]{1,0:T(2,128)S(1)} %copy-done.1), custom_call_target="tpu_custom_call" | custom-call | flops 31457280 | bytes 6291456 | tf_op jit(solution)/shard_map/inner/pallas_call | solution.py:605
  17.4 0.0 collective-permute-done.before_x
  17.5 0.0 collective-permute-done.1.after_x
  17.5 0.0 collective-permute-done.2.before_y
  17.5 0.0 collective-permute-done.3.after_y
  17.5 0.0 copy-done.2
  17.5 0.0 copy-done.5
  17.5 1.8 %halo_part.1 = (f32[16,24,128]{2,1,0:T(8,128)}, f32[64,512]{1,0:T(8,128)}, f32[3,512,512]{2,1,0:T(8,128)S(1)}) custom-call(s32[1]{0:T(128)} %bitcast.1.index, f32[16,64]{1,0:T(8,128)S(1)} %copy-done.2, f32[16,512]{1,0:T(8,128)S(1)} %collective-permute-done.before_x, f32[16,512]{1,0:T(8,128)S(1)} %collective-permute-done.1.after_x, ...), custom_call_target="tpu_custom_call", output_to_operand_aliasing={{2}: (15, {})} | custom-call | flops 512000 | bytes 256000 | tf_op jit(solution)/shard_map/halo_part/pallas_call | solution.py:619
  19.3 3.5 %all-to-all-start = ((f32[16,24,128]{2,1,0:T(8,128)}), f32[16,24,128]{2,1,0:T(8,128)S(1)}, u32[]{:S(2)}, u32[]{:S(2)}) async-start(f32[16,24,128]{2,1,0:T(8,128)} %get-tuple-element.24), calls=%async_computation | async-start | bytes 393216 | tf_op jit(solution)/shard_map/across_y/all_to_all | solution.py:634
  22.8 0.0 copy-start
  22.8 6.3 %solve.1 = (f32[3,512,512]{2,1,0:T(8,128)S(1)}, f32[8,512]{1,0:T(8,128)S(1)}) custom-call(f32[3,512,512]{2,1,0:T(8,128)S(1)} %get-tuple-element.25.inner, f32[64,512]{1,0:T(8,128)} %get-tuple-element.26.delta, bf16[2,512,512]{2,1,0:T(8,128)(2,1)} %constant.24.clone.table_y.table, ...), custom_call_target="tpu_custom_call", output_to_operand_aliasing={{0}: (0, {})} | custom-call | flops 4831838208 | bytes 6291456 | tf_op jit(solution)/shard_map/solve/pallas_call | solution.py:636
  29.2 0.5 %all-to-all-done.got = f32[16,24,128]{2,1,0:T(8,128)S(1)} async-done(((f32[16,24,128]{2,1,0:T(8,128)}), f32[16,24,128]{2,1,0:T(8,128)S(1)}, u32[]{:S(2)}, u32[]{:S(2)}) %all-to-all-start) | async-done | bytes 196640 | tf_op jit(solution)/shard_map/across_y/all_to_all | solution.py:634
  29.7 0.0 copy-done
  29.7 0.1 ends_x.2
  29.8 5.6 %collective-permute-start.4 = (f32[8,512]{1,0:T(8,128)S(1)}, f32[8,512]{1,0:T(8,128)S(1)}, u32[]{:S(2)}, u32[]{:S(2)}) collective-permute-start(f32[8,512]{1,0:T(8,128)S(1)} %get-tuple-element.28.own), channel_id=1, source_target_pairs={{0,16},{16,0},{32,48},{48,32},{64,80},{80,64},{96,112},{112,96},{1... | collective-permute-start | bytes 49160 | tf_op jit(solution)/shard_map/across_x/ppermute | solution.py:663
  35.4 0.8 %collective-permute-done.4.other = f32[8,512]{1,0:T(8,128)S(1)} collective-permute-done((f32[8,512]{1,0:T(8,128)S(1)}, f32[8,512]{1,0:T(8,128)S(1)}, u32[]{:S(2)}, u32[]{:S(2)}) %collective-permute-start.4) | collective-permute-done | bytes 16416 | tf_op jit(solution)/shard_map/across_x/ppermute | solution.py:663
  36.3 0.1 collective-permute-start.6
  36.4 2.7 %collective-permute-start.5 = (f32[8,512]{1,0:T(8,128)S(1)}, f32[8,512]{1,0:T(8,128)S(1)}, u32[]{:S(2)}, u32[]{:S(2)}) collective-permute-start(f32[8,512]{1,0:T(8,128)S(1)} %across_x.4.token.own.pair), channel_id=1, source_target_pairs={{0,224},{16,240},{32,0},{48,16},{64,32},{80,48},{96,64},{112,80},{... | collective-permute-start | bytes 49160 | tf_op jit(solution)/shard_map/across_x/ppermute | solution.py:660
  39.0 1.7 %across_x.5.token.turned = f32[512,128]{1,0:T(8,128)S(1)} custom-call(f32[8,512]{1,0:T(8,128)S(1)} %get-tuple-element.29.beside, bf16[2,512,512]{2,1,0:T(8,128)(2,1)} %constant.24.clone.table_y.table, f32[2,512]{1,0:T(2,128)S(1)} %copy-done, f32[8,512]{1,0:T(8,128)S(1)} %across_x.4.token.own.pair), custom_call_target="tpu_custom_call" | custom-call | flops 12582912 | bytes 1048576 | tf_op jit(solution)/shard_map/across_x/pallas_call | solution.py:669
  40.7 0.0 collective-permute-done.6.below
  40.7 0.0 collective-permute-done.5.above.pair_above
  40.7 2.3 %collective-permute-start.8 = (f32[8,512]{1,0:T(8,128)S(1)}, f32[8,512]{1,0:T(8,128)S(1)}, u32[]{:S(2)}, u32[]{:S(2)}) collective-permute-start(f32[8,512]{1,0:T(8,128)S(1)} %across_x.6.token), channel_id=1, source_target_pairs={{0,160},{16,176},{32,192},{48,208},{64,224},{80,240},{96,0},{112,1... | collective-permute-start | bytes 49160 | tf_op jit(solution)/shard_map/across_x/ppermute | solution.py:660
  43.1 1.9 %collective-permute-start.7 = (f32[8,512]{1,0:T(8,128)S(1)}, f32[8,512]{1,0:T(8,128)S(1)}, u32[]{:S(2)}, u32[]{:S(2)}) collective-permute-start(f32[8,512]{1,0:T(8,128)S(1)} %across_x.6.token), channel_id=1, source_target_pairs={{0,64},{16,80},{32,96},{48,112},{64,128},{80,144},{96,160},{112,17... | collective-permute-start | bytes 49160 | tf_op jit(solution)/shard_map/across_x/ppermute | solution.py:660
  45.0 4.0 %across_x.7.solved = f32[3,512,512]{2,1,0:T(8,128)S(1)} custom-call(f32[3,512,512]{2,1,0:T(8,128)S(1)} %get-tuple-element.30.solved, f32[512,128]{1,0:T(8,128)S(1)} %across_x.5.token.turned, f32[2,512]{1,0:T(2,128)S(1)} %copy-done, bf16[2,512,512]{2,1,0:T(8,128)(2,1)} %constant.23.clone.table_x.table, ...), custom_call_target="tpu_custom_call", output_to_operand_aliasing={{}: (0, {})} | custom-call | flops 805306368 | bytes 6291456 | tf_op jit(solution)/shard_map/across_x/pallas_call | solution.py:682
  49.0 0.0 collective-permute-done.8.far_above
  49.0 0.0 collective-permute-done.7.far_below
  49.0 2.6 %final.1 = f32[3,512,512]{2,1,0:T(8,128)} custom-call(s32[1]{0:T(128)} %bitcast.index, f32[8,512]{1,0:T(8,128)S(1)} %get-tuple-element.28.own, f32[8,512]{1,0:T(8,128)S(1)} %collective-permute-done.4.other, f32[8,512]{1,0:T(8,128)S(1)} %across_x.4.token.own.pair, f32[8,512]{1,0:T(8,128)S(1)} %collective-permute-done.5.above.pair_above, ...), custom_call_target="tpu_custom_call" | custom-call | flops 3145728 | bytes 6291456 | tf_op jit(solution)/shard_map/final/pallas_call | solution.py:694
  (2 shorter events, 0.0 us)
Async XLA Ops:
  0.0 10.1 %copy-start.1 = (f32[2,512]{1,0:T(2,128)S(1)}, f32[2,512]{1,0:T(2,128)}, u32[]{:S(2)}) copy-start(f32[2,512]{1,0:T(2,128)} %constant.20.clone.ends_y.ends_x) | copy-start | bytes 12292
  0.0 17.5 %copy-start.2 = (f32[16,64]{1,0:T(8,128)S(1)}, f32[16,64]{1,0:T(8,128)}, u32[]{:S(2)}) copy-start(f32[16,64]{1,0:T(8,128)} %constant.19.clone.table) | copy-start | bytes 12292
  0.0 17.5 %copy-start.5 = (f32[8,32]{1,0:T(8,128)S(1)}, f32[8,32]{1,0:T(8,128)}, u32[]{:S(2)}) copy-start(f32[8,32]{1,0:T(8,128)} %constant.21.clone.near_ends) | copy-start | bytes 3076
  0.0 10.1 %copy-start.4 = (f32[512]{0:T(512)S(1)}, f32[512]{0:T(512)}, u32[]{:S(2)}) copy-start(f32[512]{0:T(512)} %param.14) | copy-start | bytes 6148
  0.0 10.1 %copy-start.3 = (f32[512]{0:T(512)S(1)}, f32[512]{0:T(512)}, u32[]{:S(2)}) copy-start(f32[512]{0:T(512)} %param.13) | copy-start | bytes 6148
  2.0 15.4 %collective-permute-start = (f32[16,512]{1,0:T(8,128)S(1)}, f32[16,512]{1,0:T(8,128)S(1)}, u32[]{:S(2)}, u32[]{:S(2)}) collective-permute-start(f32[16,512]{1,0:T(8,128)S(1)} %get-tuple-element.18.x_tail), channel_id=1, source_target_pairs={{0,16},{16,32},{32,48},{48,64},{64,80},{80,96},{96,112},{112,128},... | collective-permute-start | bytes 98312 | tf_op jit(solution)/shard_map/halos/ppermute | solution.py:600
  5.0 12.4 %collective-permute-start.1 = (f32[16,512]{1,0:T(8,128)S(1)}, f32[16,512]{1,0:T(8,128)S(1)}, u32[]{:S(2)}, u32[]{:S(2)}) collective-permute-start(f32[16,512]{1,0:T(8,128)S(1)} %get-tuple-element.19.x_head), channel_id=1, source_target_pairs={{16,0},{32,16},{48,32},{64,48},{80,64},{96,80},{112,96},{128,112},... | collective-permute-start | bytes 98312 | tf_op jit(solution)/shard_map/halos/ppermute | solution.py:601
  5.3 12.2 %collective-permute-start.2 = (f32[16,512]{1,0:T(8,128)S(1)}, f32[16,512]{1,0:T(8,128)S(1)}, u32[]{:S(2)}, u32[]{:S(2)}) collective-permute-start(f32[16,512]{1,0:T(8,128)S(1)} %get-tuple-element.20.y_tail), channel_id=1, source_target_pairs={{0,1},{1,2},{2,3},{3,4},{4,5},{5,6},{6,7},{7,8},{8,9},{9,10},{10,1... | collective-permute-start | bytes 98312 | tf_op jit(solution)/shard_map/halos/ppermute | solution.py:602
  6.3 11.1 %collective-permute-start.3 = (f32[16,512]{1,0:T(8,128)S(1)}, f32[16,512]{1,0:T(8,128)S(1)}, u32[]{:S(2)}, u32[]{:S(2)}) collective-permute-start(f32[16,512]{1,0:T(8,128)S(1)} %get-tuple-element.21.y_head), channel_id=1, source_target_pairs={{1,0},{2,1},{3,2},{4,3},{5,4},{6,5},{7,6},{8,7},{9,8},{10,9},{11,1... | collective-permute-start | bytes 98312 | tf_op jit(solution)/shard_map/halos/ppermute | solution.py:603
  19.3 10.4 %all-to-all-start = ((f32[16,24,128]{2,1,0:T(8,128)}), f32[16,24,128]{2,1,0:T(8,128)S(1)}, u32[]{:S(2)}, u32[]{:S(2)}) async-start(f32[16,24,128]{2,1,0:T(8,128)} %get-tuple-element.24), calls=%async_computation | async-start | bytes 393216 | tf_op jit(solution)/shard_map/across_y/all_to_all | solution.py:634
  22.8 6.9 %copy-start = (f32[2,512]{1,0:T(2,128)S(1)}, f32[2,512]{1,0:T(2,128)}, u32[]{:S(2)}) copy-start(f32[2,512]{1,0:T(2,128)} %constant.22.clone.sides_y.sides_x) | copy-start | bytes 12292
  29.8 6.4 %collective-permute-start.4 = (f32[8,512]{1,0:T(8,128)S(1)}, f32[8,512]{1,0:T(8,128)S(1)}, u32[]{:S(2)}, u32[]{:S(2)}) collective-permute-start(f32[8,512]{1,0:T(8,128)S(1)} %get-tuple-element.28.own), channel_id=1, source_target_pairs={{0,16},{16,0},{32,48},{48,32},{64,80},{80,64},{96,112},{112,96},{1... | collective-permute-start | bytes 49160 | tf_op jit(solution)/shard_map/across_x/ppermute | solution.py:663
  36.3 4.4 %collective-permute-start.6 = (f32[8,512]{1,0:T(8,128)S(1)}, f32[8,512]{1,0:T(8,128)S(1)}, u32[]{:S(2)}, u32[]{:S(2)}) collective-permute-start(f32[8,512]{1,0:T(8,128)S(1)} %across_x.4.token.own.pair), channel_id=1, source_target_pairs={{0,32},{16,48},{32,64},{48,80},{64,96},{80,112},{96,128},{112,144}... | collective-permute-start | bytes 49160 | tf_op jit(solution)/shard_map/across_x/ppermute | solution.py:660
  36.4 4.3 %collective-permute-start.5 = (f32[8,512]{1,0:T(8,128)S(1)}, f32[8,512]{1,0:T(8,128)S(1)}, u32[]{:S(2)}, u32[]{:S(2)}) collective-permute-start(f32[8,512]{1,0:T(8,128)S(1)} %across_x.4.token.own.pair), channel_id=1, source_target_pairs={{0,224},{16,240},{32,0},{48,16},{64,32},{80,48},{96,64},{112,80},{... | collective-permute-start | bytes 49160 | tf_op jit(solution)/shard_map/across_x/ppermute | solution.py:660
  40.7 8.3 %collective-permute-start.8 = (f32[8,512]{1,0:T(8,128)S(1)}, f32[8,512]{1,0:T(8,128)S(1)}, u32[]{:S(2)}, u32[]{:S(2)}) collective-permute-start(f32[8,512]{1,0:T(8,128)S(1)} %across_x.6.token), channel_id=1, source_target_pairs={{0,160},{16,176},{32,192},{48,208},{64,224},{80,240},{96,0},{112,1... | collective-permute-start | bytes 49160 | tf_op jit(solution)/shard_map/across_x/ppermute | solution.py:660
  43.1 6.0 %collective-permute-start.7 = (f32[8,512]{1,0:T(8,128)S(1)}, f32[8,512]{1,0:T(8,128)S(1)}, u32[]{:S(2)}, u32[]{:S(2)}) collective-permute-start(f32[8,512]{1,0:T(8,128)S(1)} %across_x.6.token), channel_id=1, source_target_pairs={{0,64},{16,80},{32,96},{48,112},{64,128},{80,144},{96,160},{112,17... | collective-permute-start | bytes 49160 | tf_op jit(solution)/shard_map/across_x/ppermute | solution.py:660

commit v6 on v5

--- a/solution.py
+++ b/solution.py
@@ -454,16 +454,18 @@
     before = jnp.broadcast_to(sides_y[0:1, :], (8, cells_y))
     after = jnp.broadcast_to(sides_y[1:2, :], (8, cells_y))
 
-    def step(index, carry):
+    def step(comps, index, carry):
         rows = pl.ds(pl.multiple_of(index * 8, 8), 8)
         here = turned[rows, :]
-        for comp in range(3):
+        for comp in comps:
             source = updated if comp == LATER else solved
             updated[comp, rows, :] = source[comp, rows, :] + (
                 here[:, comp : comp + 1] * before + here[:, comp + 3 : comp + 4] * after
             )
         return carry
 
+    others = [comp for comp in range(3) if comp != LATER]
+    lax.fori_loop(0, cells_x // 8, functools.partial(step, others), 0, unroll=4)
     for copy in copies:
         copy.wait()
     half = cells_x // 2
@@ -473,7 +475,7 @@
             + jnp.dot(inverse[0, rows, :], low[...], preferred_element_type=F32)
             + jnp.dot(inverse[1, rows, :], high[...], preferred_element_type=F32)
         )
-    lax.fori_loop(0, cells_x // 8, step, 0, unroll=4)
+    lax.fori_loop(0, cells_x // 8, functools.partial(step, [LATER]), 0, unroll=4)
 
 
 def final_kernel(

time: 51.9 us -> 52 us (level)
  no operation moved by 1% of the time
where the time goes in v6:
time: 52 us; the launch traced here: 51.8 us
  Pallas kernels  26 us (50%)
  starting transfers between devices  24.2 us (47%)
  waiting for transfers between devices  1.4 us (3%)
    pallas_call x1, Pallas kernels, local(): call(functools.partial(inner_kernel, scale), [HBM] + [VMEM] * 3, [struct(...  7.36 us
    ppermute x4, starting transfers between devices, along(): lax.ppermute(values, 'gx', [(i, (i + shift) % blocks_x) for i in range(bl...  7 us
    pallas_call x1, Pallas kernels, local(): call(solve_kernel, [VMEM] + [HBM] * 3, [struct(3, nx, ny), struct(8, ny)]...  6.34 us
    ppermute x1, starting transfers between devices, local(): other = lax.ppermute(own, 'gx', [(i, i ^ 1) for i in range(blocks_x)])  5.58 us
    pallas_call x1, Pallas kernels, local(): call(beside_kernel, [VMEM] * 3 + [HBM, VMEM], [struct(3, nx, ny)], [pltpu...  4.18 us
    ppermute x1, starting transfers between devices, local(): after_y = lax.ppermute(y_head, 'gy', back_y)  3.73 us
    all_to_all x1, starting transfers between devices, local(): got_y = lax.all_to_all(shares_y, 'gy', 0, 0, tiled=True)  3.53 us
    ppermute x1, starting transfers between devices, local(): before_x = lax.ppermute(x_tail, 'gx', round_x)  3.04 us
  transfers between devices with their start and end apart: 10, of which 2 were waited for; matrix products, arithmetic and copies ran while one was open for 0% of the time, Pallas kernels for 38%

profile of v6, /device:TPU:1, one launch (start us, length us, event | category | flops | bytes accessed | tf_op | source)
XLA Modules:
  0.0 51.8 jit_solution(5671931413592924593)
XLA Ops:
  0.0 0.0 copy-start.1
  0.0 0.0 copy-start.2
  0.0 0.0 copy-start.5
  0.0 0.0 copy-start.4
  0.0 0.0 copy-start.3
  0.0 2.0 %edges.1 = (f32[16,512]{1,0:T(8,128)S(1)}, f32[16,512]{1,0:T(8,128)S(1)}, f32[16,512]{1,0:T(8,128)S(1)}, f32[16,512]{1,0:T(8,128)S(1)}) custom-call(f32[3,512,512]{2,1,0:T(8,128)} %field.3), custom_call_target="tpu_custom_call" | custom-call | flops 655360 | bytes 1572864 | tf_op jit(solution)/shard_map/edges/pallas_call | solution.py:591
  2.0 3.0 %collective-permute-start = (f32[16,512]{1,0:T(8,128)S(1)}, f32[16,512]{1,0:T(8,128)S(1)}, u32[]{:S(2)}, u32[]{:S(2)}) collective-permute-start(f32[16,512]{1,0:T(8,128)S(1)} %get-tuple-element.18.x_tail), channel_id=1, source_target_pairs={{0,16},{16,32},{32,48},{48,64},{64,80},{80,96},{96,112},{112,128},... | collective-permute-start | bytes 98312 | tf_op jit(solution)/shard_map/halos/ppermute | solution.py:602
  5.0 0.2 collective-permute-start.1
  5.3 1.1 %collective-permute-start.2 = (f32[16,512]{1,0:T(8,128)S(1)}, f32[16,512]{1,0:T(8,128)S(1)}, u32[]{:S(2)}, u32[]{:S(2)}) collective-permute-start(f32[16,512]{1,0:T(8,128)S(1)} %get-tuple-element.20.y_tail), channel_id=1, source_target_pairs={{0,1},{1,2},{2,3},{3,4},{4,5},{5,6},{6,7},{7,8},{8,9},{9,10},{10,1... | collective-permute-start | bytes 98312 | tf_op jit(solution)/shard_map/halos/ppermute | solution.py:604
  6.3 3.7 %collective-permute-start.3 = (f32[16,512]{1,0:T(8,128)S(1)}, f32[16,512]{1,0:T(8,128)S(1)}, u32[]{:S(2)}, u32[]{:S(2)}) collective-permute-start(f32[16,512]{1,0:T(8,128)S(1)} %get-tuple-element.21.y_head), channel_id=1, source_target_pairs={{1,0},{2,1},{3,2},{4,3},{5,4},{6,5},{7,6},{8,7},{9,8},{10,9},{11,1... | collective-permute-start | bytes 98312 | tf_op jit(solution)/shard_map/halos/ppermute | solution.py:605
  10.1 0.0 copy-done.1
  10.1 0.0 copy-done.4
  10.1 0.0 copy-done.3
  10.1 7.4 %inner.1 = (f32[3,512,512]{2,1,0:T(8,128)S(1)}, f32[8,512]{1,0:T(8,128)S(1)}) custom-call(f32[3,512,512]{2,1,0:T(8,128)} %field.3, f32[1,512]{1,0:T(1,128)S(1)} %bitcast.4, f32[1,512]{1,0:T(1,128)S(1)} %bitcast.6, f32[2,512]{1,0:T(2,128)S(1)} %copy-done.1), custom_call_target="tpu_custom_call" | custom-call | flops 31457280 | bytes 6291456 | tf_op jit(solution)/shard_map/inner/pallas_call | solution.py:607
  17.4 0.0 collective-permute-done.before_x
  17.5 0.0 collective-permute-done.1.after_x
  17.5 0.0 collective-permute-done.2.before_y
  17.5 0.0 collective-permute-done.3.after_y
  17.5 0.0 copy-done.2
  17.5 0.0 copy-done.5
  17.5 1.8 %halo_part.1 = (f32[16,24,128]{2,1,0:T(8,128)}, f32[64,512]{1,0:T(8,128)}, f32[3,512,512]{2,1,0:T(8,128)S(1)}) custom-call(s32[1]{0:T(128)} %bitcast.1.index, f32[16,64]{1,0:T(8,128)S(1)} %copy-done.2, f32[16,512]{1,0:T(8,128)S(1)} %collective-permute-done.before_x, f32[16,512]{1,0:T(8,128)S(1)} %collective-permute-done.1.after_x, ...), custom_call_target="tpu_custom_call", output_to_operand_aliasing={{2}: (15, {})} | custom-call | flops 512000 | bytes 256000 | tf_op jit(solution)/shard_map/halo_part/pallas_call | solution.py:621
  19.3 3.5 %all-to-all-start = ((f32[16,24,128]{2,1,0:T(8,128)}), f32[16,24,128]{2,1,0:T(8,128)S(1)}, u32[]{:S(2)}, u32[]{:S(2)}) async-start(f32[16,24,128]{2,1,0:T(8,128)} %get-tuple-element.24), calls=%async_computation | async-start | bytes 393216 | tf_op jit(solution)/shard_map/across_y/all_to_all | solution.py:636
  22.8 0.0 copy-start
  22.8 6.3 %solve.1 = (f32[3,512,512]{2,1,0:T(8,128)S(1)}, f32[8,512]{1,0:T(8,128)S(1)}) custom-call(f32[3,512,512]{2,1,0:T(8,128)S(1)} %get-tuple-element.25.inner, f32[64,512]{1,0:T(8,128)} %get-tuple-element.26.delta, bf16[2,512,512]{2,1,0:T(8,128)(2,1)} %constant.24.clone.table_y.table, ...), custom_call_target="tpu_custom_call", output_to_operand_aliasing={{0}: (0, {})} | custom-call | flops 4831838208 | bytes 6291456 | tf_op jit(solution)/shard_map/solve/pallas_call | solution.py:638
  29.2 0.5 %all-to-all-done.got = f32[16,24,128]{2,1,0:T(8,128)S(1)} async-done(((f32[16,24,128]{2,1,0:T(8,128)}), f32[16,24,128]{2,1,0:T(8,128)S(1)}, u32[]{:S(2)}, u32[]{:S(2)}) %all-to-all-start) | async-done | bytes 196640 | tf_op jit(solution)/shard_map/across_y/all_to_all | solution.py:636
  29.7 0.0 copy-done
  29.7 0.1 ends_x.2
  29.8 5.6 %collective-permute-start.4 = (f32[8,512]{1,0:T(8,128)S(1)}, f32[8,512]{1,0:T(8,128)S(1)}, u32[]{:S(2)}, u32[]{:S(2)}) collective-permute-start(f32[8,512]{1,0:T(8,128)S(1)} %get-tuple-element.28.own), channel_id=1, source_target_pairs={{0,16},{16,0},{32,48},{48,32},{64,80},{80,64},{96,112},{112,96},{1... | collective-permute-start | bytes 49160 | tf_op jit(solution)/shard_map/across_x/ppermute | solution.py:665
  35.4 0.8 %collective-permute-done.4.other = f32[8,512]{1,0:T(8,128)S(1)} collective-permute-done((f32[8,512]{1,0:T(8,128)S(1)}, f32[8,512]{1,0:T(8,128)S(1)}, u32[]{:S(2)}, u32[]{:S(2)}) %collective-permute-start.4) | collective-permute-done | bytes 16416 | tf_op jit(solution)/shard_map/across_x/ppermute | solution.py:665
  36.3 0.1 collective-permute-start.6
  36.4 2.7 %collective-permute-start.5 = (f32[8,512]{1,0:T(8,128)S(1)}, f32[8,512]{1,0:T(8,128)S(1)}, u32[]{:S(2)}, u32[]{:S(2)}) collective-permute-start(f32[8,512]{1,0:T(8,128)S(1)} %across_x.4.token.own.pair), channel_id=1, source_target_pairs={{0,224},{16,240},{32,0},{48,16},{64,32},{80,48},{96,64},{112,80},{... | collective-permute-start | bytes 49160 | tf_op jit(solution)/shard_map/across_x/ppermute | solution.py:662
  39.0 1.7 %across_x.5.token.turned = f32[512,128]{1,0:T(8,128)S(1)} custom-call(f32[8,512]{1,0:T(8,128)S(1)} %get-tuple-element.29.beside, bf16[2,512,512]{2,1,0:T(8,128)(2,1)} %constant.24.clone.table_y.table, f32[2,512]{1,0:T(2,128)S(1)} %copy-done, f32[8,512]{1,0:T(8,128)S(1)} %across_x.4.token.own.pair), custom_call_target="tpu_custom_call" | custom-call | flops 12582912 | bytes 1048576 | tf_op jit(solution)/shard_map/across_x/pallas_call | solution.py:671
  40.7 0.0 collective-permute-done.6.below
  40.7 0.0 collective-permute-done.5.above.pair_above
  40.7 2.3 %collective-permute-start.8 = (f32[8,512]{1,0:T(8,128)S(1)}, f32[8,512]{1,0:T(8,128)S(1)}, u32[]{:S(2)}, u32[]{:S(2)}) collective-permute-start(f32[8,512]{1,0:T(8,128)S(1)} %across_x.6.token), channel_id=1, source_target_pairs={{0,160},{16,176},{32,192},{48,208},{64,224},{80,240},{96,0},{112,1... | collective-permute-start | bytes 49160 | tf_op jit(solution)/shard_map/across_x/ppermute | solution.py:662
  43.1 1.9 %collective-permute-start.7 = (f32[8,512]{1,0:T(8,128)S(1)}, f32[8,512]{1,0:T(8,128)S(1)}, u32[]{:S(2)}, u32[]{:S(2)}) collective-permute-start(f32[8,512]{1,0:T(8,128)S(1)} %across_x.6.token), channel_id=1, source_target_pairs={{0,64},{16,80},{32,96},{48,112},{64,128},{80,144},{96,160},{112,17... | collective-permute-start | bytes 49160 | tf_op jit(solution)/shard_map/across_x/ppermute | solution.py:662
  45.0 4.2 %across_x.7.solved = f32[3,512,512]{2,1,0:T(8,128)S(1)} custom-call(f32[3,512,512]{2,1,0:T(8,128)S(1)} %get-tuple-element.30.solved, f32[512,128]{1,0:T(8,128)S(1)} %across_x.5.token.turned, f32[2,512]{1,0:T(2,128)S(1)} %copy-done, bf16[2,512,512]{2,1,0:T(8,128)(2,1)} %constant.23.clone.table_x.table, ...), custom_call_target="tpu_custom_call", output_to_operand_aliasing={{}: (0, {})} | custom-call | flops 805306368 | bytes 6291456 | tf_op jit(solution)/shard_map/across_x/pallas_call | solution.py:684
  49.2 0.0 collective-permute-done.8.far_above
  49.2 0.0 collective-permute-done.7.far_below
  49.2 2.6 %final.1 = f32[3,512,512]{2,1,0:T(8,128)} custom-call(s32[1]{0:T(128)} %bitcast.index, f32[8,512]{1,0:T(8,128)S(1)} %get-tuple-element.28.own, f32[8,512]{1,0:T(8,128)S(1)} %collective-permute-done.4.other, f32[8,512]{1,0:T(8,128)S(1)} %across_x.4.token.own.pair, f32[8,512]{1,0:T(8,128)S(1)} %collective-permute-done.5.above.pair_above, ...), custom_call_target="tpu_custom_call" | custom-call | flops 3145728 | bytes 6291456 | tf_op jit(solution)/shard_map/final/pallas_call | solution.py:696
  (2 shorter events, 0.0 us)
Async XLA Ops:
  0.0 10.1 %copy-start.1 = (f32[2,512]{1,0:T(2,128)S(1)}, f32[2,512]{1,0:T(2,128)}, u32[]{:S(2)}) copy-start(f32[2,512]{1,0:T(2,128)} %constant.20.clone.ends_y.ends_x) | copy-start | bytes 12292
  0.0 17.5 %copy-start.2 = (f32[16,64]{1,0:T(8,128)S(1)}, f32[16,64]{1,0:T(8,128)}, u32[]{:S(2)}) copy-start(f32[16,64]{1,0:T(8,128)} %constant.19.clone.table) | copy-start | bytes 12292
  0.0 17.5 %copy-start.5 = (f32[8,32]{1,0:T(8,128)S(1)}, f32[8,32]{1,0:T(8,128)}, u32[]{:S(2)}) copy-start(f32[8,32]{1,0:T(8,128)} %constant.21.clone.near_ends) | copy-start | bytes 3076
  0.0 10.1 %copy-start.4 = (f32[512]{0:T(512)S(1)}, f32[512]{0:T(512)}, u32[]{:S(2)}) copy-start(f32[512]{0:T(512)} %param.14) | copy-start | bytes 6148
  0.0 10.1 %copy-start.3 = (f32[512]{0:T(512)S(1)}, f32[512]{0:T(512)}, u32[]{:S(2)}) copy-start(f32[512]{0:T(512)} %param.13) | copy-start | bytes 6148
  2.0 15.4 %collective-permute-start = (f32[16,512]{1,0:T(8,128)S(1)}, f32[16,512]{1,0:T(8,128)S(1)}, u32[]{:S(2)}, u32[]{:S(2)}) collective-permute-start(f32[16,512]{1,0:T(8,128)S(1)} %get-tuple-element.18.x_tail), channel_id=1, source_target_pairs={{0,16},{16,32},{32,48},{48,64},{64,80},{80,96},{96,112},{112,128},... | collective-permute-start | bytes 98312 | tf_op jit(solution)/shard_map/halos/ppermute | solution.py:602
  5.0 12.4 %collective-permute-start.1 = (f32[16,512]{1,0:T(8,128)S(1)}, f32[16,512]{1,0:T(8,128)S(1)}, u32[]{:S(2)}, u32[]{:S(2)}) collective-permute-start(f32[16,512]{1,0:T(8,128)S(1)} %get-tuple-element.19.x_head), channel_id=1, source_target_pairs={{16,0},{32,16},{48,32},{64,48},{80,64},{96,80},{112,96},{128,112},... | collective-permute-start | bytes 98312 | tf_op jit(solution)/shard_map/halos/ppermute | solution.py:603
  5.3 12.2 %collective-permute-start.2 = (f32[16,512]{1,0:T(8,128)S(1)}, f32[16,512]{1,0:T(8,128)S(1)}, u32[]{:S(2)}, u32[]{:S(2)}) collective-permute-start(f32[16,512]{1,0:T(8,128)S(1)} %get-tuple-element.20.y_tail), channel_id=1, source_target_pairs={{0,1},{1,2},{2,3},{3,4},{4,5},{5,6},{6,7},{7,8},{8,9},{9,10},{10,1... | collective-permute-start | bytes 98312 | tf_op jit(solution)/shard_map/halos/ppermute | solution.py:604
  6.3 11.1 %collective-permute-start.3 = (f32[16,512]{1,0:T(8,128)S(1)}, f32[16,512]{1,0:T(8,128)S(1)}, u32[]{:S(2)}, u32[]{:S(2)}) collective-permute-start(f32[16,512]{1,0:T(8,128)S(1)} %get-tuple-element.21.y_head), channel_id=1, source_target_pairs={{1,0},{2,1},{3,2},{4,3},{5,4},{6,5},{7,6},{8,7},{9,8},{10,9},{11,1... | collective-permute-start | bytes 98312 | tf_op jit(solution)/shard_map/halos/ppermute | solution.py:605
  19.3 10.4 %all-to-all-start = ((f32[16,24,128]{2,1,0:T(8,128)}), f32[16,24,128]{2,1,0:T(8,128)S(1)}, u32[]{:S(2)}, u32[]{:S(2)}) async-start(f32[16,24,128]{2,1,0:T(8,128)} %get-tuple-element.24), calls=%async_computation | async-start | bytes 393216 | tf_op jit(solution)/shard_map/across_y/all_to_all | solution.py:636
  22.8 6.9 %copy-start = (f32[2,512]{1,0:T(2,128)S(1)}, f32[2,512]{1,0:T(2,128)}, u32[]{:S(2)}) copy-start(f32[2,512]{1,0:T(2,128)} %constant.22.clone.sides_y.sides_x) | copy-start | bytes 12292
  29.8 6.4 %collective-permute-start.4 = (f32[8,512]{1,0:T(8,128)S(1)}, f32[8,512]{1,0:T(8,128)S(1)}, u32[]{:S(2)}, u32[]{:S(2)}) collective-permute-start(f32[8,512]{1,0:T(8,128)S(1)} %get-tuple-element.28.own), channel_id=1, source_target_pairs={{0,16},{16,0},{32,48},{48,32},{64,80},{80,64},{96,112},{112,96},{1... | collective-permute-start | bytes 49160 | tf_op jit(solution)/shard_map/across_x/ppermute | solution.py:665
  36.3 4.4 %collective-permute-start.6 = (f32[8,512]{1,0:T(8,128)S(1)}, f32[8,512]{1,0:T(8,128)S(1)}, u32[]{:S(2)}, u32[]{:S(2)}) collective-permute-start(f32[8,512]{1,0:T(8,128)S(1)} %across_x.4.token.own.pair), channel_id=1, source_target_pairs={{0,32},{16,48},{32,64},{48,80},{64,96},{80,112},{96,128},{112,144}... | collective-permute-start | bytes 49160 | tf_op jit(solution)/shard_map/across_x/ppermute | solution.py:662
  36.4 4.3 %collective-permute-start.5 = (f32[8,512]{1,0:T(8,128)S(1)}, f32[8,512]{1,0:T(8,128)S(1)}, u32[]{:S(2)}, u32[]{:S(2)}) collective-permute-start(f32[8,512]{1,0:T(8,128)S(1)} %across_x.4.token.own.pair), channel_id=1, source_target_pairs={{0,224},{16,240},{32,0},{48,16},{64,32},{80,48},{96,64},{112,80},{... | collective-permute-start | bytes 49160 | tf_op jit(solution)/shard_map/across_x/ppermute | solution.py:662
  40.7 8.4 %collective-permute-start.8 = (f32[8,512]{1,0:T(8,128)S(1)}, f32[8,512]{1,0:T(8,128)S(1)}, u32[]{:S(2)}, u32[]{:S(2)}) collective-permute-start(f32[8,512]{1,0:T(8,128)S(1)} %across_x.6.token), channel_id=1, source_target_pairs={{0,160},{16,176},{32,192},{48,208},{64,224},{80,240},{96,0},{112,1... | collective-permute-start | bytes 49160 | tf_op jit(solution)/shard_map/across_x/ppermute | solution.py:662
  43.1 6.1 %collective-permute-start.7 = (f32[8,512]{1,0:T(8,128)S(1)}, f32[8,512]{1,0:T(8,128)S(1)}, u32[]{:S(2)}, u32[]{:S(2)}) collective-permute-start(f32[8,512]{1,0:T(8,128)S(1)} %across_x.6.token), channel_id=1, source_target_pairs={{0,64},{16,80},{32,96},{48,112},{64,128},{80,144},{96,160},{112,17... | collective-permute-start | bytes 49160 | tf_op jit(solution)/shard_map/across_x/ppermute | solution.py:662
